TPU v7x, 128 devices: a whole 4x4x4 slice. The times are simulated.
128 devices in a mesh: dp: 32 (over x, y_lo, z), tensor: 4 (over y_hi, core).
Axes of the slice: x: 4, y: 4 (y_hi: 2, y_lo: 2; y = y_hi * 2 + y_lo), z: 4, core: 2. Of those that a mesh axis runs over, the one named last changes fastest.
Arguments:
- queries: bfloat16 [768, 32, 128], P('dp'), as said below
- passages: bfloat16 [768, 128, 128], P('dp', 'tensor'), as said below
- positives: int32 [768], P('dp'), may hold values from 0 to 767
Outputs:
- query_grad: float32 [768, 32, 128], P('dp')
- passage_grad: float32 [768, 128, 128], P('dp', 'tensor')
- loss: float32 [], replicated
Inputs may be any that keep to these rules, and one draw needn't show every extreme that they name: `queries`: Real-valued token vectors. `passages`: Real-valued token vectors.
All inputs are finite; a program needn't handle non-finite values.
Results may differ from a plain program's by a relative error of at most 0.0029.
Values may be sent and summed in bfloat16 or wider, within the bound.
No kernel may reach another device: no remote copies, remote signals or barrier semaphores. Data moves between devices by JAX's collectives and lax.ppermute only.
A program may use at most 192 MiB of HBM per device.

v0:
```python
import jax
import jax.numpy as jnp
from jax import lax
from jax.sharding import PartitionSpec as P

sharpness = 4.0
softness = 0.25


def block_lse(queries, piece):
    sims = (
        jnp.einsum("qid,pjd->qipj", queries, piece, preferred_element_type=jnp.float32) * sharpness
    )
    top = jnp.max(sims, axis=3, keepdims=True)
    return top[..., 0] + jnp.log(jnp.sum(jnp.exp(sims - top), axis=3))


def forward_blocks(queries, gathered, blocks):
    count, tokens, width = gathered.shape
    stacked = gathered.reshape(blocks, count // blocks, tokens, width)
    parts = lax.map(lambda piece: block_lse(queries, piece), stacked)
    return jnp.transpose(parts, (1, 2, 0, 3)).reshape(queries.shape[0], queries.shape[1], count)


def backward_blocks(queries, gathered, token_lse, score_grad, blocks):
    count, tokens, width = gathered.shape
    span = count // blocks
    stacked = gathered.reshape(blocks, span, tokens, width)

    def step(carry, inputs):
        piece, number = inputs
        start = number * span
        lse_piece = lax.dynamic_slice_in_dim(token_lse, start, span, 2)
        grad_piece = lax.dynamic_slice_in_dim(score_grad, start, span, 1)
        sims = (
            jnp.einsum("qid,pjd->qipj", queries, piece, preferred_element_type=jnp.float32)
            * sharpness
        )
        weights = jnp.exp(sims - lse_piece[..., None])
        mixed = (grad_piece[:, None, :, None] * weights).astype(jnp.bfloat16)
        carry = carry + jnp.einsum(
            "qipj,pjd->qid", mixed, piece, preferred_element_type=jnp.float32
        )
        terms = jnp.einsum("qipj,qid->pjd", mixed, queries, preferred_element_type=jnp.float32)
        return (carry, terms)

    start_value = jnp.zeros(queries.shape, jnp.float32)
    numbers = jnp.arange(blocks, dtype=jnp.int32)
    query_part, terms = lax.scan(step, start_value, (stacked, numbers))
    return (query_part, terms.reshape(count, tokens, width))


def cross_entropy(scores, positives, column_ids):
    top = jnp.max(scores, axis=1, keepdims=True)
    row_lse = top[:, 0] + jnp.log(jnp.sum(jnp.exp(scores - top), axis=1))
    hit = column_ids[None, :] == positives[:, None]
    positive_score = jnp.sum(jnp.where(hit, scores, 0.0), axis=1)
    score_grad = jnp.exp(scores - row_lse[:, None]) - hit.astype(jnp.float32)
    return (score_grad, jnp.sum(row_lse - positive_score))


def body(queries, passages, positives):
    cycle_size = lax.axis_size("dp")
    blocks = cycle_size // 4
    gathered = lax.all_gather(passages, "dp", axis=0, tiled=True)
    partial_value = forward_blocks(queries, gathered, blocks)
    top = lax.pmax(partial_value.astype(jnp.bfloat16), "tensor").astype(partial_value.dtype)
    total = lax.psum(jnp.exp(partial_value - top), "tensor")
    token_lse = top + jnp.log(total)
    scores = softness * jnp.sum(token_lse, axis=1)
    column_ids = jnp.arange(scores.shape[1], dtype=jnp.int32)
    score_grad, loss_part = cross_entropy(scores, positives, column_ids)
    query_part, terms = backward_blocks(queries, gathered, token_lse, score_grad, blocks)
    summed = lax.psum_scatter(terms, "dp", scatter_dimension=0, tiled=True)
    query_grad = lax.psum(query_part, "tensor")
    loss = lax.psum(loss_part, "dp") / (queries.shape[0] * cycle_size)
    return (query_grad, summed, loss)


def solution(mesh):
    placed = (P("dp", None, None), P("dp", "tensor", None), P("dp"))
    return jax.shard_map(
        body,
        mesh=mesh,
        in_specs=placed,
        out_specs=(P("dp", None, None), P("dp", "tensor", None), P()),
        check_vma=False,
    )
```

profile of v0, /device:TPU:0, one launch (start us, length us, event | category | flops | bytes accessed | tf_op | source)
XLA Modules:
  0.0 1296.3 jit_solution(5499956340668792043)
XLA Ops:
  8.0 167.4 %all-gather.2.cloned.1.call-done = bf16[768,32,128]{2,1,0:T(8,128)(2,1)} async-done(((bf16[24,32,128]{2,1,0:T(8,128)(2,1)}), bf16[768,32,128]{2,1,0:T(8,128)(2,1)}) %all-gather.2.cloned.1.call-update) | async-done | bytes 6291472 | tf_op jit(solution)/shard_map/all_gather | solution.py:65
  175.4 287.8 %while.23 = (s32[]{:T(128)}, f32[8,24,32,96]{2,1,3,0:T(8,128)}, bf16[8,96,32,128]{3,2,1,0:T(8,128)(2,1)}, bf16[24,32,128]{2,1,0:T(8,128)(2,1)}, s32[]{:T(128)}) while((s32[]{:T(128)}, f32[8,24,32,96]{2,1,3,0:T(8,128)}, bf16[8,96,32,128]{3,2,1,0:T(8,128)(2,1)}, bf16[24,32,128]{2,1,0:T(8,128)(2,1)}, s32[]{:T(128)}) %tuple.63), condition=%wide.region_3.4_spmd, body=%wide.region_0.3_spmd.sunk | while | flops 615702528 | bytes 22512700 | solution.py:21
  175.4 16.7 %bitcast_reduce_fusion.2 = (f32[24,32,96]{1,0,2:T(8,128)S(1)}, f32[96,32,24,32]{3,1,2,0:T(8,128)}) fusion(bf16[24,32,128]{2,1,0:T(8,128)(2,1)} %get-tuple-element.221, bf16[8,96,32,128]{3,2,1,0:T(8,128)(2,1)} %get-tuple-element.220, s32[]{:T(128)} %get-tuple-element.213), kind=kOutput, calls=%fused_computation.1.clone.1 | convolution fusion | flops 608624640 | bytes 10715648 | tf_op jit(solution)/shard_map/while/body/eval_jaxpr/qid,pjd->qipj/dot_general | solution.py:12
  192.0 18.1 %fusion.32 = f32[24,32,96]{1,0,2:T(8,128)S(1)} fusion(f32[96,32,24,32]{3,1,2,0:T(8,128)} %get-tuple-element.199, f32[24,32,96]{1,0,2:T(8,128)S(1)} %get-tuple-element.198), kind=kLoop, calls=%fused_computation.3.clone.1 | loop fusion | flops 7004160 | bytes 10027008 | tf_op jit(solution)/shard_map/while/body/eval_jaxpr/reduce_sum | solution.py:15
  210.1 1.2 bitcast_dynamic-update-slice_fusion.4
  211.3 16.7 %bitcast_reduce_fusion.2 = (f32[24,32,96]{1,0,2:T(8,128)S(1)}, f32[96,32,24,32]{3,1,2,0:T(8,128)}) fusion(bf16[24,32,128]{2,1,0:T(8,128)(2,1)} %get-tuple-element.221, bf16[8,96,32,128]{3,2,1,0:T(8,128)(2,1)} %get-tuple-element.220, s32[]{:T(128)} %get-tuple-element.213), kind=kOutput, calls=%fused_computation.1.clone.1 | convolution fusion | flops 608624640 | bytes 10715648 | tf_op jit(solution)/shard_map/while/body/eval_jaxpr/qid,pjd->qipj/dot_general | solution.py:12
  228.0 18.1 %fusion.32 = f32[24,32,96]{1,0,2:T(8,128)S(1)} fusion(f32[96,32,24,32]{3,1,2,0:T(8,128)} %get-tuple-element.199, f32[24,32,96]{1,0,2:T(8,128)S(1)} %get-tuple-element.198), kind=kLoop, calls=%fused_computation.3.clone.1 | loop fusion | flops 7004160 | bytes 10027008 | tf_op jit(solution)/shard_map/while/body/eval_jaxpr/reduce_sum | solution.py:15
  246.1 1.2 bitcast_dynamic-update-slice_fusion.4
  247.3 16.7 %bitcast_reduce_fusion.2 = (f32[24,32,96]{1,0,2:T(8,128)S(1)}, f32[96,32,24,32]{3,1,2,0:T(8,128)}) fusion(bf16[24,32,128]{2,1,0:T(8,128)(2,1)} %get-tuple-element.221, bf16[8,96,32,128]{3,2,1,0:T(8,128)(2,1)} %get-tuple-element.220, s32[]{:T(128)} %get-tuple-element.213), kind=kOutput, calls=%fused_computation.1.clone.1 | convolution fusion | flops 608624640 | bytes 10715648 | tf_op jit(solution)/shard_map/while/body/eval_jaxpr/qid,pjd->qipj/dot_general | solution.py:12
  264.0 18.1 %fusion.32 = f32[24,32,96]{1,0,2:T(8,128)S(1)} fusion(f32[96,32,24,32]{3,1,2,0:T(8,128)} %get-tuple-element.199, f32[24,32,96]{1,0,2:T(8,128)S(1)} %get-tuple-element.198), kind=kLoop, calls=%fused_computation.3.clone.1 | loop fusion | flops 7004160 | bytes 10027008 | tf_op jit(solution)/shard_map/while/body/eval_jaxpr/reduce_sum | solution.py:15
  282.0 1.3 bitcast_dynamic-update-slice_fusion.4
  283.3 16.7 %bitcast_reduce_fusion.2 = (f32[24,32,96]{1,0,2:T(8,128)S(1)}, f32[96,32,24,32]{3,1,2,0:T(8,128)}) fusion(bf16[24,32,128]{2,1,0:T(8,128)(2,1)} %get-tuple-element.221, bf16[8,96,32,128]{3,2,1,0:T(8,128)(2,1)} %get-tuple-element.220, s32[]{:T(128)} %get-tuple-element.213), kind=kOutput, calls=%fused_computation.1.clone.1 | convolution fusion | flops 608624640 | bytes 10715648 | tf_op jit(solution)/shard_map/while/body/eval_jaxpr/qid,pjd->qipj/dot_general | solution.py:12
  300.0 18.1 %fusion.32 = f32[24,32,96]{1,0,2:T(8,128)S(1)} fusion(f32[96,32,24,32]{3,1,2,0:T(8,128)} %get-tuple-element.199, f32[24,32,96]{1,0,2:T(8,128)S(1)} %get-tuple-element.198), kind=kLoop, calls=%fused_computation.3.clone.1 | loop fusion | flops 7004160 | bytes 10027008 | tf_op jit(solution)/shard_map/while/body/eval_jaxpr/reduce_sum | solution.py:15
  318.1 1.2 bitcast_dynamic-update-slice_fusion.4
  319.3 16.7 %bitcast_reduce_fusion.2 = (f32[24,32,96]{1,0,2:T(8,128)S(1)}, f32[96,32,24,32]{3,1,2,0:T(8,128)}) fusion(bf16[24,32,128]{2,1,0:T(8,128)(2,1)} %get-tuple-element.221, bf16[8,96,32,128]{3,2,1,0:T(8,128)(2,1)} %get-tuple-element.220, s32[]{:T(128)} %get-tuple-element.213), kind=kOutput, calls=%fused_computation.1.clone.1 | convolution fusion | flops 608624640 | bytes 10715648 | tf_op jit(solution)/shard_map/while/body/eval_jaxpr/qid,pjd->qipj/dot_general | solution.py:12
  336.0 18.1 %fusion.32 = f32[24,32,96]{1,0,2:T(8,128)S(1)} fusion(f32[96,32,24,32]{3,1,2,0:T(8,128)} %get-tuple-element.199, f32[24,32,96]{1,0,2:T(8,128)S(1)} %get-tuple-element.198), kind=kLoop, calls=%fused_computation.3.clone.1 | loop fusion | flops 7004160 | bytes 10027008 | tf_op jit(solution)/shard_map/while/body/eval_jaxpr/reduce_sum | solution.py:15
  355.2 16.7 %bitcast_reduce_fusion.2 = (f32[24,32,96]{1,0,2:T(8,128)S(1)}, f32[96,32,24,32]{3,1,2,0:T(8,128)}) fusion(bf16[24,32,128]{2,1,0:T(8,128)(2,1)} %get-tuple-element.221, bf16[8,96,32,128]{3,2,1,0:T(8,128)(2,1)} %get-tuple-element.220, s32[]{:T(128)} %get-tuple-element.213), kind=kOutput, calls=%fused_computation.1.clone.1 | convolution fusion | flops 608624640 | bytes 10715648 | tf_op jit(solution)/shard_map/while/body/eval_jaxpr/qid,pjd->qipj/dot_general | solution.py:12
  371.9 18.1 %fusion.32 = f32[24,32,96]{1,0,2:T(8,128)S(1)} fusion(f32[96,32,24,32]{3,1,2,0:T(8,128)} %get-tuple-element.199, f32[24,32,96]{1,0,2:T(8,128)S(1)} %get-tuple-element.198), kind=kLoop, calls=%fused_computation.3.clone.1 | loop fusion | flops 7004160 | bytes 10027008 | tf_op jit(solution)/shard_map/while/body/eval_jaxpr/reduce_sum | solution.py:15
  390.0 1.2 bitcast_dynamic-update-slice_fusion.4
  391.2 16.7 %bitcast_reduce_fusion.2 = (f32[24,32,96]{1,0,2:T(8,128)S(1)}, f32[96,32,24,32]{3,1,2,0:T(8,128)}) fusion(bf16[24,32,128]{2,1,0:T(8,128)(2,1)} %get-tuple-element.221, bf16[8,96,32,128]{3,2,1,0:T(8,128)(2,1)} %get-tuple-element.220, s32[]{:T(128)} %get-tuple-element.213), kind=kOutput, calls=%fused_computation.1.clone.1 | convolution fusion | flops 608624640 | bytes 10715648 | tf_op jit(solution)/shard_map/while/body/eval_jaxpr/qid,pjd->qipj/dot_general | solution.py:12
  407.9 18.1 %fusion.32 = f32[24,32,96]{1,0,2:T(8,128)S(1)} fusion(f32[96,32,24,32]{3,1,2,0:T(8,128)} %get-tuple-element.199, f32[24,32,96]{1,0,2:T(8,128)S(1)} %get-tuple-element.198), kind=kLoop, calls=%fused_computation.3.clone.1 | loop fusion | flops 7004160 | bytes 10027008 | tf_op jit(solution)/shard_map/while/body/eval_jaxpr/reduce_sum | solution.py:15
  427.2 16.7 %bitcast_reduce_fusion.2 = (f32[24,32,96]{1,0,2:T(8,128)S(1)}, f32[96,32,24,32]{3,1,2,0:T(8,128)}) fusion(bf16[24,32,128]{2,1,0:T(8,128)(2,1)} %get-tuple-element.221, bf16[8,96,32,128]{3,2,1,0:T(8,128)(2,1)} %get-tuple-element.220, s32[]{:T(128)} %get-tuple-element.213), kind=kOutput, calls=%fused_computation.1.clone.1 | convolution fusion | flops 608624640 | bytes 10715648 | tf_op jit(solution)/shard_map/while/body/eval_jaxpr/qid,pjd->qipj/dot_general | solution.py:12
  443.9 18.1 %fusion.32 = f32[24,32,96]{1,0,2:T(8,128)S(1)} fusion(f32[96,32,24,32]{3,1,2,0:T(8,128)} %get-tuple-element.199, f32[24,32,96]{1,0,2:T(8,128)S(1)} %get-tuple-element.198), kind=kLoop, calls=%fused_computation.3.clone.1 | loop fusion | flops 7004160 | bytes 10027008 | tf_op jit(solution)/shard_map/while/body/eval_jaxpr/reduce_sum | solution.py:15
  463.1 6.4 bitcast_convert_fusion
  469.6 102.0 %all-reduce.4.cloned.1.call-done = bf16[24,32,768]{1,0,2:T(8,128)(2,1)} async-done(((bf16[24,32,768]{1,0,2:T(8,128)(2,1)}), bf16[24,32,768]{1,0,2:T(8,128)(2,1)}) %all-reduce.4.cloned.1.call-update) | async-done | bytes 1179664 | tf_op jit(solution)/shard_map/pmax | solution.py:67
  571.6 10.1 fusion.19
  581.9 176.5 %all-reduce.6.cloned.1.call-done = f32[24,32,768]{1,0,2:T(8,128)} async-done(((f32[24,32,768]{1,0,2:T(8,128)}), f32[24,32,768]{1,0,2:T(8,128)}) %all-reduce.6.cloned.1.call-update) | async-done | bytes 2359312 | tf_op jit(solution)/shard_map/psum | solution.py:68
  758.4 11.1 fusion.20
  770.7 283.0 %while.24 = (s32[]{:T(128)}, f32[24,32,128]{2,1,0:T(8,128)S(1)}, f32[8,96,32,128]{3,2,1,0:T(8,128)}, s32[8]{0:T(128)S(1)}, f32[24,768]{0,1:T(8,128)S(1)}, /*inde...) while((s32[]{:T(128)}, f32[24,32,128]{2,1,0:T(8,128)S(1)}, ...), condition=%wide.region_10.11_spmd.clone, body=%wide.region_9.10_spmd.clone.sunk | while | flops 1821573120 | bytes 47706816 | solution.py:49
  771.9 1.4 constant_dynamic-slice_fusion.4
  773.3 12.2 fusion.39
  785.5 11.3 bitcast_dynamic-update-slice_fusion.5
  796.7 9.3 fusion.40
  807.3 1.4 constant_dynamic-slice_fusion.4
  808.6 12.2 fusion.39
  820.8 11.4 bitcast_dynamic-update-slice_fusion.5
  832.2 9.3 fusion.40
  842.8 1.4 constant_dynamic-slice_fusion.4
  844.1 12.2 fusion.39
  856.3 11.3 bitcast_dynamic-update-slice_fusion.5
  867.6 9.3 fusion.40
  878.1 1.4 constant_dynamic-slice_fusion.4
  879.5 12.2 fusion.39
  891.7 11.3 bitcast_dynamic-update-slice_fusion.5
  902.9 9.3 fusion.40
  913.4 1.4 constant_dynamic-slice_fusion.4
  914.8 12.2 fusion.39
  927.0 11.3 bitcast_dynamic-update-slice_fusion.5
  938.3 9.3 fusion.40
  948.9 1.4 constant_dynamic-slice_fusion.4
  950.2 12.2 fusion.39
  962.4 11.3 bitcast_dynamic-update-slice_fusion.5
  973.7 9.3 fusion.40
  984.2 1.4 constant_dynamic-slice_fusion.4
  985.6 12.1 fusion.39
  997.7 11.3 bitcast_dynamic-update-slice_fusion.5
  1009.0 9.3 fusion.40
  1019.5 1.4 constant_dynamic-slice_fusion.4
  1020.9 12.1 fusion.39
  1033.1 11.3 bitcast_dynamic-update-slice_fusion.5
  1044.4 9.3 fusion.40
  1055.0 82.9 %psum.23 = f32[]{:T(128)} all-reduce(f32[]{:T(128)} %get-tuple-element.124), channel_id=1, replica_groups=mesh['dp'=32,'tensor'=4] {'dp'}, use_global_device_ids=true, to_apply=%region_15.16 | all-reduce | flops 1 | bytes 8 | tf_op jit(solution)/shard_map/psum | solution.py:76
  1138.6 148.3 %reduce-scatter.2.cloned.1.call-done = f32[24,32,128]{2,1,0:T(8,128)} async-done(((f32[768,32,128]{2,1,0:T(8,128)}), f32[24,32,128]{2,1,0:T(8,128)}) %reduce-scatter.2.cloned.1.call-update) | async-done | bytes 393232 | tf_op jit(solution)/shard_map/reduce_scatter | solution.py:74
  1286.9 1.8 copy.38
  (44 shorter events, 11.9 us)
Async XLA Ops:
  7.2 168.2 %all-gather.2.cloned.1.call-start = ((), (), s32[]{:S(2)}) async-start(), calls=%async_computation.1 | async-start | bytes 6488064 | tf_op jit(solution)/shard_map/all_gather | solution.py:65
  7.9 563.7 %all-reduce.4.cloned.1.call-start = ((), (), s32[]{:S(2)}) async-start(), calls=%async_computation.2 | async-start | bytes 9437184 | tf_op jit(solution)/shard_map/pmax | solution.py:67
  469.6 288.9 %all-reduce.6.cloned.1.call-start = ((), (), s32[]{:S(2)}) async-start(), calls=%async_computation.3 | async-start | bytes 18874368 | tf_op jit(solution)/shard_map/psum | solution.py:68
  581.7 556.9 %all-reduce.8.cloned.1.call-start = ((), (), s32[]{:S(2)}) async-start(), calls=%async_computation.4 | async-start | bytes 786432 | tf_op jit(solution)/shard_map/psum | solution.py:75
  581.9 187.8 %copy-start.2 = (s32[24]{0:T(128)S(1)}, s32[24]{0:T(128)}, u32[]{:S(2)}) copy-start(s32[24]{0:T(128)} %param.9) | copy-start | bytes 292
  581.9 188.7 %copy-start = (bf16[24,32,128]{2,1,0:T(8,128)(2,1)S(1)}, bf16[24,32,128]{2,1,0:T(8,128)(2,1)}, u32[]{:S(2)}) copy-start(bf16[24,32,128]{2,1,0:T(8,128)(2,1)} %get-tuple-element.273) | copy-start | bytes 589828
  1053.7 0.7 copy-start.1
  1054.4 232.4 %reduce-scatter.2.cloned.1.call-start = ((), (), s32[]{:S(2)}) async-start(), calls=%async_computation.5 | async-start | bytes 12976128 | tf_op jit(solution)/shard_map/reduce_scatter | solution.py:74
Sparse Core Ops, SparseCore 0:
  9.6 165.6 all-gather.1
  469.7 101.8 all-reduce.3
  581.8 176.5 all-reduce.5
  1054.6 41.1 all-reduce.7
  1098.5 188.2 reduce-scatter.1
where the time goes:
time: 1300 us
  waiting for transfers between devices  595 us (46%)
  matrix products  395 us (30%)
  other arithmetic  183 us (14%)
  blocking collectives  82.9 us (6%)
  local copies, waits for them, and re-layouts  18.1 us (1%)
  between operations  15.6 us (1%)
    psum x1, waiting for transfers between devices, body(): total = lax.psum(jnp.exp(partial_value - top), 'tensor')  176 us
    all_gather x1, waiting for transfers between devices, body(): gathered = lax.all_gather(passages, 'dp', axis=0, tiled=True)  167 us
    reduce_scatter x1, waiting for transfers between devices, body(): summed = lax.psum_scatter(terms, 'dp', scatter_dimension=0, tiled=True)  148 us
    reduce_sum x8, other arithmetic, block_lse(): return top[..., 0] + jnp.log(jnp.sum(jnp.exp(sims - top), axis=3))  145 us
    dot_general x8, matrix products, block_lse(): jnp.einsum('qid,pjd->qipj', queries, piece, preferred_element_type=jnp.fl...  133 us
    pmax x1, waiting for transfers between devices, body(): lax.pmax(partial_value.astype(jnp.bfloat16), 'tensor')  102 us
    dot_general x8, matrix products, step(): jnp.einsum('qid,pjd->qipj', queries, piece, preferred_element_type=jnp.fl...  97.3 us
    dot_general x8, matrix products, step(): jnp.einsum('qipj,qid->pjd', mixed, queries, preferred_element_type=jnp.fl...  90.3 us
  transfers between devices with their start and end apart: 5, of which 4 were waited for; matrix products, arithmetic and copies ran while one was open for 0% of the time, Pallas kernels for 0%

commit v1 on v0

v1 whole, which is shorter than its diff:
```python
import jax
import jax.numpy as jnp
import numpy as np
from jax import lax
from jax.experimental import pallas as pl
from jax.experimental.pallas import tpu as pltpu
from jax.sharding import Mesh
from jax.sharding import PartitionSpec as P

sharpness = 4.0
to_base2 = sharpness * float(np.log2(np.e))
f32 = jnp.float32
bf16 = jnp.bfloat16

chunks = (8, 4)
peers = 8
span = 24
tokens = 32
ptok = 128
dim = 128
extra = 16
lane_tile = 256
block = 1024

nt = (((1,), (1,)), ((), ()))
params = pltpu.CompilerParams(vmem_limit_bytes=56 * 2**20)


def load_queries(qin, qs):
    rows = qin.shape[1] - extra
    for peer in range(peers):
        qs[peer * rows : (peer + 1) * rows, :] = qin[peer, :rows, :]


def load_passages(pin, ps):
    for x in range(4):
        for k in range(6):
            for part in range(4):
                row = (x * 6 + k) * ptok + part * tokens
                ps[row : row + tokens, :] = pin[x * 4 + part, k * tokens : (k + 1) * tokens, :]


def load_positives(qin, out):
    rows = qin.shape[1] - extra
    width = rows // dim
    for peer in range(peers):
        tail = qin[peer, rows : rows + extra, :].astype(f32)
        for piece in range(width):
            start = peer * rows + piece * dim
            out[0:1, start : start + dim] = (
                tail[piece : piece + 1] * 32.0 + tail[8 + piece : 9 + piece]
            )


def group_sum(values, ones):
    high = values.astype(bf16)
    rest = values - high.astype(f32)
    middle = rest.astype(bf16)
    low = (rest - middle.astype(f32)).astype(bf16)
    dot = lambda part: jnp.dot(part, ones, preferred_element_type=f32)
    return dot(high) + (dot(middle) + dot(low))


def forward_kernel(first, *refs):
    if first:
        qin, pin, ids, lse, scores, part, qs, ps, pos, ones = refs
    else:
        qin, pin, ids, before, lse, scores, part, qs, ps, pos, ones = refs
    load_queries(qin, qs)
    load_passages(pin, ps)
    load_positives(qin, pos)
    groups = [
        lax.shift_right_logical(lax.broadcasted_iota(jnp.int32, ones.shape, axis), 5)
        for axis in (0, 1)
    ]
    ones[...] = (groups[0] == groups[1]).astype(f32).astype(bf16)

    @pl.loop(0, qs.shape[0] // lane_tile)
    def _(number):
        here = pl.ds(pl.multiple_of(number * lane_tile, lane_tile), lane_tile)
        tile = qs[here, :]
        for i in range(span):
            sims = lax.dot_general(
                ps[i * ptok : (i + 1) * ptok, :], tile, nt, preferred_element_type=f32
            )
            top = jnp.max(sims, axis=0, keepdims=True)
            total = jnp.sum(jnp.exp2((sims - top) * to_base2), axis=0, keepdims=True)
            lse[i : i + 1, here] = top + jnp.log(total) * (1.0 / sharpness)
        summed = group_sum(lse[:, here], ones[...])
        scores[:, here] = summed
        hit = pos[0:1, here] == ids[...]
        positive = jnp.sum(jnp.where(hit, summed, 0.0), axis=0, keepdims=True)
        top = jnp.max(summed, axis=0, keepdims=True)
        if not first:
            top = jnp.maximum(top, before[0, 0:1, here])
            positive = positive + before[0, 1:2, here]
        total = jnp.sum(jnp.exp(summed - top), axis=0, keepdims=True)
        if not first:
            total = total + jnp.exp(before[0, 0:1, here] - top)
        row = top + jnp.log(total)
        for peer in range(part.shape[0]):
            part[peer, 0:1, here] = row
            part[peer, 1:2, here] = positive


def forward(qin, pin, ids, before):
    lanes = peers * (qin.shape[1] - extra)
    first = before is None
    copies = 1 if first else 16
    shapes = [(span, lanes), (span, lanes), (copies, 2, lanes)]
    ops = (qin, pin, ids) if first else (qin, pin, ids, before)
    return pl.pallas_call(
        lambda *refs: forward_kernel(first, *refs),
        out_shape=[jax.ShapeDtypeStruct(s, f32) for s in shapes],
        scratch_shapes=[
            pltpu.VMEM((lanes, dim), bf16),
            pltpu.VMEM((span * ptok, dim), bf16),
            pltpu.VMEM((1, lanes), f32),
            pltpu.VMEM((lane_tile, lane_tile), bf16),
        ],
        compiler_params=params,
        cost_estimate=pl.CostEstimate(
            flops=lanes * span * ptok * dim * 2,
            bytes_accessed=4 * 2**20,
            transcendentals=lanes * span * ptok,
        ),
    )(*ops)


def backward_kernel(has_pg, has_qg, *refs):
    refs = list(refs)
    qin, pin, ids, lse, scores, gathered = refs[:6]
    del refs[:6]
    pg_in = refs.pop(0) if has_pg else None
    qg_in = refs.pop(0) if has_qg else None
    pg, qg, loss, qs, ps, pt, pos, grad, mixed = refs
    load_queries(qin, qs)
    load_passages(pin, ps)
    load_positives(qin, pos)
    pt[...] = ps[...].T
    rows = gathered[:, 0, :]
    top = jnp.max(rows, axis=0, keepdims=True)
    row_lse = top + jnp.log(jnp.sum(jnp.exp(rows - top), axis=0, keepdims=True))
    positive = jnp.sum(gathered[:, 1, :], axis=0, keepdims=True)
    loss[...] = jnp.broadcast_to(jnp.sum(row_lse - positive, axis=1, keepdims=True), loss.shape)
    hit = (pos[...] == ids[...]).astype(f32)
    grad[...] = jnp.exp(scores[...] - row_lse) - hit
    if has_pg:
        pg[...] = pg_in[...]
    else:
        pg[...] = jnp.zeros_like(pg)

    @pl.loop(0, qs.shape[0] // block)
    def _(number):
        for part in range(block // lane_tile):
            here = pl.ds(
                pl.multiple_of(number * block + part * lane_tile, lane_tile), lane_tile
            )
            tile = qs[here, :]
            for i in range(span):
                sims = lax.dot_general(
                    ps[i * ptok : (i + 1) * ptok, :], tile, nt, preferred_element_type=f32
                )
                weights = jnp.exp2((sims - lse[i : i + 1, here]) * to_base2)
                mixed[i * ptok : (i + 1) * ptok, part * lane_tile : (part + 1) * lane_tile] = (
                    weights * grad[i : i + 1, here]
                ).astype(bf16)
        whole = pl.ds(pl.multiple_of(number * block, block), block)
        pg[...] += jnp.dot(mixed[...], qs[whole, :], preferred_element_type=f32)
        terms = jnp.dot(pt[...], mixed[...], preferred_element_type=f32).T
        if has_qg:
            terms = terms + qg_in[whole, :]
        qg[whole, :] = terms.astype(qg.dtype)


def backward(qin, pin, ids, lse, scores, gathered, pg_in, qg_in):
    lanes = peers * (qin.shape[1] - extra)
    ops = [qin, pin, ids, lse, scores, gathered]
    ops += [v for v in (pg_in, qg_in) if v is not None]
    return pl.pallas_call(
        lambda *refs: backward_kernel(pg_in is not None, qg_in is not None, *refs),
        out_shape=[
            jax.ShapeDtypeStruct((span * ptok, dim), f32),
            jax.ShapeDtypeStruct((lanes, dim), f32 if qg_in is None else bf16),
            jax.ShapeDtypeStruct((8, dim), f32),
        ],
        scratch_shapes=[
            pltpu.VMEM((lanes, dim), bf16),
            pltpu.VMEM((span * ptok, dim), bf16),
            pltpu.VMEM((dim, span * ptok), bf16),
            pltpu.VMEM((1, lanes), f32),
            pltpu.VMEM((span, lanes), f32),
            pltpu.VMEM((span * ptok, block), bf16),
        ],
        compiler_params=params,
        cost_estimate=pl.CostEstimate(
            flops=lanes * span * ptok * dim * 6,
            bytes_accessed=4 * 2**20,
            transcendentals=lanes * span * ptok,
        ),
    )(*ops)


def combine_kernel(own, other, loss, out):
    for x in range(4):
        for k in range(6):
            for part in range(4):
                row = (x * 6 + k) * ptok + part * tokens
                out[x * 4 + part, k * tokens : (k + 1) * tokens, :] = (
                    own[row : row + tokens, :] + other[row : row + tokens, :]
                ).astype(bf16)
    value = loss[...]
    high = value.astype(bf16).astype(f32)
    middle = (value - high).astype(bf16).astype(f32)
    low = value - high - middle
    which = lax.broadcasted_iota(jnp.int32, (extra, dim), 0)
    rows = jnp.where(which == 0, high[0:1], jnp.where(which == 1, middle[0:1], low[0:1]))
    for dest in range(16):
        out[dest, 6 * tokens :, :] = rows.astype(bf16)


def combine(own, other, loss):
    return pl.pallas_call(
        combine_kernel,
        out_shape=jax.ShapeDtypeStruct((16, 6 * tokens + extra, dim), bf16),
        compiler_params=params,
    )(own, other, loss)


def body(queries, passages, positives):
    core = lax.axis_index("c")
    half = lax.dynamic_slice_in_dim(queries, core * 12, 12, 0)
    half_positives = lax.dynamic_slice_in_dim(positives, core * 12, 12, 0)
    pieces = []
    start = 0
    for count in chunks:
        rows = half[start : start + count].reshape(count * tokens, dim)
        spread = jnp.repeat(half_positives[start : start + count], tokens).reshape(-1, dim)
        pad = ((0, 8 - spread.shape[0]), (0, 0))
        tail = jnp.concatenate([jnp.pad(spread // 32, pad), jnp.pad(spread % 32, pad)])
        pieces.append(jnp.concatenate([rows, tail.astype(bf16)]))
        start += count

    def spread_to(piece, count, axes):
        return lax.all_to_all(
            jnp.broadcast_to(piece[None], (count,) + piece.shape), axes, 0, 0, tiled=True
        )

    own = passages.reshape(1, 4, 6 * tokens, dim)
    own = jnp.broadcast_to(own, (4, 4, 6 * tokens, dim)).reshape(16, 6 * tokens, dim)
    own = lax.all_to_all(own, ("x", "yh", "c"), 0, 0, tiled=True)
    qins = [spread_to(piece, peers, ("yl", "z")) for piece in pieces]
    swap = ((0, 1), (1, 0))
    pins = [own, lax.ppermute(own, "c", swap)]

    place = lax.axis_index(("yl", "z")) * 24
    numbers = jnp.arange(span, dtype=jnp.int32)
    local = (numbers // 6) * 192 + numbers % 6
    ids = [
        (local + place + (lax.axis_index("yh") * 2 + side) * 6).astype(f32)[:, None]
        for side in (core, 1 - core)
    ]

    saved = []
    gathered = []
    for qin in qins:
        part = None
        tables = []
        for pin, numbers in zip(pins, ids):
            lse, scores, part = forward(qin, pin, numbers, part)
            tables.append((lse, scores))
        saved.append(tables)
        gathered.append(lax.all_to_all(part, ("yl", "z", "yh"), 0, 0, tiled=True))

    pgs = [None, None]
    losses = []
    arrived = []
    other = None
    for number, qin in enumerate(qins):
        qg = None
        for slot in (1, 0):
            lse, scores = saved[number][slot]
            pgs[slot], qg, loss = backward(
                qin, pins[slot], ids[slot], lse, scores, gathered[number], pgs[slot], qg
            )
            if slot == 1 and number == len(qins) - 1:
                other = lax.ppermute(pgs[1], "c", swap)
        losses.append(loss)
        arrived.append(
            lax.all_to_all(qg.reshape(16, -1, dim), ("yl", "z", "yh"), 0, 0, tiled=True)
        )

    payload = combine(pgs[0], other, sum(losses))
    landed = lax.all_to_all(payload, ("x", "yh", "c"), 0, 0, tiled=True)
    landed = landed.reshape(4, 4, 6 * tokens + extra, dim).astype(f32)
    passage_grad = jnp.sum(landed[:, :, : 6 * tokens], axis=0).reshape(24, tokens, dim)
    total = jnp.sum(landed[:, :2, 6 * tokens : 6 * tokens + 3, 0])
    loss = total / (768 * tokens)

    mine = jnp.concatenate([jnp.sum(a.astype(f32), axis=0) for a in arrived], axis=0)
    full = lax.all_gather(mine, ("yh", "c"), axis=0, tiled=False)
    full = full.reshape(2, 2, 6 * tokens, dim)
    parts = []
    for side in range(2):
        start = 0
        for count in chunks:
            rows = count // 2 * tokens
            parts += [full[yh, side, start : start + rows] for yh in range(2)]
            start += rows
    query_grad = jnp.concatenate(parts, axis=0).reshape(24, tokens, dim)
    return query_grad, passage_grad, loss


def solution(mesh):
    fine = Mesh(mesh.devices.reshape(4, 2, 4, 2, 2), ("x", "yl", "z", "yh", "c"))
    dp = ("x", "yl", "z")
    tensor = ("yh", "c")
    return jax.shard_map(
        body,
        mesh=fine,
        in_specs=(P(dp, None, None), P(dp, tensor, None), P(dp)),
        out_specs=(P(dp, None, None), P(dp, tensor, None), P()),
        check_vma=False,
    )
```

time: 1300 us -> 200 us (0.15)
  waiting for transfers between devices: 595 us -> 48.9 us
  matrix products: 395 us -> 0 us
  other arithmetic: 183 us -> 2.94 us
  Pallas kernels: 0 us -> 76.7 us
  blocking collectives: 82.9 us -> 23.6 us
  starting transfers between devices: 0.38 us -> 36.3 us
    dot_general x32 -> x0, matrix products: 395 us -> none  [the longest x8 133 us: block_lse(): jnp.einsum('qid,pjd->qipj', queries, piece, preferred_element_type=jnp.fl...]
    psum x2 -> x0, waiting for transfers between devices: 177 us -> none  [the longest x1 176 us: body(): total = lax.psum(jnp.exp(partial_value - top), 'tensor')]
    all_gather x1 -> x0, waiting for transfers between devices: 167 us -> none  [body(): gathered = lax.all_gather(passages, 'dp', axis=0, tiled=True)]
    reduce_sum x11 -> x4, other arithmetic: 157 us -> 1.54 us  [the longest x1 0.82 us: body(): jnp.sum(landed[:, :, :6 * tokens], axis=0).reshape(24, tokens, dim)]
    reduce_scatter x1 -> x0, waiting for transfers between devices: 148 us -> none  [body(): summed = lax.psum_scatter(terms, 'dp', scatter_dimension=0, tiled=True)]
    pmax x1 -> x0, waiting for transfers between devices: 102 us -> none  [body(): lax.pmax(partial_value.astype(jnp.bfloat16), 'tensor')]
    psum x1 -> x0, blocking collectives: 82.9 us -> none  [body(): loss = lax.psum(loss_part, 'dp') / (queries.shape[0] * cycle_size)]
    pallas_call x0 -> x9, Pallas kernels: none -> 76.7 us  [the longest x4 38.1 us: backward(): pl.pallas_call(lambda *refs: backward_kernel(pg_in is not None, qg_in is...]
  transfers between devices with their start and end apart: 5 -> 9, of which waited for: 4 -> 4; matrix products, arithmetic and copies ran while one was open for 0% -> 2% of each run, Pallas kernels for 0% -> 30%
where the time goes in v1:
time: 200 us; the launch traced here: 198 us
  Pallas kernels  76.7 us (38%)
  waiting for transfers between devices  48.9 us (24%)
  starting transfers between devices  36.3 us (18%)
  blocking collectives  23.6 us (12%)
  local copies, waits for them, and re-layouts  7.18 us (4%)
  other arithmetic  2.94 us (1%)
  between operations  2.67 us (1%)
    pallas_call x4, Pallas kernels, backward(): pl.pallas_call(lambda *refs: backward_kernel(pg_in is not None, qg_in is...  38.1 us
    pallas_call x4, Pallas kernels, forward(): pl.pallas_call(lambda *refs: forward_kernel(first, *refs), out_shape=[jax...  35.7 us
    all_to_all x1, blocking collectives, body(): lax.all_to_all(qg.reshape(16, -1, dim), ('yl', 'z', 'yh'), 0, 0, tiled=True)  16 us
    all_to_all x1, waiting for transfers between devices, body(): landed = lax.all_to_all(payload, ('x', 'yh', 'c'), 0, 0, tiled=True)  15.8 us
    all_to_all x1, waiting for transfers between devices, body(): own = lax.all_to_all(own, ('x', 'yh', 'c'), 0, 0, tiled=True)  14.8 us
    all_to_all x2, starting transfers between devices, body(): gathered.append(lax.all_to_all(part, ('yl', 'z', 'yh'), 0, 0, tiled=True))  13 us
    all_to_all x2, waiting for transfers between devices, spread_to(): lax.all_to_all(jnp.broadcast_to(piece[None], (count,) + piece.shape), axe...  9.45 us
    all_to_all x2, starting transfers between devices, spread_to(): lax.all_to_all(jnp.broadcast_to(piece[None], (count,) + piece.shape), axe...  8.86 us
  transfers between devices with their start and end apart: 9, of which 4 were waited for; matrix products, arithmetic and copies ran while one was open for 2% of the time, Pallas kernels for 30%

profile of v1, /device:TPU:0, one launch (start us, length us, event | category | flops | bytes accessed | tf_op | source)
XLA Modules:
  0.0 198.3 jit_solution(16451139226765464653)
XLA Ops:
  0.6 0.0 copy-start
  0.6 0.0 copy-start.11
  0.7 2.0 %broadcast_in_dim.36 = bf16[4,4,192,128]{3,2,1,0:T(8,128)(2,1)} broadcast(bf16[4,192,128]{2,1,0:T(8,128)(2,1)} %bitcast.56), dimensions={1,2,3} | broadcast | bytes 983040 | tf_op jit(solution)/shard_map/broadcast_in_dim | solution.py:250
  2.7 7.1 %all-to-all-start.1 = ((bf16[16,192,128]{2,1,0:T(8,128)(2,1)}), bf16[16,192,128]{2,1,0:T(8,128)(2,1)S(1)}, u32[]{:S(2)}, u32[]{:S(2)}) async-start(bf16[16,192,128]{2,1,0:T(8,128)(2,1)} %bitcast.2), calls=%async_computation.1 | async-start | bytes 1572864 | tf_op jit(solution)/shard_map/all_to_all | solution.py:251
  9.8 0.0 copy-done.11
  9.8 0.1 dynamic_slice.7
  9.9 0.1 broadcast_in_dim.31
  10.0 0.1 broadcast_in_dim.32
  10.1 0.1 broadcast_in_dim.33
  10.1 0.0 copy-done
  10.2 14.8 %all-to-all-done.1.refs_1_ = bf16[16,192,128]{2,1,0:T(8,128)(2,1)S(1)} async-done(((bf16[16,192,128]{2,1,0:T(8,128)(2,1)}), bf16[16,192,128]{2,1,0:T(8,128)(2,1)S(1)}, u32[]{:S(2)}, u32[]{:S(2)}) %all-to-all-start.1) | async-done | bytes 786464 | tf_op jit(solution)/shard_map/all_to_all | solution.py:251
  25.0 0.0 copy-start.2
  25.0 0.0 collective-permute-start
  25.0 1.0 broadcast_in_dim.34
  26.0 5.4 %all-to-all-start = ((bf16[8,272,128]{2,1,0:T(8,128)(2,1)}), bf16[8,272,128]{2,1,0:T(8,128)(2,1)S(1)}, u32[]{:S(2)}, u32[]{:S(2)}) async-start(bf16[8,272,128]{2,1,0:T(8,128)(2,1)} %broadcast_in_dim.34), calls=%async_computation | async-start | bytes 1114112 | tf_op jit(solution)/shard_map/all_to_all | solution.py:245
  31.4 0.6 add_convert_fusion
  32.0 0.1 slice.51
  32.1 0.1 broadcast_in_dim.37
  32.2 0.1 reshape_reshape.4
  32.3 9.4 %all-to-all-done.refs_0_ = bf16[8,272,128]{2,1,0:T(8,128)(2,1)S(1)} async-done(((bf16[8,272,128]{2,1,0:T(8,128)(2,1)}), bf16[8,272,128]{2,1,0:T(8,128)(2,1)S(1)}, u32[]{:S(2)}, u32[]{:S(2)}) %all-to-all-start) | async-done | bytes 557088 | tf_op jit(solution)/shard_map/all_to_all | solution.py:245
  41.8 0.8 broadcast_in_dim.38
  42.6 3.4 %all-to-all-start.4 = ((bf16[8,144,128]{2,1,0:T(8,128)(2,1)}), bf16[8,144,128]{2,1,0:T(8,128)(2,1)S(1)}, u32[]{:S(2)}, u32[]{:S(2)}) async-start(bf16[8,144,128]{2,1,0:T(8,128)(2,1)} %broadcast_in_dim.38), calls=%async_computation.4 | async-start | bytes 589824 | tf_op jit(solution)/shard_map/all_to_all | solution.py:245
  46.0 0.0 copy-done.2
  46.0 0.0 copy-done.3
  46.0 11.3 %shard_map.58 = (f32[24,2048]{1,0:T(8,128)}, f32[24,2048]{1,0:T(8,128)}, f32[1,2,2048]{2,1,0:T(2,128)}) custom-call(bf16[8,272,128]{2,1,0:T(8,128)(2,1)} %copy-done.3, bf16[16,192,128]{2,1,0:T(8,128)(2,1)} %copy-done.2, f32[24,1]{1,0:T(8,128)} %get-tuple-element.52.refs_2_), custom_call_target="tpu_custom_call" | custom-call | flops 1610612736 | bytes 4194304 | tf_op jit(solution)/shard_map/pallas_call | solution.py:112
  57.3 0.0 collective-permute-done.refs_1_
  57.3 0.0 copy-start.10
  57.3 0.9 copy-done.10
  58.2 11.4 %shard_map.59 = (f32[24,2048]{1,0:T(8,128)}, f32[24,2048]{1,0:T(8,128)}, f32[16,2,2048]{2,1,0:T(2,128)}) custom-call(bf16[8,272,128]{2,1,0:T(8,128)(2,1)} %copy-done.3, bf16[16,192,128]{2,1,0:T(8,128)(2,1)} %copy-done.10, f32[24,1]{1,0:T(8,128)} %get-tuple-element.51.refs_2_, f32[1,2,2048]{2,1,0:T(2,128)} %get-tuple-element.27.refs_3_), custom_call_target="tpu_custom_call" | custom-call | flops 1610612736 | bytes 4194304 | tf_op jit(solution)/shard_map/pallas_call | solution.py:112
  69.6 0.0 all-to-all-done.4.refs_0_
  69.6 0.0 copy-start.4
  69.6 5.8 %all-to-all-start.2 = ((f32[16,2,2048]{2,1,0:T(2,128)}), f32[16,2,2048]{2,1,0:T(2,128)S(1)}, u32[]{:S(2)}, u32[]{:S(2)}) async-start(f32[16,2,2048]{2,1,0:T(2,128)} %get-tuple-element.28), calls=%async_computation.2 | async-start | bytes 524288 | tf_op jit(solution)/shard_map/all_to_all | solution.py:273
  75.4 0.0 copy-done.4
  75.4 6.5 %shard_map.62 = (f32[24,1024]{1,0:T(8,128)}, f32[24,1024]{1,0:T(8,128)}, f32[1,2,1024]{2,1,0:T(2,128)}) custom-call(bf16[8,144,128]{2,1,0:T(8,128)(2,1)} %copy-done.4, bf16[16,192,128]{2,1,0:T(8,128)(2,1)} %copy-done.2, f32[24,1]{1,0:T(8,128)} %get-tuple-element.52.refs_2_), custom_call_target="tpu_custom_call" | custom-call | flops 805306368 | bytes 4194304 | tf_op jit(solution)/shard_map/pallas_call | solution.py:112
  81.8 6.6 %shard_map.63 = (f32[24,1024]{1,0:T(8,128)}, f32[24,1024]{1,0:T(8,128)}, f32[16,2,1024]{2,1,0:T(2,128)}) custom-call(bf16[8,144,128]{2,1,0:T(8,128)(2,1)} %copy-done.4, bf16[16,192,128]{2,1,0:T(8,128)(2,1)} %copy-done.10, f32[24,1]{1,0:T(8,128)} %get-tuple-element.51.refs_2_, f32[1,2,1024]{2,1,0:T(2,128)} %get-tuple-element.35.refs_3_), custom_call_target="tpu_custom_call" | custom-call | flops 805306368 | bytes 4194304 | tf_op jit(solution)/shard_map/pallas_call | solution.py:112
  88.4 0.0 all-to-all-done.2.refs_5_
  88.4 7.2 %all-to-all-start.5 = ((f32[16,2,1024]{2,1,0:T(2,128)}), f32[16,2,1024]{2,1,0:T(2,128)S(1)}, u32[]{:S(2)}, u32[]{:S(2)}) async-start(f32[16,2,1024]{2,1,0:T(2,128)} %get-tuple-element.36), calls=%async_computation.5 | async-start | bytes 262144 | tf_op jit(solution)/shard_map/all_to_all | solution.py:273
  95.6 0.0 copy-done.5
  95.6 11.8 %shard_map.60 = (f32[3072,128]{1,0:T(8,128)}, f32[2048,128]{1,0:T(8,128)}, f32[8,128]{1,0:T(8,128)}) custom-call(bf16[8,272,128]{2,1,0:T(8,128)(2,1)} %copy-done.3, bf16[16,192,128]{2,1,0:T(8,128)(2,1)} %copy-done.10, f32[24,1]{1,0:T(8,128)} %get-tuple-element.51.refs_2_, f32[24,2048]{1,0:T(8,128)} %get-tuple-element.29.refs_3_, ...), custom_call_target="tpu_custom_call" | custom-call | flops 4831838208 | bytes 4194304 | tf_op jit(solution)/shard_map/pallas_call | solution.py:180
  107.4 12.2 %shard_map.61 = (f32[3072,128]{1,0:T(8,128)}, bf16[2048,128]{1,0:T(8,128)(2,1)}, f32[8,128]{1,0:T(8,128)}) custom-call(bf16[8,272,128]{2,1,0:T(8,128)(2,1)} %copy-done.3, bf16[16,192,128]{2,1,0:T(8,128)(2,1)} %copy-done.2, f32[24,1]{1,0:T(8,128)} %get-tuple-element.52.refs_2_, f32[24,2048]{1,0:T(8,128)} %get-tuple-element.25.refs_3_, ...), custom_call_target="tpu_custom_call" | custom-call | flops 4831838208 | bytes 4194304 | tf_op jit(solution)/shard_map/pallas_call | solution.py:180
  119.6 0.0 all-to-all-done.5.refs_5_
  119.6 0.6 copy-done.6
  120.2 7.1 %shard_map.64 = (f32[3072,128]{1,0:T(8,128)}, f32[1024,128]{1,0:T(8,128)}, f32[8,128]{1,0:T(8,128)}) custom-call(bf16[8,144,128]{2,1,0:T(8,128)(2,1)} %copy-done.4, bf16[16,192,128]{2,1,0:T(8,128)(2,1)} %copy-done.10, f32[24,1]{1,0:T(8,128)} %get-tuple-element.51.refs_2_, f32[24,1024]{1,0:T(8,128)} %get-tuple-element.38.refs_3_, ...), custom_call_target="tpu_custom_call" | custom-call | flops 2415919104 | bytes 4194304 | tf_op jit(solution)/shard_map/pallas_call | solution.py:180
  127.3 7.1 %shard_map.65 = (f32[3072,128]{1,0:T(8,128)}, bf16[1024,128]{1,0:T(8,128)(2,1)}, f32[8,128]{1,0:T(8,128)}) custom-call(bf16[8,144,128]{2,1,0:T(8,128)(2,1)} %copy-done.4, bf16[16,192,128]{2,1,0:T(8,128)(2,1)} %copy-done.2, f32[24,1]{1,0:T(8,128)} %get-tuple-element.52.refs_2_, f32[24,1024]{1,0:T(8,128)} %get-tuple-element.33.refs_3_, ...), custom_call_target="tpu_custom_call" | custom-call | flops 2415919104 | bytes 4194304 | tf_op jit(solution)/shard_map/pallas_call | solution.py:180
  134.4 16.0 %all_to_all.40 = bf16[16,64,128]{2,1,0:T(8,128)(2,1)S(1)} all-to-all(bf16[16,64,128]{2,1,0:T(8,128)(2,1)} %bitcast.54), channel_id=1, replica_groups=mesh['x'=4,'yl'=2,'z'=4,'yh'=2,'c'=2] {'yl','z','yh'}, dimensions={0} | all-to-all | bytes 524288 | tf_op jit(solution)/shard_map/all_to_all | solution.py:290
  150.4 3.6 %all-to-all-start.3 = ((bf16[16,128,128]{2,1,0:T(8,128)(2,1)}), bf16[16,128,128]{2,1,0:T(8,128)(2,1)S(1)}, u32[]{:S(2)}, u32[]{:S(2)}) async-start(bf16[16,128,128]{2,1,0:T(8,128)(2,1)} %bitcast.3), calls=%async_computation.3 | async-start | bytes 1048576 | tf_op jit(solution)/shard_map/all_to_all | solution.py:290
  153.9 0.1 collective-permute-start.1
  154.0 0.0 copy-done.8
  154.0 0.0 copy-done.9
  154.0 0.6 add.156.loss
  154.7 8.8 %all-to-all-done.3 = bf16[16,128,128]{2,1,0:T(8,128)(2,1)S(1)} async-done(((bf16[16,128,128]{2,1,0:T(8,128)(2,1)}), bf16[16,128,128]{2,1,0:T(8,128)(2,1)S(1)}, u32[]{:S(2)}, u32[]{:S(2)}) %all-to-all-start.3) | async-done | bytes 524320 | tf_op jit(solution)/shard_map/all_to_all | solution.py:290
  163.5 0.1 convert_reduce_fusion
  163.6 7.7 %all-gather = f32[768,128]{1,0:T(8,128)S(1)} all-gather(f32[192,128]{1,0:T(8,128)S(1)} %pad_maximum_fusion), channel_id=2, replica_groups=mesh['x'=4,'yl'=2,'z'=4,'yh'=2,'c'=2] {'yh','c'}, dimensions={0}, use_global_device_ids=true | all-gather | bytes 491520 | tf_op jit(solution)/shard_map/all_gather | solution.py:301
  171.3 0.0 collective-permute-done.1.other
  171.3 0.0 copy-start.1
  171.3 1.2 copy-done.1
  172.5 3.0 %shard_map.66 = bf16[16,208,128]{2,1,0:T(8,128)(2,1)} custom-call(f32[3072,128]{1,0:T(8,128)} %get-tuple-element.43.own, f32[3072,128]{1,0:T(8,128)} %copy-done.1, f32[8,128]{1,0:T(8,128)} %add.156.loss), custom_call_target="tpu_custom_call" | custom-call | tf_op jit(solution)/shard_map/pallas_call | solution.py:223
  175.5 3.6 %all-to-all-start.7 = ((bf16[16,208,128]{2,1,0:T(8,128)(2,1)}), bf16[16,208,128]{2,1,0:T(8,128)(2,1)S(1)}, u32[]{:S(2)}, u32[]{:S(2)}) async-start(bf16[16,208,128]{2,1,0:T(8,128)(2,1)} %shard_map.66), calls=%async_computation.7 | async-start | bytes 1703936 | tf_op jit(solution)/shard_map/all_to_all | solution.py:294
  179.1 0.0 copy-start.7
  179.2 15.8 %all-to-all-done.7 = bf16[16,208,128]{2,1,0:T(8,128)(2,1)S(1)} async-done(((bf16[16,208,128]{2,1,0:T(8,128)(2,1)}), bf16[16,208,128]{2,1,0:T(8,128)(2,1)S(1)}, u32[]{:S(2)}, u32[]{:S(2)}) %all-to-all-start.7) | async-done | bytes 852000 | tf_op jit(solution)/shard_map/all_to_all | solution.py:294
  194.9 0.1 bitcast_convert_fusion
  195.1 0.6 slice_reduce_fusion.1
  195.7 0.8 slice_reduce_fusion
  196.5 0.0 copy-done.7
  (21 shorter events, 0.2 us)
Async XLA Ops:
  0.6 9.5 %copy-start = (bf16[24,32,128]{2,1,0:T(8,128)(2,1)S(1)}, bf16[24,32,128]{2,1,0:T(8,128)(2,1)}, u32[]{:S(2)}) copy-start(bf16[24,32,128]{2,1,0:T(8,128)(2,1)} %param.3) | copy-start | bytes 589828
  0.6 9.2 %copy-start.11 = (s32[24]{0:T(128)S(1)}, s32[24]{0:T(128)}, u32[]{:S(2)}) copy-start(s32[24]{0:T(128)} %param.5) | copy-start | bytes 292
  2.7 22.3 %all-to-all-start.1 = ((bf16[16,192,128]{2,1,0:T(8,128)(2,1)}), bf16[16,192,128]{2,1,0:T(8,128)(2,1)S(1)}, u32[]{:S(2)}, u32[]{:S(2)}) async-start(bf16[16,192,128]{2,1,0:T(8,128)(2,1)} %bitcast.2), calls=%async_computation.1 | async-start | bytes 1572864 | tf_op jit(solution)/shard_map/all_to_all | solution.py:251
  25.0 21.0 %copy-start.2 = (bf16[16,192,128]{2,1,0:T(8,128)(2,1)}, bf16[16,192,128]{2,1,0:T(8,128)(2,1)S(1)}, u32[]{:S(2)}) copy-start(bf16[16,192,128]{2,1,0:T(8,128)(2,1)S(1)} %all-to-all-done.1.refs_1_) | copy-start | bytes 2359300
  25.0 32.3 %collective-permute-start = (bf16[16,192,128]{2,1,0:T(8,128)(2,1)S(1)}, bf16[16,192,128]{2,1,0:T(8,128)(2,1)S(1)}, u32[]{:S(2)}, u32[]{:S(2)}) collective-permute-start(bf16[16,192,128]{2,1,0:T(8,128)(2,1)S(1)} %all-to-all-done.1.refs_1_), channel_id=1, source_target_pairs={{0,1},{1,0},{2,3},{3,2},{4,5},{5,4},{6,7},{7,6},{8,9},{9,8},{10,11... | collective-permute-start | bytes 2359304 | tf_op jit(solution)/shard_map/ppermute | solution.py:254
  26.0 15.8 %all-to-all-start = ((bf16[8,272,128]{2,1,0:T(8,128)(2,1)}), bf16[8,272,128]{2,1,0:T(8,128)(2,1)S(1)}, u32[]{:S(2)}, u32[]{:S(2)}) async-start(bf16[8,272,128]{2,1,0:T(8,128)(2,1)} %broadcast_in_dim.34), calls=%async_computation | async-start | bytes 1114112 | tf_op jit(solution)/shard_map/all_to_all | solution.py:245
  41.7 4.2 %copy-start.3 = (bf16[8,272,128]{2,1,0:T(8,128)(2,1)}, bf16[8,272,128]{2,1,0:T(8,128)(2,1)S(1)}, u32[]{:S(2)}) copy-start(bf16[8,272,128]{2,1,0:T(8,128)(2,1)S(1)} %all-to-all-done.refs_0_) | copy-start | bytes 1671172
  42.6 27.0 %all-to-all-start.4 = ((bf16[8,144,128]{2,1,0:T(8,128)(2,1)}), bf16[8,144,128]{2,1,0:T(8,128)(2,1)S(1)}, u32[]{:S(2)}, u32[]{:S(2)}) async-start(bf16[8,144,128]{2,1,0:T(8,128)(2,1)} %broadcast_in_dim.38), calls=%async_computation.4 | async-start | bytes 589824 | tf_op jit(solution)/shard_map/all_to_all | solution.py:245
  57.3 0.9 copy-start.10
  69.6 5.8 %copy-start.4 = (bf16[8,144,128]{2,1,0:T(8,128)(2,1)}, bf16[8,144,128]{2,1,0:T(8,128)(2,1)S(1)}, u32[]{:S(2)}) copy-start(bf16[8,144,128]{2,1,0:T(8,128)(2,1)S(1)} %all-to-all-done.4.refs_0_) | copy-start | bytes 884740
  69.6 18.8 %all-to-all-start.2 = ((f32[16,2,2048]{2,1,0:T(2,128)}), f32[16,2,2048]{2,1,0:T(2,128)S(1)}, u32[]{:S(2)}, u32[]{:S(2)}) async-start(f32[16,2,2048]{2,1,0:T(2,128)} %get-tuple-element.28), calls=%async_computation.2 | async-start | bytes 524288 | tf_op jit(solution)/shard_map/all_to_all | solution.py:273
  88.4 7.2 %copy-start.5 = (f32[16,2,2048]{2,1,0:T(2,128)}, f32[16,2,2048]{2,1,0:T(2,128)S(1)}, u32[]{:S(2)}) copy-start(f32[16,2,2048]{2,1,0:T(2,128)S(1)} %all-to-all-done.2.refs_5_) | copy-start | bytes 786436
  88.4 31.1 %all-to-all-start.5 = ((f32[16,2,1024]{2,1,0:T(2,128)}), f32[16,2,1024]{2,1,0:T(2,128)S(1)}, u32[]{:S(2)}, u32[]{:S(2)}) async-start(f32[16,2,1024]{2,1,0:T(2,128)} %get-tuple-element.36), calls=%async_computation.5 | async-start | bytes 262144 | tf_op jit(solution)/shard_map/all_to_all | solution.py:273
  119.6 0.6 copy-start.6
  134.4 19.6 %copy-start.8 = (f32[8,128]{1,0:T(8,128)S(1)}, f32[8,128]{1,0:T(8,128)}, u32[]{:S(2)}) copy-start(f32[8,128]{1,0:T(8,128)} %get-tuple-element.45) | copy-start | bytes 12292
  134.4 19.6 %copy-start.9 = (f32[8,128]{1,0:T(8,128)S(1)}, f32[8,128]{1,0:T(8,128)}, u32[]{:S(2)}) copy-start(f32[8,128]{1,0:T(8,128)} %get-tuple-element.46) | copy-start | bytes 12292
  150.4 13.2 %all-to-all-start.3 = ((bf16[16,128,128]{2,1,0:T(8,128)(2,1)}), bf16[16,128,128]{2,1,0:T(8,128)(2,1)S(1)}, u32[]{:S(2)}, u32[]{:S(2)}) async-start(bf16[16,128,128]{2,1,0:T(8,128)(2,1)} %bitcast.3), calls=%async_computation.3 | async-start | bytes 1048576 | tf_op jit(solution)/shard_map/all_to_all | solution.py:290
  153.9 17.4 %collective-permute-start.1 = (f32[3072,128]{1,0:T(8,128)}, f32[3072,128]{1,0:T(8,128)S(1)}, u32[]{:S(2)}, u32[]{:S(2)}) collective-permute-start(f32[3072,128]{1,0:T(8,128)} %get-tuple-element.44), channel_id=1, source_target_pairs={{0,1},{1,0},{2,3},{3,2},{4,5},{5,4},{6,7},{7,6},{8,9},{9,8},{10,11... | collective-permute-start | bytes 4718600 | tf_op jit(solution)/shard_map/ppermute | solution.py:287
  171.3 1.2 copy-start.1
  175.5 19.5 %all-to-all-start.7 = ((bf16[16,208,128]{2,1,0:T(8,128)(2,1)}), bf16[16,208,128]{2,1,0:T(8,128)(2,1)S(1)}, u32[]{:S(2)}, u32[]{:S(2)}) async-start(bf16[16,208,128]{2,1,0:T(8,128)(2,1)} %shard_map.66), calls=%async_computation.7 | async-start | bytes 1703936 | tf_op jit(solution)/shard_map/all_to_all | solution.py:294
  179.1 17.3 %copy-start.7 = (f32[768,128]{1,0:T(8,128)}, f32[768,128]{1,0:T(8,128)S(1)}, u32[]{:S(2)}) copy-start(f32[768,128]{1,0:T(8,128)S(1)} %fusion.14) | copy-start | bytes 1179652

commit v2 on v0

v2 whole, which is shorter than its diff:
```python
import jax
import jax.numpy as jnp
import numpy as np
from jax import lax
from jax.experimental import pallas as pl
from jax.experimental.pallas import tpu as pltpu
from jax.sharding import Mesh
from jax.sharding import PartitionSpec as P

sharpness = 4.0
to_base2 = sharpness * float(np.log2(np.e))
f32 = jnp.float32
bf16 = jnp.bfloat16

chunks = (8, 4)
peers = 8
span = 24
tokens = 32
ptok = 128
dim = 128
extra = 16
lane_tile = 256
block = 1024

nt = (((1,), (1,)), ((), ()))
params = pltpu.CompilerParams(vmem_limit_bytes=56 * 2**20)
cost = pl.CostEstimate(flops=3 * 10**10, bytes_accessed=8 * 10**6, transcendentals=10**7)
smem = pl.BlockSpec(memory_space=pltpu.SMEM)
vmem = pl.BlockSpec(memory_space=pltpu.VMEM)


def absolute(place, peer):
    back, side = peer // 2, peer % 2
    return lax.rem(place[0] + side, 2) * 4 + lax.rem(place[1] + 4 - back, 4)


def chunk_rows(number):
    start = sum(c * tokens + extra for c in chunks[:number])
    lane = sum(c * tokens * peers for c in chunks[:number])
    return start, chunks[number] * tokens, lane


def load_queries(numbers, qins, qs, pos):
    first = chunk_rows(numbers[0])[2]
    for number in numbers:
        start, rows, lane = chunk_rows(number)
        for peer in range(peers):
            source = qins[peer % 2].at[peer // 2]
            here = lane - first + peer * rows
            qs[here : here + rows, :] = source[start : start + rows, :]
            tail = source[start + rows : start + rows + extra, :].astype(f32)
            for piece in range(rows // dim):
                pos[0:1, here + piece * dim : here + (piece + 1) * dim] = (
                    tail[piece : piece + 1] * 32.0 + tail[8 + piece : 9 + piece]
                )


def load_passages(pins, ps):
    for slot, pin in enumerate(pins):
        for x in range(4):
            for k in range(6):
                for part in range(4):
                    row = (slot * span + x * 6 + k) * ptok + part * tokens
                    ps[row : row + tokens, :] = pin[x * 4 + part, k * tokens : (k + 1) * tokens, :]


def group_sum(values, ones):
    high = values.astype(bf16)
    rest = values - high.astype(f32)
    middle = rest.astype(bf16)
    low = (rest - middle.astype(f32)).astype(bf16)
    dot = lambda part: jnp.dot(part, ones, preferred_element_type=f32)
    return dot(high) + (dot(middle) + dot(low))


def forward_kernel(slots, first, copies, *refs):
    refs = list(refs)
    place = refs.pop(0)
    qins = [refs.pop(0) for _ in range(2)]
    pins = [refs.pop(0) for _ in range(slots)]
    ids = [refs.pop(0) for _ in range(slots)]
    before = None if first else refs.pop(0)
    lses = [refs.pop(0) for _ in range(slots)]
    tables = [refs.pop(0) for _ in range(slots)]
    part, qs, ps, pos, ones, local = refs
    load_queries((0, 1), qins, qs, pos)
    load_passages(pins, ps)
    groups = [
        lax.shift_right_logical(lax.broadcasted_iota(jnp.int32, ones.shape, axis), 5)
        for axis in (0, 1)
    ]
    ones[...] = (groups[0] == groups[1]).astype(f32).astype(bf16)

    @pl.loop(0, qs.shape[0] // (2 * lane_tile))
    def _(step):
        for side in range(2):
            start = pl.multiple_of(step * (2 * lane_tile) + side * lane_tile, lane_tile)
            here = pl.ds(start, lane_tile)
            tile = qs[here, :]
            for i in range(slots * span):
                sims = lax.dot_general(
                    ps[i * ptok : (i + 1) * ptok, :], tile, nt, preferred_element_type=f32
                )
                top = jnp.max(sims, axis=0, keepdims=True)
                total = jnp.sum(jnp.exp2((sims - top) * to_base2), axis=0, keepdims=True)
                lses[i // span][i % span : i % span + 1, here] = top + jnp.log(total) * (
                    1.0 / sharpness
                )

    for tile in range(qs.shape[0] // lane_tile):
        here = slice(tile * lane_tile, (tile + 1) * lane_tile)
        positive = top = None
        for slot in range(slots):
            summed = group_sum(lses[slot][:, here], ones[...])
            tables[slot][:, here] = summed
            hit = pos[0:1, here] == ids[slot][...]
            found = jnp.sum(jnp.where(hit, summed, 0.0), axis=0, keepdims=True)
            most = jnp.max(summed, axis=0, keepdims=True)
            positive = found if slot == 0 else positive + found
            top = most if slot == 0 else jnp.maximum(top, most)
        if not first:
            top = jnp.maximum(top, before[0:1, here])
            positive = positive + before[1:2, here]
        total = jnp.exp(before[0:1, here] - top) if not first else 0.0
        for slot in range(slots):
            total = total + jnp.sum(jnp.exp(tables[slot][:, here] - top), axis=0, keepdims=True)
        local[0:1, here] = top + jnp.log(total)
        local[1:2, here] = positive

    if copies == 1:
        part[...] = local[...]
    else:
        for number in range(len(chunks)):
            _, rows, lane = chunk_rows(number)
            for peer in range(peers):
                start = lane + absolute(place, peer) * rows
                there = pl.ds(pl.multiple_of(start, rows), rows)
                for copy in range(copies):
                    part[copy, :, there] = local[:, lane + peer * rows : lane + (peer + 1) * rows]


def forward(place, qins, pins, ids, before, copies):
    lanes = peers * sum(chunks) * tokens
    slots = len(pins)
    first = before is None
    shapes = [(span, lanes)] * (2 * slots)
    shapes.append((2, lanes) if copies == 1 else (copies, 2, lanes))
    ops = [place, *qins, *pins, *ids] + ([] if first else [before])
    outs = pl.pallas_call(
        lambda *refs: forward_kernel(slots, first, copies, *refs),
        out_shape=[jax.ShapeDtypeStruct(s, f32) for s in shapes],
        in_specs=[smem] + [vmem] * (len(ops) - 1),
        scratch_shapes=[
            pltpu.VMEM((lanes, dim), bf16),
            pltpu.VMEM((slots * span * ptok, dim), bf16),
            pltpu.VMEM((1, lanes), f32),
            pltpu.VMEM((lane_tile, lane_tile), bf16),
            pltpu.VMEM((2, lanes), f32),
        ],
        compiler_params=params,
        cost_estimate=cost,
    )(*ops)
    return outs[:slots], outs[slots : 2 * slots], outs[-1]


def backward_kernel(number, slots, has_pg, has_qg, has_loss, doubled, *refs):
    refs = list(refs)
    place = refs.pop(0)
    qins = [refs.pop(0) for _ in range(2)]
    pins = [refs.pop(0) for _ in range(slots)]
    ids = [refs.pop(0) for _ in range(slots)]
    lses = [refs.pop(0) for _ in range(slots)]
    tables = [refs.pop(0) for _ in range(slots)]
    gathered = refs.pop(0)
    pg_in = refs.pop(0) if has_pg else None
    qg_in = refs.pop(0) if has_qg else None
    loss_in = refs.pop(0) if has_loss else None
    pgs = [refs.pop(0) for _ in range(slots)]
    qg, loss, qs, ps, pt, pos, grad, mixed, gap = refs
    load_queries((number,), qins, qs, pos)
    load_passages(pins, ps)
    pt[...] = ps[...].T
    rows = chunk_rows(number)[1]
    _, rows, lane = chunk_rows(number)
    for peer in range(peers):
        there = pl.ds(pl.multiple_of(lane + absolute(place, peer) * rows, rows), rows)
        here = slice(peer * rows, (peer + 1) * rows)
        parts = gathered[:, 0, there]
        top = jnp.max(parts, axis=0, keepdims=True)
        row_lse = top + jnp.log(jnp.sum(jnp.exp(parts - top), axis=0, keepdims=True))
        positive = jnp.sum(gathered[:, 1, there], axis=0, keepdims=True)
        ordered = pl.ds(pl.multiple_of(absolute(place, peer) * rows, rows), rows)
        gap[0:1, ordered] = row_lse - positive
        for slot in range(slots):
            hit = (pos[0:1, here] == ids[slot][...]).astype(f32)
            lines = slice(slot * span, (slot + 1) * span)
            score = tables[slot][:, lane + peer * rows : lane + (peer + 1) * rows]
            grad[lines, here] = jnp.exp(score - row_lse) - hit
    value = jnp.sum(gap[...], axis=1, keepdims=True)
    loss[...] = jnp.broadcast_to(value, loss.shape)
    if has_loss:
        loss[...] += loss_in[...]
    for pg in pgs:
        pg[...] = pg_in[...] if has_pg else jnp.zeros_like(pg)

    @pl.loop(0, qs.shape[0] // block)
    def _(step):
        for piece in range(block // lane_tile):
            here = pl.ds(pl.multiple_of(step * block + piece * lane_tile, lane_tile), lane_tile)
            there = pl.ds(
                pl.multiple_of(lane + step * block + piece * lane_tile, lane_tile), lane_tile
            )
            tile = qs[here, :]
            for i in range(slots * span):
                sims = lax.dot_general(
                    ps[i * ptok : (i + 1) * ptok, :], tile, nt, preferred_element_type=f32
                )
                row = lses[i // span][i % span : i % span + 1, there]
                weights = jnp.exp2((sims - row) * to_base2)
                mixed[i * ptok : (i + 1) * ptok, piece * lane_tile : (piece + 1) * lane_tile] = (
                    weights * grad[i : i + 1, here]
                ).astype(bf16)
        whole = pl.ds(pl.multiple_of(step * block, block), block)
        for slot, pg in enumerate(pgs):
            lines = slice(slot * span * ptok, (slot + 1) * span * ptok)
            pg[...] += jnp.dot(mixed[lines, :], qs[whole, :], preferred_element_type=f32)
        terms = jnp.dot(pt[...], mixed[...], preferred_element_type=f32).T
        if has_qg:
            terms = terms + qg_in[whole, :]
        if doubled:
            for part in range(block // rows):
                start = absolute(place, step * (block // rows) + part) * (2 * rows)
                piece = terms[part * rows : (part + 1) * rows].astype(qg.dtype)
                for copy in range(2):
                    qg[pl.ds(pl.multiple_of(start + copy * rows, rows), rows), :] = piece
        else:
            qg[whole, :] = terms.astype(qg.dtype)


def backward(number, place, qins, pins, ids, lses, tables, gathered, before, doubled, kind):
    lanes = peers * chunk_rows(number)[1]
    slots = len(pins)
    ops = [place, *qins, *pins, *ids, *lses, *tables, gathered] + [v for v in before if v is not None]
    flags = [v is not None for v in before] + [doubled]
    outs = pl.pallas_call(
        lambda *refs: backward_kernel(number, slots, *flags, *refs),
        out_shape=[jax.ShapeDtypeStruct((span * ptok, dim), f32)] * slots
        + [
            jax.ShapeDtypeStruct((2 * lanes if doubled else lanes, dim), kind),
            jax.ShapeDtypeStruct((8, dim), f32),
        ],
        in_specs=[smem] + [vmem] * (len(ops) - 1),
        scratch_shapes=[
            pltpu.VMEM((lanes, dim), bf16),
            pltpu.VMEM((slots * span * ptok, dim), bf16),
            pltpu.VMEM((dim, slots * span * ptok), bf16),
            pltpu.VMEM((1, lanes), f32),
            pltpu.VMEM((slots * span, lanes), f32),
            pltpu.VMEM((slots * span * ptok, block), bf16),
            pltpu.VMEM((1, lanes), f32),
        ],
        compiler_params=params,
        cost_estimate=cost,
    )(*ops)
    return outs[:slots], outs[slots], outs[slots + 1]


def combine_kernel(own, other, loss_own, loss_other, *outs):
    for x in range(4):
        out = outs[x]
        for k in range(6):
            for part in range(4):
                row = (x * 6 + k) * ptok + part * tokens
                there = part * 6 * tokens + k * tokens
                out[there : there + tokens, :] = (
                    own[row : row + tokens, :] + other[row : row + tokens, :]
                ).astype(out.dtype)
    value = loss_own[...] + loss_other[...]
    high = value.astype(bf16).astype(f32)
    middle = (value - high).astype(bf16).astype(f32)
    low = value - high - middle
    which = lax.broadcasted_iota(jnp.int32, (extra, dim), 0)
    rows = jnp.where(which == 0, high[0:1], jnp.where(which == 1, middle[0:1], low[0:1]))
    for out in outs:
        out[4 * 6 * tokens :, :] = rows.astype(out.dtype)


def combine(own, other, loss_own, loss_other):
    rows = 4 * 6 * tokens + extra
    return pl.pallas_call(
        combine_kernel,
        out_shape=[jax.ShapeDtypeStruct((rows, dim), f32 if x == 0 else bf16) for x in range(4)],
        in_specs=[vmem] * 4,
        compiler_params=params,
        cost_estimate=cost,
    )(own, other, loss_own, loss_other)


def exchange(value, axes, step):
    size = 4 if isinstance(axes, tuple) else 2
    return lax.ppermute(value, axes, [(i, i ^ step) for i in range(size)])


def rotate(value, step):
    return lax.ppermute(value, "x", [(i, (i + step) % 4) for i in range(4)])


def by_tensor(blocks, yh, core):
    a, b, c, d = blocks
    a, b = jnp.where(core == 0, a, b), jnp.where(core == 0, b, a)
    c, d = jnp.where(core == 0, c, d), jnp.where(core == 0, d, c)
    low = [jnp.where(yh == 0, u, v) for u, v in ((a, c), (b, d), (c, a), (d, b))]
    return jnp.concatenate(low)


def body(queries, passages, positives):
    core, yh, yl, z, x = (lax.axis_index(a) for a in ("c", "yh", "yl", "z", "x"))
    spot = yh * 2 + core
    both = ("yh", "c")
    group = ("yl", "z", "yh")

    half = lax.dynamic_slice_in_dim(queries, core * 12, 12, 0)
    half_positives = lax.dynamic_slice_in_dim(positives, core * 12, 12, 0)
    pieces = []
    start = 0
    for count in chunks:
        rows = half[start : start + count].reshape(count * tokens, dim)
        spread = jnp.repeat(half_positives[start : start + count], tokens).reshape(-1, dim)
        pad = ((0, 8 - spread.shape[0]), (0, 0))
        tail = jnp.concatenate([jnp.pad(spread // 32, pad), jnp.pad(spread % 32, pad)])
        pieces += [rows, tail.astype(bf16)]
        start += count
    piece = jnp.concatenate(pieces)
    blocks = passages.reshape(4, 6 * tokens, dim)
    part_of = lambda s: lax.dynamic_slice_in_dim(blocks, spot ^ s, 1, 0)
    quarters = [part_of(0)] + [exchange(part_of(s), both, s) for s in (1, 2, 3)]
    around = [piece] + [
        lax.ppermute(piece, "z", [(i, (i + s) % 4) for i in range(4)]) for s in (1, 2, 3)
    ]
    quarters, around = lax.optimization_barrier((quarters, around))
    quarters = jnp.concatenate(quarters)
    around = jnp.stack(around)
    own = [quarters] + [rotate(quarters, s) for s in (1, 2, 3)]
    qins = [around, exchange(around, "yl", 1)]
    own, qins = lax.optimization_barrier((own, qins))
    own = jnp.concatenate(own)
    pins = [own, exchange(own, "c", 1)]
    place = jnp.stack([yl, z]).astype(jnp.int32)

    numbers = jnp.arange(span, dtype=jnp.int32)
    local = ((x + 4 - numbers // 6) % 4) * 192 + numbers % 6 + (yl * 4 + z) * 24
    ids = [(local + (spot ^ side) * 6).astype(f32)[:, None] for side in (0, 1)]

    lse0, table0, part = forward(place, qins, pins[:1], ids[:1], None, 1)
    lse1, table1, part = forward(place, qins, pins[1:], ids[1:], part, 16)
    gathered = lax.all_to_all(part, group, 0, 0, tiled=True)

    pgs, qg, loss = backward(
        0, place, qins, pins, ids, lse0 + lse1, table0 + table1, gathered, (None,) * 3, False, bf16
    )
    qg = qg.reshape(4, 2, -1, dim)
    terms = [qg[0]] + [
        lax.ppermute(qg[s], "z", [(i, (i + 4 - s) % 4) for i in range(4)]) for s in (1, 2, 3)
    ]
    terms = [t.astype(f32) for t in terms]
    early = (terms[0] + terms[1]) + (terms[2] + terms[3])
    early = early[0] + exchange(early[1], "yl", 1)
    early = early + exchange(early, "yh", 1)

    (pg1,), qg, loss = backward(
        1, place, qins, pins[1:], ids[1:], lse1, table1, gathered, (pgs[1], None, loss), False, f32
    )
    other = exchange(pg1, "c", 1)
    loss_other = exchange(loss, "c", 1)
    (pg0,), qg, _ = backward(
        1, place, qins, pins[:1], ids[:1], lse0, table0, gathered, (pgs[0], qg, None), True, bf16
    )

    sent = combine(pg0, other, loss, loss_other)
    qg, sent = lax.optimization_barrier((qg, sent))
    arrived = lax.all_to_all(qg.reshape(16, -1, dim), group, 0, 0, tiled=True)
    landed = [sent[0]] + [rotate(sent[s], 4 - s).astype(f32) for s in (1, 2, 3)]
    summed = (landed[0] + landed[2]) + (landed[1] + landed[3])
    arrived, summed = lax.optimization_barrier((arrived, summed))
    values = [jnp.sum(part[4 * 6 * tokens : 4 * 6 * tokens + 3, 0]) for part in landed]
    loss = ((values[0] + values[2]) + (values[1] + values[3])) / (768 * tokens)

    rows = 6 * tokens
    done = jnp.concatenate([early, jnp.sum(arrived.astype(f32), axis=0)])
    sibling = exchange(done, "c", 1)
    query_grad = jnp.concatenate(
        [jnp.where(core == 0, done, sibling), jnp.where(core == 0, sibling, done)]
    ).reshape(24, tokens, dim)

    homes = [summed[:rows]] + [
        exchange(summed[s * rows : (s + 1) * rows], both, s) for s in (1, 2, 3)
    ]
    passage_grad = by_tensor(homes, yh, core).reshape(24, tokens, dim)
    return query_grad, passage_grad, loss


def solution(mesh):
    fine = Mesh(mesh.devices.reshape(4, 2, 4, 2, 2), ("x", "yl", "z", "yh", "c"))
    dp = ("x", "yl", "z")
    tensor = ("yh", "c")
    return jax.shard_map(
        body,
        mesh=fine,
        in_specs=(P(dp, None, None), P(dp, tensor, None), P(dp)),
        out_specs=(P(dp, None, None), P(dp, tensor, None), P()),
        check_vma=False,
    )
```

time: 1300 us -> 158 us (0.12)
  waiting for transfers between devices: 595 us -> 22.1 us
  matrix products: 395 us -> 0 us
  other arithmetic: 183 us -> 6.45 us
  Pallas kernels: 0 us -> 67.4 us
  blocking collectives: 82.9 us -> 15.7 us
  starting transfers between devices: 0.38 us -> 34.2 us
    dot_general x32 -> x0, matrix products: 395 us -> none  [the longest x8 133 us: block_lse(): jnp.einsum('qid,pjd->qipj', queries, piece, preferred_element_type=jnp.fl...]
    psum x2 -> x0, waiting for transfers between devices: 177 us -> none  [the longest x1 176 us: body(): total = lax.psum(jnp.exp(partial_value - top), 'tensor')]
    all_gather x1 -> x0, waiting for transfers between devices: 167 us -> none  [body(): gathered = lax.all_gather(passages, 'dp', axis=0, tiled=True)]
    reduce_sum x11 -> x5, other arithmetic: 157 us -> 3.16 us  [the longest x4 3.08 us: body(): jnp.sum(part[4 * 6 * tokens:4 * 6 * tokens + 3, 0])]
    reduce_scatter x1 -> x0, waiting for transfers between devices: 148 us -> none  [body(): summed = lax.psum_scatter(terms, 'dp', scatter_dimension=0, tiled=True)]
    pmax x1 -> x0, waiting for transfers between devices: 102 us -> none  [body(): lax.pmax(partial_value.astype(jnp.bfloat16), 'tensor')]
    psum x1 -> x0, blocking collectives: 82.9 us -> none  [body(): loss = lax.psum(loss_part, 'dp') / (queries.shape[0] * cycle_size)]
    pallas_call x0 -> x6, Pallas kernels: none -> 67.4 us  [the longest x3 36.2 us: backward(): pl.pallas_call(lambda *refs: backward_kernel(number, slots, *flags, *refs...]
  transfers between devices with their start and end apart: 5 -> 26, of which waited for: 4 -> 9; matrix products, arithmetic and copies ran while one was open for 0% -> 4% of each run, Pallas kernels for 0% -> 21%
where the time goes in v2:
time: 158 us; the launch traced here: 157 us
  Pallas kernels  67.4 us (43%)
  starting transfers between devices  34.2 us (22%)
  waiting for transfers between devices  22.1 us (14%)
  blocking collectives  15.7 us (10%)
  other arithmetic  6.45 us (4%)
  local copies, waits for them, and re-layouts  6.4 us (4%)
  between operations  4.68 us (3%)
    pallas_call x3, Pallas kernels, backward(): pl.pallas_call(lambda *refs: backward_kernel(number, slots, *flags, *refs...  36.2 us
    pallas_call x2, Pallas kernels, forward(): pl.pallas_call(lambda *refs: forward_kernel(slots, first, copies, *refs),...  28.4 us
    all_to_all x1, blocking collectives, body(): gathered = lax.all_to_all(part, group, 0, 0, tiled=True)  15.7 us
    ppermute x6, waiting for transfers between devices, rotate(): return lax.ppermute(value, 'x', [(i, (i + step) % 4) for i in range(4)])  12.1 us
    ppermute x13, starting transfers between devices, exchange(): return lax.ppermute(value, axes, [(i, i ^ step) for i in range(size)])  11.7 us
    ppermute x13, waiting for transfers between devices, exchange(): return lax.ppermute(value, axes, [(i, i ^ step) for i in range(size)])  9.99 us
    ppermute x6, starting transfers between devices, rotate(): return lax.ppermute(value, 'x', [(i, (i + step) % 4) for i in range(4)])  7.47 us
    all_to_all x1, starting transfers between devices, body(): arrived = lax.all_to_all(qg.reshape(16, -1, dim), group, 0, 0, tiled=True)  6.28 us
  transfers between devices with their start and end apart: 26, of which 9 were waited for; matrix products, arithmetic and copies ran while one was open for 4% of the time, Pallas kernels for 21%

profile of v2, /device:TPU:0, one launch (start us, length us, event | category | flops | bytes accessed | tf_op | source)
XLA Modules:
  0.0 157.0 jit_solution(4541825086675993156)
XLA Ops:
  0.7 0.8 dynamic_slice.23
  1.4 0.1 slice.67
  1.5 0.1 broadcast_in_dim.12
  1.6 0.1 broadcast_in_dim.15
  1.6 0.1 reshape_reshape.4
  1.7 0.1 broadcast_in_dim.13
  1.8 0.1 broadcast_in_dim.14
  2.1 4.2 %collective-permute-start.5 = (bf16[416,128]{1,0:T(8,128)(2,1)S(1)}, bf16[416,128]{1,0:T(8,128)(2,1)S(1)}, u32[]{:S(2)}, u32[]{:S(2)}) collective-permute-start(bf16[416,128]{1,0:T(8,128)(2,1)S(1)} %constant_dynamic-update-slice_fusion), channel_id=1, source_target_pairs={{0,12},{4,0},{8,4},{12,8},{1,13},{5,1},{9,5},{13,9},{2,14},{6,2},{... | collective-permute-start | bytes 319496 | tf_op jit(solution)/shard_map/ppermute | solution.py:338
  6.3 1.3 collective-permute-start.3
  7.5 0.9 constant_dynamic-slice_fusion.2
  8.4 1.9 %collective-permute-start.2 = (bf16[1,192,128]{2,1,0:T(8,128)(2,1)S(1)}, bf16[1,192,128]{2,1,0:T(8,128)(2,1)S(1)}, u32[]{:S(2)}, u32[]{:S(2)}) collective-permute-start(bf16[1,192,128]{2,1,0:T(8,128)(2,1)S(1)} %get-tuple-element.96), channel_id=1, source_target_pairs={{0,3},{1,2},{2,1},{3,0},{4,7},{5,6},{6,5},{7,4},{8,11},{9,10},{10,... | collective-permute-start | bytes 147464 | tf_op jit(solution)/shard_map/ppermute | solution.py:301
  10.3 1.5 collective-permute-start.1
  11.8 2.0 %collective-permute-done.2 = bf16[1,192,128]{2,1,0:T(8,128)(2,1)S(1)} collective-permute-done((bf16[1,192,128]{2,1,0:T(8,128)(2,1)S(1)}, bf16[1,192,128]{2,1,0:T(8,128)(2,1)S(1)}, u32[]{:S(2)}, u32[]{:S(2)}) %collective-permute-start.2) | collective-permute-done | bytes 49184 | tf_op jit(solution)/shard_map/ppermute | solution.py:301
  13.8 0.1 collective-permute-start
  13.9 2.0 %collective-permute-done.1 = bf16[1,192,128]{2,1,0:T(8,128)(2,1)S(1)} collective-permute-done((bf16[1,192,128]{2,1,0:T(8,128)(2,1)S(1)}, bf16[1,192,128]{2,1,0:T(8,128)(2,1)S(1)}, u32[]{:S(2)}, u32[]{:S(2)}) %collective-permute-start.1) | collective-permute-done | bytes 49184 | tf_op jit(solution)/shard_map/ppermute | solution.py:301
  16.0 0.8 collective-permute-start.9
  16.8 2.8 %collective-permute-start.8 = (bf16[4,192,128]{2,1,0:T(8,128)(2,1)S(1)}, bf16[4,192,128]{2,1,0:T(8,128)(2,1)S(1)}, u32[]{:S(2)}, u32[]{:S(2)}) collective-permute-start(bf16[4,192,128]{2,1,0:T(8,128)(2,1)S(1)} %constant_dynamic-update-slice_fusion.6), channel_id=1, source_target_pairs={{0,96},{32,0},{64,32},{96,64},{1,97},{33,1},{65,33},{97,65},{2,98}... | collective-permute-start | bytes 589832 | tf_op jit(solution)/shard_map/ppermute | solution.py:305
  19.6 0.8 collective-permute-start.7
  20.4 0.9 collective-permute-start.6
  21.3 0.7 pad_add_fusion.refs_0_
  22.0 0.6 add_convert_fusion
  22.6 5.7 %collective-permute-done.8 = bf16[4,192,128]{2,1,0:T(8,128)(2,1)S(1)} collective-permute-done((bf16[4,192,128]{2,1,0:T(8,128)(2,1)S(1)}, bf16[4,192,128]{2,1,0:T(8,128)(2,1)S(1)}, u32[]{:S(2)}, u32[]{:S(2)}) %collective-permute-start.8) | collective-permute-done | bytes 196640 | tf_op jit(solution)/shard_map/ppermute | solution.py:305
  28.3 0.7 collective-permute-done.7
  29.0 3.0 %collective-permute-done.6 = bf16[4,192,128]{2,1,0:T(8,128)(2,1)S(1)} collective-permute-done((bf16[4,192,128]{2,1,0:T(8,128)(2,1)S(1)}, bf16[4,192,128]{2,1,0:T(8,128)(2,1)S(1)}, u32[]{:S(2)}, u32[]{:S(2)}) %collective-permute-start.6) | collective-permute-done | bytes 196640 | tf_op jit(solution)/shard_map/ppermute | solution.py:305
  32.1 0.1 collective-permute-start.10
  32.2 0.5 copy-done.6
  32.7 0.3 copy-done.3
  33.0 14.2 %shard_map.58 = (f32[24,3072]{1,0:T(8,128)}, f32[24,3072]{1,0:T(8,128)}, f32[2,3072]{1,0:T(2,128)}) custom-call(s32[2]{0:T(128)} %pad_add_fusion.refs_0_, bf16[4,416,128]{2,1,0:T(8,128)(2,1)} %copy-done.1, bf16[4,416,128]{2,1,0:T(8,128)(2,1)} %copy-done.6, bf16[16,192,128]{2,1,0:T(8,128)(2,1)} %copy-done.3, f32[24,1]{1,0:T(8,128)} %get-tuple-element.105.refs_4_.refs_5_), custom_call_target="tpu_custom_call" | custom-call | flops 30000001024 | bytes 8000000 | tf_op jit(solution)/shard_map/pallas_call | solution.py:149
  47.2 0.9 copy-done.5
  48.1 14.2 %shard_map.59 = (f32[24,3072]{1,0:T(8,128)}, f32[24,3072]{1,0:T(8,128)}, f32[16,2,3072]{2,1,0:T(2,128)}) custom-call(s32[2]{0:T(128)} %pad_add_fusion.refs_0_, bf16[4,416,128]{2,1,0:T(8,128)(2,1)} %copy-done.1, bf16[4,416,128]{2,1,0:T(8,128)(2,1)} %copy-done.6, bf16[16,192,128]{2,1,0:T(8,128)(2,1)} %copy-done.5, f32[24,1]{1,0:T(8,128)} %get-tuple-element.104.refs_4_.refs_6_, ...), custom_call_target="tpu_custom_call" | custom-call | flops 30000001024 | bytes 8000000 | tf_op jit(solution)/shard_map/pallas_call | solution.py:149
  62.3 15.7 %all_to_all.10.refs_11_.refs_7_ = f32[16,2,3072]{2,1,0:T(2,128)} all-to-all(f32[16,2,3072]{2,1,0:T(2,128)} %get-tuple-element.62), channel_id=1, replica_groups=mesh['x'=4,'yl'=2,'z'=4,'yh'=2,'c'=2] {'yl','z','yh'}, dimensions={0} | all-to-all | bytes 786432 | tf_op jit(solution)/shard_map/all_to_all | solution.py:356
  78.0 20.6 %shard_map.60 = (f32[3072,128]{1,0:T(8,128)}, f32[3072,128]{1,0:T(8,128)}, bf16[2048,128]{1,0:T(8,128)(2,1)}, f32[8,128]{1,0:T(8,128)}) custom-call(s32[2]{0:T(128)} %pad_add_fusion.refs_0_, bf16[4,416,128]{2,1,0:T(8,128)(2,1)} %copy-done.1, bf16[4,416,128]{2,1,0:T(8,128)(2,1)} %copy-done.6, bf16[16,192,128]{2,1,0:T(8,128)(2,1)} %copy-done.3, ...), custom_call_target="tpu_custom_call" | custom-call | flops 30000001024 | bytes 8000000 | tf_op jit(solution)/shard_map/pallas_call | solution.py:245
  98.6 1.1 fusion.18
  99.7 0.6 collective-permute-start.13
  100.3 2.8 %collective-permute-start.11 = (bf16[2,256,128]{2,1,0:T(8,128)(2,1)S(1)}, bf16[2,256,128]{2,1,0:T(8,128)(2,1)S(1)}, u32[]{:S(2)}, u32[]{:S(2)}) collective-permute-start(bf16[2,256,128]{2,1,0:T(8,128)(2,1)S(1)} %bitcast.32), channel_id=1, source_target_pairs={{0,12},{4,0},{8,4},{12,8},{1,13},{5,1},{9,5},{13,9},{2,14},{6,2},{... | collective-permute-start | bytes 393224 | tf_op jit(solution)/shard_map/ppermute | solution.py:363
  103.0 7.5 %shard_map.61 = (f32[3072,128]{1,0:T(8,128)}, f32[1024,128]{1,0:T(8,128)}, f32[8,128]{1,0:T(8,128)}) custom-call(s32[2]{0:T(128)} %pad_add_fusion.refs_0_, bf16[4,416,128]{2,1,0:T(8,128)(2,1)} %copy-done.1, bf16[4,416,128]{2,1,0:T(8,128)(2,1)} %copy-done.6, bf16[16,192,128]{2,1,0:T(8,128)(2,1)} %copy-done.5, f32[24,1]{1,0:T(8,128)} %get-tuple-element.104.refs_4_.refs_6_, ...), custom_call_target="tpu_custom_call" | custom-call | flops 30000001024 | bytes 8000000 | tf_op jit(solution)/shard_map/pallas_call | solution.py:245
  110.6 0.5 collective-permute-start.16
  111.1 0.1 fusion
  111.2 0.7 collective-permute-start.14
  111.8 8.0 %shard_map.62 = (f32[3072,128]{1,0:T(8,128)}, bf16[2048,128]{1,0:T(8,128)(2,1)}, f32[8,128]{1,0:T(8,128)}) custom-call(s32[2]{0:T(128)} %pad_add_fusion.refs_0_, bf16[4,416,128]{2,1,0:T(8,128)(2,1)} %copy-done.1, bf16[4,416,128]{2,1,0:T(8,128)(2,1)} %copy-done.6, bf16[16,192,128]{2,1,0:T(8,128)(2,1)} %copy-done.3, ...), custom_call_target="tpu_custom_call" | custom-call | flops 30000001024 | bytes 8000000 | tf_op jit(solution)/shard_map/pallas_call | solution.py:245
  119.9 2.4 %collective-permute-start.15 = (f32[256,128]{1,0:T(8,128)S(1)}, f32[256,128]{1,0:T(8,128)S(1)}, u32[]{:S(2)}, u32[]{:S(2)}) collective-permute-start(f32[256,128]{1,0:T(8,128)S(1)} %fusion.1), channel_id=1, source_target_pairs={{0,2},{2,0},{1,3},{3,1},{4,6},{6,4},{5,7},{7,5},{8,10},{10,8},{9,1... | collective-permute-start | bytes 393224 | tf_op jit(solution)/shard_map/ppermute | solution.py:301
  122.3 0.6 copy-done.7
  122.9 0.6 copy-done.4
  123.5 2.9 %shard_map.63 = (f32[784,128]{1,0:T(8,128)}, bf16[784,128]{1,0:T(8,128)(2,1)}, bf16[784,128]{1,0:T(8,128)(2,1)}, bf16[784,128]{1,0:T(8,128)(2,1)}) custom-call(f32[3072,128]{1,0:T(8,128)} %get-tuple-element.69.own, f32[3072,128]{1,0:T(8,128)} %copy-done.4, f32[8,128]{1,0:T(8,128)} %get-tuple-element.71.loss_own, f32[8,128]{1,0:T(8,128)} %copy-done.7), custom_call_target="tpu_custom_call" | custom-call | flops 30000001024 | bytes 8000000 | tf_op jit(solution)/shard_map/pallas_call | solution.py:290
  126.3 0.9 collective-permute-start.18
  127.2 6.3 %all-to-all-start.1 = ((bf16[16,128,128]{2,1,0:T(8,128)(2,1)}), bf16[16,128,128]{2,1,0:T(8,128)(2,1)S(1)}, u32[]{:S(2)}, u32[]{:S(2)}) async-start(bf16[16,128,128]{2,1,0:T(8,128)(2,1)} %bitcast.15), calls=%async_computation.1 | async-start | bytes 1048576 | tf_op jit(solution)/shard_map/all_to_all | solution.py:381
  133.5 0.9 collective-permute-start.19
  134.4 1.2 collective-permute-start.20
  135.6 1.3 slice_reduce_fusion.3
  136.9 0.6 slice_reduce_fusion.2
  138.8 0.8 collective-permute-done.19
  139.6 2.0 %collective-permute-done.20 = bf16[784,128]{1,0:T(8,128)(2,1)S(1)} collective-permute-done((bf16[784,128]{1,0:T(8,128)(2,1)}, bf16[784,128]{1,0:T(8,128)(2,1)S(1)}, u32[]{:S(2)}, u32[]{:S(2)}) %collective-permute-start.20) | collective-permute-done | bytes 200736 | tf_op jit(solution)/shard_map/ppermute | solution.py:305
  141.6 0.6 slice_reduce_fusion.1
  142.2 0.6 slice_reduce_fusion
  144.1 0.1 add_add_fusion
  144.2 0.1 convert_reduce_fusion
  144.4 0.1 collective-permute-start.22
  144.4 3.5 %collective-permute-start.24 = (f32[192,128]{1,0:T(8,128)S(1)}, f32[192,128]{1,0:T(8,128)S(1)}, u32[]{:S(2)}, u32[]{:S(2)}) collective-permute-start(f32[192,128]{1,0:T(8,128)S(1)} %get-tuple-element.92), channel_id=1, source_target_pairs={{0,3},{1,2},{2,1},{3,0},{4,7},{5,6},{6,5},{7,4},{8,11},{9,10},{10,... | collective-permute-start | bytes 294920 | tf_op jit(solution)/shard_map/ppermute | solution.py:301
  147.9 0.2 collective-permute-start.23
  148.1 0.1 collective-permute-start.21
  148.2 2.8 %collective-permute-done.24 = f32[192,128]{1,0:T(8,128)S(1)} collective-permute-done((f32[192,128]{1,0:T(8,128)S(1)}, f32[192,128]{1,0:T(8,128)S(1)}, u32[]{:S(2)}, u32[]{:S(2)}) %collective-permute-start.24) | collective-permute-done | bytes 98336 | tf_op jit(solution)/shard_map/ppermute | solution.py:301
  151.1 3.2 %collective-permute-done.23 = f32[192,128]{1,0:T(8,128)S(1)} collective-permute-done((f32[192,128]{1,0:T(8,128)S(1)}, f32[192,128]{1,0:T(8,128)S(1)}, u32[]{:S(2)}, u32[]{:S(2)}) %collective-permute-start.23) | collective-permute-done | bytes 98336 | tf_op jit(solution)/shard_map/ppermute | solution.py:301
  154.3 0.8 pad_maximum_fusion.2
  155.1 0.8 pad_maximum_fusion.1
  (60 shorter events, 0.6 us)
Async XLA Ops:
  0.6 1.3 copy-start
  2.1 13.8 %collective-permute-start.5 = (bf16[416,128]{1,0:T(8,128)(2,1)S(1)}, bf16[416,128]{1,0:T(8,128)(2,1)S(1)}, u32[]{:S(2)}, u32[]{:S(2)}) collective-permute-start(bf16[416,128]{1,0:T(8,128)(2,1)S(1)} %constant_dynamic-update-slice_fusion), channel_id=1, source_target_pairs={{0,12},{4,0},{8,4},{12,8},{1,13},{5,1},{9,5},{13,9},{2,14},{6,2},{... | collective-permute-start | bytes 319496 | tf_op jit(solution)/shard_map/ppermute | solution.py:338
  6.3 9.6 %collective-permute-start.4 = (bf16[416,128]{1,0:T(8,128)(2,1)S(1)}, bf16[416,128]{1,0:T(8,128)(2,1)S(1)}, u32[]{:S(2)}, u32[]{:S(2)}) collective-permute-start(bf16[416,128]{1,0:T(8,128)(2,1)S(1)} %constant_dynamic-update-slice_fusion), channel_id=1, source_target_pairs={{0,8},{4,12},{8,0},{12,4},{1,9},{5,13},{9,1},{13,5},{2,10},{6,14},... | collective-permute-start | bytes 319496 | tf_op jit(solution)/shard_map/ppermute | solution.py:338
  6.3 9.6 %collective-permute-start.3 = (bf16[416,128]{1,0:T(8,128)(2,1)S(1)}, bf16[416,128]{1,0:T(8,128)(2,1)S(1)}, u32[]{:S(2)}, u32[]{:S(2)}) collective-permute-start(bf16[416,128]{1,0:T(8,128)(2,1)S(1)} %constant_dynamic-update-slice_fusion), channel_id=1, source_target_pairs={{0,4},{4,8},{8,12},{12,0},{1,5},{5,9},{9,13},{13,1},{2,6},{6,10},{... | collective-permute-start | bytes 319496 | tf_op jit(solution)/shard_map/ppermute | solution.py:338
  8.4 5.4 %collective-permute-start.2 = (bf16[1,192,128]{2,1,0:T(8,128)(2,1)S(1)}, bf16[1,192,128]{2,1,0:T(8,128)(2,1)S(1)}, u32[]{:S(2)}, u32[]{:S(2)}) collective-permute-start(bf16[1,192,128]{2,1,0:T(8,128)(2,1)S(1)} %get-tuple-element.96), channel_id=1, source_target_pairs={{0,3},{1,2},{2,1},{3,0},{4,7},{5,6},{6,5},{7,4},{8,11},{9,10},{10,... | collective-permute-start | bytes 147464 | tf_op jit(solution)/shard_map/ppermute | solution.py:301
  10.3 5.6 %collective-permute-start.1 = (bf16[1,192,128]{2,1,0:T(8,128)(2,1)S(1)}, bf16[1,192,128]{2,1,0:T(8,128)(2,1)S(1)}, u32[]{:S(2)}, u32[]{:S(2)}) collective-permute-start(bf16[1,192,128]{2,1,0:T(8,128)(2,1)S(1)} %get-tuple-element.97), channel_id=1, source_target_pairs={{0,2},{1,3},{2,0},{3,1},{4,6},{5,7},{6,4},{7,5},{8,10},{9,11},{10,... | collective-permute-start | bytes 147464 | tf_op jit(solution)/shard_map/ppermute | solution.py:301
  13.8 2.1 %collective-permute-start = (bf16[1,192,128]{2,1,0:T(8,128)(2,1)S(1)}, bf16[1,192,128]{2,1,0:T(8,128)(2,1)S(1)}, u32[]{:S(2)}, u32[]{:S(2)}) collective-permute-start(bf16[1,192,128]{2,1,0:T(8,128)(2,1)S(1)} %get-tuple-element.98), channel_id=1, source_target_pairs={{0,1},{1,0},{2,3},{3,2},{4,5},{5,4},{6,7},{7,6},{8,9},{9,8},{10,11... | collective-permute-start | bytes 147464 | tf_op jit(solution)/shard_map/ppermute | solution.py:301
  16.0 16.2 %copy-start.1 = (bf16[4,416,128]{2,1,0:T(8,128)(2,1)}, bf16[4,416,128]{2,1,0:T(8,128)(2,1)S(1)}, u32[]{:S(2)}) copy-start(bf16[4,416,128]{2,1,0:T(8,128)(2,1)S(1)} %pad_maximum_fusion.refs_1_) | copy-start | bytes 1277956
  16.0 16.0 %collective-permute-start.9 = (bf16[4,416,128]{2,1,0:T(8,128)(2,1)S(1)}, bf16[4,416,128]{2,1,0:T(8,128)(2,1)S(1)}, u32[]{:S(2)}, u32[]{:S(2)}) collective-permute-start(bf16[4,416,128]{2,1,0:T(8,128)(2,1)S(1)} %pad_maximum_fusion.refs_1_), channel_id=1, source_target_pairs={{0,16},{16,0},{1,17},{17,1},{2,18},{18,2},{3,19},{19,3},{4,20},{20... | collective-permute-start | bytes 1277960 | tf_op jit(solution)/shard_map/ppermute | solution.py:301
  16.8 11.5 %collective-permute-start.8 = (bf16[4,192,128]{2,1,0:T(8,128)(2,1)S(1)}, bf16[4,192,128]{2,1,0:T(8,128)(2,1)S(1)}, u32[]{:S(2)}, u32[]{:S(2)}) collective-permute-start(bf16[4,192,128]{2,1,0:T(8,128)(2,1)S(1)} %constant_dynamic-update-slice_fusion.6), channel_id=1, source_target_pairs={{0,96},{32,0},{64,32},{96,64},{1,97},{33,1},{65,33},{97,65},{2,98}... | collective-permute-start | bytes 589832 | tf_op jit(solution)/shard_map/ppermute | solution.py:305
  19.6 9.3 %collective-permute-start.7 = (bf16[4,192,128]{2,1,0:T(8,128)(2,1)S(1)}, bf16[4,192,128]{2,1,0:T(8,128)(2,1)S(1)}, u32[]{:S(2)}, u32[]{:S(2)}) collective-permute-start(bf16[4,192,128]{2,1,0:T(8,128)(2,1)S(1)} %constant_dynamic-update-slice_fusion.6), channel_id=1, source_target_pairs={{0,64},{32,96},{64,0},{96,32},{1,65},{33,97},{65,1},{97,33},{2,66}... | collective-permute-start | bytes 589832 | tf_op jit(solution)/shard_map/ppermute | solution.py:305
  20.4 11.5 %collective-permute-start.6 = (bf16[4,192,128]{2,1,0:T(8,128)(2,1)S(1)}, bf16[4,192,128]{2,1,0:T(8,128)(2,1)S(1)}, u32[]{:S(2)}, u32[]{:S(2)}) collective-permute-start(bf16[4,192,128]{2,1,0:T(8,128)(2,1)S(1)} %constant_dynamic-update-slice_fusion.6), channel_id=1, source_target_pairs={{0,32},{32,64},{64,96},{96,0},{1,33},{33,65},{65,97},{97,1},{2,34}... | collective-permute-start | bytes 589832 | tf_op jit(solution)/shard_map/ppermute | solution.py:305
  31.9 0.8 copy-start.6
  32.1 0.9 copy-start.3
  32.1 15.1 %collective-permute-start.10 = (bf16[16,192,128]{2,1,0:T(8,128)(2,1)S(1)}, bf16[16,192,128]{2,1,0:T(8,128)(2,1)S(1)}, u32[]{:S(2)}, u32[]{:S(2)}) collective-permute-start(bf16[16,192,128]{2,1,0:T(8,128)(2,1)S(1)} %constant_dynamic-update-slice_fusion.10.refs_3_), channel_id=1, source_target_pairs={{0,1},{1,0},{2,3},{3,2},{4,5},{5,4},{6,7},{7,6},{8,9},{9,8},{10,11... | collective-permute-start | bytes 2359304 | tf_op jit(solution)/shard_map/ppermute | solution.py:301
  47.2 0.9 copy-start.5
  99.7 11.4 %collective-permute-start.13 = (bf16[2,256,128]{2,1,0:T(8,128)(2,1)S(1)}, bf16[2,256,128]{2,1,0:T(8,128)(2,1)S(1)}, u32[]{:S(2)}, u32[]{:S(2)}) collective-permute-start(bf16[2,256,128]{2,1,0:T(8,128)(2,1)S(1)} %bitcast.33), channel_id=1, source_target_pairs={{0,4},{4,8},{8,12},{12,0},{1,5},{5,9},{9,13},{13,1},{2,6},{6,10},{... | collective-permute-start | bytes 393224 | tf_op jit(solution)/shard_map/ppermute | solution.py:363
  100.3 10.8 %collective-permute-start.11 = (bf16[2,256,128]{2,1,0:T(8,128)(2,1)S(1)}, bf16[2,256,128]{2,1,0:T(8,128)(2,1)S(1)}, u32[]{:S(2)}, u32[]{:S(2)}) collective-permute-start(bf16[2,256,128]{2,1,0:T(8,128)(2,1)S(1)} %bitcast.32), channel_id=1, source_target_pairs={{0,12},{4,0},{8,4},{12,8},{1,13},{5,1},{9,5},{13,9},{2,14},{6,2},{... | collective-permute-start | bytes 393224 | tf_op jit(solution)/shard_map/ppermute | solution.py:363
  103.0 8.1 %collective-permute-start.12 = (bf16[2,256,128]{2,1,0:T(8,128)(2,1)S(1)}, bf16[2,256,128]{2,1,0:T(8,128)(2,1)S(1)}, u32[]{:S(2)}, u32[]{:S(2)}) collective-permute-start(bf16[2,256,128]{2,1,0:T(8,128)(2,1)S(1)} %bitcast.31), channel_id=1, source_target_pairs={{0,8},{4,12},{8,0},{12,4},{1,9},{5,13},{9,1},{13,5},{2,10},{6,14},... | collective-permute-start | bytes 393224 | tf_op jit(solution)/shard_map/ppermute | solution.py:363
  110.6 11.7 %collective-permute-start.17 = (f32[8,128]{1,0:T(8,128)}, f32[8,128]{1,0:T(8,128)S(1)}, u32[]{:S(2)}, u32[]{:S(2)}) collective-permute-start(f32[8,128]{1,0:T(8,128)} %get-tuple-element.71.loss_own), channel_id=1, source_target_pairs={{0,1},{1,0},{2,3},{3,2},{4,5},{5,4},{6,7},{7,6},{8,9},{9,8},{10,11... | collective-permute-start | bytes 12296 | tf_op jit(solution)/shard_map/ppermute | solution.py:301
  110.6 11.7 %collective-permute-start.16 = (f32[3072,128]{1,0:T(8,128)}, f32[3072,128]{1,0:T(8,128)S(1)}, u32[]{:S(2)}, u32[]{:S(2)}) collective-permute-start(f32[3072,128]{1,0:T(8,128)} %get-tuple-element.70), channel_id=1, source_target_pairs={{0,1},{1,0},{2,3},{3,2},{4,5},{5,4},{6,7},{7,6},{8,9},{9,8},{10,11... | collective-permute-start | bytes 4718600 | tf_op jit(solution)/shard_map/ppermute | solution.py:301
  111.2 8.7 %collective-permute-start.14 = (f32[256,128]{1,0:T(8,128)S(1)}, f32[256,128]{1,0:T(8,128)S(1)}, u32[]{:S(2)}, u32[]{:S(2)}) collective-permute-start(f32[256,128]{1,0:T(8,128)S(1)} %slice_bitcast_fusion), channel_id=1, source_target_pairs={{0,16},{16,0},{1,17},{17,1},{2,18},{18,2},{3,19},{19,3},{4,20},{20... | collective-permute-start | bytes 393224 | tf_op jit(solution)/shard_map/ppermute | solution.py:301
  119.9 7.3 %collective-permute-start.15 = (f32[256,128]{1,0:T(8,128)S(1)}, f32[256,128]{1,0:T(8,128)S(1)}, u32[]{:S(2)}, u32[]{:S(2)}) collective-permute-start(f32[256,128]{1,0:T(8,128)S(1)} %fusion.1), channel_id=1, source_target_pairs={{0,2},{2,0},{1,3},{3,1},{4,6},{6,4},{5,7},{7,5},{8,10},{10,8},{9,1... | collective-permute-start | bytes 393224 | tf_op jit(solution)/shard_map/ppermute | solution.py:301
  122.3 0.6 copy-start.7
  122.3 1.2 copy-start.4
  126.3 10.6 %collective-permute-start.18 = (bf16[784,128]{1,0:T(8,128)(2,1)}, bf16[784,128]{1,0:T(8,128)(2,1)S(1)}, u32[]{:S(2)}, u32[]{:S(2)}) collective-permute-start(bf16[784,128]{1,0:T(8,128)(2,1)} %get-tuple-element.78), channel_id=1, source_target_pairs={{0,64},{32,96},{64,0},{96,32},{1,65},{33,97},{65,1},{97,33},{2,66}... | collective-permute-start | bytes 602120 | tf_op jit(solution)/shard_map/ppermute | solution.py:305
  127.2 16.9 %copy-start.2 = (f32[784,128]{1,0:T(8,128)S(1)}, f32[784,128]{1,0:T(8,128)}, u32[]{:S(2)}) copy-start(f32[784,128]{1,0:T(8,128)} %get-tuple-element.77) | copy-start | bytes 1204228
  127.2 17.0 %all-to-all-start.1 = ((bf16[16,128,128]{2,1,0:T(8,128)(2,1)}), bf16[16,128,128]{2,1,0:T(8,128)(2,1)S(1)}, u32[]{:S(2)}, u32[]{:S(2)}) async-start(bf16[16,128,128]{2,1,0:T(8,128)(2,1)} %bitcast.15), calls=%async_computation.1 | async-start | bytes 1048576 | tf_op jit(solution)/shard_map/all_to_all | solution.py:381
  133.5 6.1 %collective-permute-start.19 = (bf16[784,128]{1,0:T(8,128)(2,1)}, bf16[784,128]{1,0:T(8,128)(2,1)S(1)}, u32[]{:S(2)}, u32[]{:S(2)}) collective-permute-start(bf16[784,128]{1,0:T(8,128)(2,1)} %get-tuple-element.79), channel_id=1, source_target_pairs={{0,96},{32,0},{64,32},{96,64},{1,97},{33,1},{65,33},{97,65},{2,98}... | collective-permute-start | bytes 602120 | tf_op jit(solution)/shard_map/ppermute | solution.py:305
  134.4 7.1 %collective-permute-start.20 = (bf16[784,128]{1,0:T(8,128)(2,1)}, bf16[784,128]{1,0:T(8,128)(2,1)S(1)}, u32[]{:S(2)}, u32[]{:S(2)}) collective-permute-start(bf16[784,128]{1,0:T(8,128)(2,1)} %get-tuple-element.80), channel_id=1, source_target_pairs={{0,32},{32,64},{64,96},{96,0},{1,33},{33,65},{65,97},{97,1},{2,34}... | collective-permute-start | bytes 602120 | tf_op jit(solution)/shard_map/ppermute | solution.py:305
  144.4 3.9 %collective-permute-start.22 = (f32[192,128]{1,0:T(8,128)S(1)}, f32[192,128]{1,0:T(8,128)S(1)}, u32[]{:S(2)}, u32[]{:S(2)}) collective-permute-start(f32[192,128]{1,0:T(8,128)S(1)} %get-tuple-element.91), channel_id=1, source_target_pairs={{0,1},{1,0},{2,3},{3,2},{4,5},{5,4},{6,7},{7,6},{8,9},{9,8},{10,11... | collective-permute-start | bytes 294920 | tf_op jit(solution)/shard_map/ppermute | solution.py:301
  144.4 6.6 %collective-permute-start.24 = (f32[192,128]{1,0:T(8,128)S(1)}, f32[192,128]{1,0:T(8,128)S(1)}, u32[]{:S(2)}, u32[]{:S(2)}) collective-permute-start(f32[192,128]{1,0:T(8,128)S(1)} %get-tuple-element.92), channel_id=1, source_target_pairs={{0,3},{1,2},{2,1},{3,0},{4,7},{5,6},{6,5},{7,4},{8,11},{9,10},{10,... | collective-permute-start | bytes 294920 | tf_op jit(solution)/shard_map/ppermute | solution.py:301
  147.9 6.3 %collective-permute-start.23 = (f32[192,128]{1,0:T(8,128)S(1)}, f32[192,128]{1,0:T(8,128)S(1)}, u32[]{:S(2)}, u32[]{:S(2)}) collective-permute-start(f32[192,128]{1,0:T(8,128)S(1)} %get-tuple-element.93), channel_id=1, source_target_pairs={{0,2},{1,3},{2,0},{3,1},{4,6},{5,7},{6,4},{7,5},{8,10},{9,11},{10,... | collective-permute-start | bytes 294920 | tf_op jit(solution)/shard_map/ppermute | solution.py:301
  148.1 6.9 %collective-permute-start.21 = (f32[384,128]{1,0:T(8,128)S(1)}, f32[384,128]{1,0:T(8,128)S(1)}, u32[]{:S(2)}, u32[]{:S(2)}) collective-permute-start(f32[384,128]{1,0:T(8,128)S(1)} %pad_maximum_fusion.3), channel_id=1, source_target_pairs={{0,1},{1,0},{2,3},{3,2},{4,5},{5,4},{6,7},{7,6},{8,9},{9,8},{10,11... | collective-permute-start | bytes 589832 | tf_op jit(solution)/shard_map/ppermute | solution.py:301

commit v3 on v2

--- a/solution.py
+++ b/solution.py
@@ -163,109 +163,11 @@
     return outs[:slots], outs[slots : 2 * slots], outs[-1]
 
 
-def backward_kernel(number, slots, has_pg, has_qg, has_loss, doubled, *refs):
-    refs = list(refs)
-    place = refs.pop(0)
-    qins = [refs.pop(0) for _ in range(2)]
-    pins = [refs.pop(0) for _ in range(slots)]
-    ids = [refs.pop(0) for _ in range(slots)]
-    lses = [refs.pop(0) for _ in range(slots)]
-    tables = [refs.pop(0) for _ in range(slots)]
-    gathered = refs.pop(0)
-    pg_in = refs.pop(0) if has_pg else None
-    qg_in = refs.pop(0) if has_qg else None
-    loss_in = refs.pop(0) if has_loss else None
-    pgs = [refs.pop(0) for _ in range(slots)]
-    qg, loss, qs, ps, pt, pos, grad, mixed, gap = refs
-    load_queries((number,), qins, qs, pos)
-    load_passages(pins, ps)
-    pt[...] = ps[...].T
-    rows = chunk_rows(number)[1]
-    _, rows, lane = chunk_rows(number)
-    for peer in range(peers):
-        there = pl.ds(pl.multiple_of(lane + absolute(place, peer) * rows, rows), rows)
-        here = slice(peer * rows, (peer + 1) * rows)
-        parts = gathered[:, 0, there]
-        top = jnp.max(parts, axis=0, keepdims=True)
-        row_lse = top + jnp.log(jnp.sum(jnp.exp(parts - top), axis=0, keepdims=True))
-        positive = jnp.sum(gathered[:, 1, there], axis=0, keepdims=True)
-        ordered = pl.ds(pl.multiple_of(absolute(place, peer) * rows, rows), rows)
-        gap[0:1, ordered] = row_lse - positive
-        for slot in range(slots):
-            hit = (pos[0:1, here] == ids[slot][...]).astype(f32)
-            lines = slice(slot * span, (slot + 1) * span)
-            score = tables[slot][:, lane + peer * rows : lane + (peer + 1) * rows]
-            grad[lines, here] = jnp.exp(score - row_lse) - hit
-    value = jnp.sum(gap[...], axis=1, keepdims=True)
-    loss[...] = jnp.broadcast_to(value, loss.shape)
-    if has_loss:
-        loss[...] += loss_in[...]
-    for pg in pgs:
-        pg[...] = pg_in[...] if has_pg else jnp.zeros_like(pg)
-
-    @pl.loop(0, qs.shape[0] // block)
-    def _(step):
-        for piece in range(block // lane_tile):
-            here = pl.ds(pl.multiple_of(step * block + piece * lane_tile, lane_tile), lane_tile)
-            there = pl.ds(
-                pl.multiple_of(lane + step * block + piece * lane_tile, lane_tile), lane_tile
-            )
-            tile = qs[here, :]
-            for i in range(slots * span):
-                sims = lax.dot_general(
-                    ps[i * ptok : (i + 1) * ptok, :], tile, nt, preferred_element_type=f32
-                )
-                row = lses[i // span][i % span : i % span + 1, there]
-                weights = jnp.exp2((sims - row) * to_base2)
-                mixed[i * ptok : (i + 1) * ptok, piece * lane_tile : (piece + 1) * lane_tile] = (
-                    weights * grad[i : i + 1, here]
-                ).astype(bf16)
-        whole = pl.ds(pl.multiple_of(step * block, block), block)
-        for slot, pg in enumerate(pgs):
-            lines = slice(slot * span * ptok, (slot + 1) * span * ptok)
-            pg[...] += jnp.dot(mixed[lines, :], qs[whole, :], preferred_element_type=f32)
-        terms = jnp.dot(pt[...], mixed[...], preferred_element_type=f32).T
-        if has_qg:
-            terms = terms + qg_in[whole, :]
-        if doubled:
-            for part in range(block // rows):
-                start = absolute(place, step * (block // rows) + part) * (2 * rows)
-                piece = terms[part * rows : (part + 1) * rows].astype(qg.dtype)
-                for copy in range(2):
-                    qg[pl.ds(pl.multiple_of(start + copy * rows, rows), rows), :] = piece
-        else:
-            qg[whole, :] = terms.astype(qg.dtype)
-
-
-def backward(number, place, qins, pins, ids, lses, tables, gathered, before, doubled, kind):
-    lanes = peers * chunk_rows(number)[1]
-    slots = len(pins)
-    ops = [place, *qins, *pins, *ids, *lses, *tables, gathered] + [v for v in before if v is not None]
-    flags = [v is not None for v in before] + [doubled]
-    outs = pl.pallas_call(
-        lambda *refs: backward_kernel(number, slots, *flags, *refs),
-        out_shape=[jax.ShapeDtypeStruct((span * ptok, dim), f32)] * slots
-        + [
-            jax.ShapeDtypeStruct((2 * lanes if doubled else lanes, dim), kind),
-            jax.ShapeDtypeStruct((8, dim), f32),
-        ],
-        in_specs=[smem] + [vmem] * (len(ops) - 1),
-        scratch_shapes=[
-            pltpu.VMEM((lanes, dim), bf16),
-            pltpu.VMEM((slots * span * ptok, dim), bf16),
-            pltpu.VMEM((dim, slots * span * ptok), bf16),
-            pltpu.VMEM((1, lanes), f32),
-            pltpu.VMEM((slots * span, lanes), f32),
-            pltpu.VMEM((slots * span * ptok, block), bf16),
-            pltpu.VMEM((1, lanes), f32),
-        ],
-        compiler_params=params,
-        cost_estimate=cost,
-    )(*ops)
-    return outs[:slots], outs[slots], outs[slots + 1]
-
-
-def combine_kernel(own, other, loss_own, loss_other, *outs):
+def aligned(value, size):
+    return value if isinstance(value, int) else pl.multiple_of(value, size)
+
+
+def write_payload(own, other, loss_own, loss_other, outs):
     for x in range(4):
         out = outs[x]
         for k in range(6):
@@ -285,15 +187,117 @@
         out[4 * 6 * tokens :, :] = rows.astype(out.dtype)
 
 
-def combine(own, other, loss_own, loss_other):
-    rows = 4 * 6 * tokens + extra
+def backward_kernel(stage, numbers, *refs):
+    refs = list(refs)
+    place, qa, qb, pin, ids, lse, table, gathered = refs[:8]
+    del refs[:8]
+    qg_in = refs.pop(0) if stage > 0 else None
+    if stage == 2:
+        pg_in, other, loss_own, loss_other, *outs = refs[:8]
+        del refs[:8]
+        qg, qs, ps, pt, pos, grad, mixed, pg = refs
+    elif stage == 1:
+        pg, *parts_out, qs, ps, pt, pos, grad, mixed = refs
+    else:
+        pg, qg, loss, qs, ps, pt, pos, grad, mixed, gap = refs
+    load_queries(numbers, (qa, qb), qs, pos)
+    load_passages([pin], ps)
+    pt[...] = ps[...].T
+    first = chunk_rows(numbers[0])[2]
+    for number in numbers:
+        _, rows, lane = chunk_rows(number)
+        for peer in range(peers):
+            there = pl.ds(pl.multiple_of(lane + absolute(place, peer) * rows, rows), rows)
+            here = slice(lane - first + peer * rows, lane - first + (peer + 1) * rows)
+            parts = gathered[:, 0, there]
+            top = jnp.max(parts, axis=0, keepdims=True)
+            row_lse = top + jnp.log(jnp.sum(jnp.exp(parts - top), axis=0, keepdims=True))
+            if stage == 0:
+                gap[0:1, there] = row_lse - jnp.sum(gathered[:, 1, there], axis=0, keepdims=True)
+            hit = (pos[0:1, here] == ids[...]).astype(f32)
+            score = table[:, lane + peer * rows : lane + (peer + 1) * rows]
+            grad[:, here] = jnp.exp(score - row_lse) - hit
+    if stage == 0:
+        value = jnp.sum(gap[...], axis=1, keepdims=True)
+        loss[...] = jnp.broadcast_to(value, loss.shape)
+    pg[...] = pg_in[...] if stage == 2 else jnp.zeros_like(pg)
+
+    def work(step):
+        for piece in range(block // lane_tile):
+            start = aligned(step * block + piece * lane_tile, lane_tile)
+            here = pl.ds(start, lane_tile)
+            there = pl.ds(aligned(first + start, lane_tile), lane_tile)
+            tile = qs[here, :]
+            for i in range(span):
+                sims = lax.dot_general(
+                    ps[i * ptok : (i + 1) * ptok, :], tile, nt, preferred_element_type=f32
+                )
+                weights = jnp.exp2((sims - lse[i : i + 1, there]) * to_base2)
+                mixed[i * ptok : (i + 1) * ptok, piece * lane_tile : (piece + 1) * lane_tile] = (
+                    weights * grad[i : i + 1, here]
+                ).astype(bf16)
+        whole = pl.ds(aligned(step * block, block), block)
+        pg[...] += jnp.dot(mixed[...], qs[whole, :], preferred_element_type=f32)
+        terms = jnp.dot(pt[...], mixed[...], preferred_element_type=f32).T
+        if stage > 0:
+            terms = terms + qg_in[pl.ds(aligned(first + step * block, block), block), :]
+        if stage == 0:
+            qg[whole, :] = terms
+        elif stage == 1:
+            size = parts_out[0].shape[0]
+            for part in range(block // size):
+                parts_out[step * (block // size) + part][...] = terms[
+                    part * size : (part + 1) * size
+                ].astype(bf16)
+        else:
+            rows = chunk_rows(numbers[0])[1]
+            for part in range(block // rows):
+                start = absolute(place, step * (block // rows) + part) * (2 * rows)
+                piece = terms[part * rows : (part + 1) * rows].astype(qg.dtype)
+                for copy in range(2):
+                    qg[pl.ds(pl.multiple_of(start + copy * rows, rows), rows), :] = piece
+
+    if stage == 0:
+        pl.loop(0, qs.shape[0] // block)(work)
+    else:
+        for step in range(qs.shape[0] // block):
+            work(step)
+    if stage == 2:
+        write_payload(pg, other, loss_own, loss_other, outs)
+
+
+def backward(stage, *ops):
+    numbers = ((0, 1), (0,), (1,))[stage]
+    lanes = peers * sum(chunks[n] for n in numbers) * tokens
+    shape = jax.ShapeDtypeStruct
+    gradient = shape((span * ptok, dim), f32)
+    payload = 4 * 6 * tokens + extra
+    outs = [
+        [gradient, shape((lanes, dim), f32), shape((8, dim), f32)],
+        [gradient] + [shape((lanes // 4, dim), bf16)] * 4,
+        [shape((payload, dim), f32 if x == 0 else bf16) for x in range(4)]
+        + [shape((2 * lanes, dim), bf16)],
+    ][stage]
+    scratch = [
+        pltpu.VMEM((lanes, dim), bf16),
+        pltpu.VMEM((span * ptok, dim), bf16),
+        pltpu.VMEM((dim, span * ptok), bf16),
+        pltpu.VMEM((1, lanes), f32),
+        pltpu.VMEM((span, lanes), f32),
+        pltpu.VMEM((span * ptok, block), bf16),
+    ]
+    if stage == 0:
+        scratch.append(pltpu.VMEM((1, lanes), f32))
+    if stage == 2:
+        scratch.append(pltpu.VMEM((span * ptok, dim), f32))
     return pl.pallas_call(
-        combine_kernel,
-        out_shape=[jax.ShapeDtypeStruct((rows, dim), f32 if x == 0 else bf16) for x in range(4)],
-        in_specs=[vmem] * 4,
+        lambda *refs: backward_kernel(stage, numbers, *refs),
+        out_shape=outs,
+        in_specs=[smem] + [vmem] * (len(ops) - 1),
+        scratch_shapes=scratch,
         compiler_params=params,
         cost_estimate=cost,
-    )(own, other, loss_own, loss_other)
+    )(*ops)
 
 
 def exchange(value, axes, step):
@@ -355,35 +359,28 @@
     lse1, table1, part = forward(place, qins, pins[1:], ids[1:], part, 16)
     gathered = lax.all_to_all(part, group, 0, 0, tiled=True)
 
-    pgs, qg, loss = backward(
-        0, place, qins, pins, ids, lse0 + lse1, table0 + table1, gathered, (None,) * 3, False, bf16
-    )
-    qg = qg.reshape(4, 2, -1, dim)
-    terms = [qg[0]] + [
-        lax.ppermute(qg[s], "z", [(i, (i + 4 - s) % 4) for i in range(4)]) for s in (1, 2, 3)
+    common = (place, *qins)
+    own_side = (pins[0], ids[0], *lse0, *table0, gathered)
+    pg1, qg1, loss = backward(0, *common, pins[1], ids[1], *lse1, *table1, gathered)
+    other = exchange(pg1, "c", 1)
+    loss_other = exchange(loss, "c", 1)
+    pg0, *terms = backward(1, *common, *own_side, qg1)
+    terms = [terms[0]] + [
+        lax.ppermute(terms[s], "z", [(i, (i + 4 - s) % 4) for i in range(4)]) for s in (1, 2, 3)
     ]
-    terms = [t.astype(f32) for t in terms]
+    *sent, qg = backward(2, *common, *own_side, qg1, pg0, other, loss, loss_other)
+
+    sent, terms = lax.optimization_barrier((sent, terms))
+    landed = [sent[0]] + [rotate(sent[s], 4 - s) for s in (1, 2, 3)]
+    terms = [t.astype(f32).reshape(2, -1, dim) for t in terms]
     early = (terms[0] + terms[1]) + (terms[2] + terms[3])
     early = early[0] + exchange(early[1], "yl", 1)
+    qg, early = lax.optimization_barrier((qg, early))
+    arrived = lax.all_to_all(qg.reshape(16, -1, dim), group, 0, 0, tiled=True)
     early = early + exchange(early, "yh", 1)
-
-    (pg1,), qg, loss = backward(
-        1, place, qins, pins[1:], ids[1:], lse1, table1, gathered, (pgs[1], None, loss), False, f32
-    )
-    other = exchange(pg1, "c", 1)
-    loss_other = exchange(loss, "c", 1)
-    (pg0,), qg, _ = backward(
-        1, place, qins, pins[:1], ids[:1], lse0, table0, gathered, (pgs[0], qg, None), True, bf16
-    )
-
-    sent = combine(pg0, other, loss, loss_other)
-    qg, sent = lax.optimization_barrier((qg, sent))
-    arrived = lax.all_to_all(qg.reshape(16, -1, dim), group, 0, 0, tiled=True)
-    landed = [sent[0]] + [rotate(sent[s], 4 - s).astype(f32) for s in (1, 2, 3)]
+    landed = [part.astype(f32) for part in landed]
     summed = (landed[0] + landed[2]) + (landed[1] + landed[3])
-    arrived, summed = lax.optimization_barrier((arrived, summed))
-    values = [jnp.sum(part[4 * 6 * tokens : 4 * 6 * tokens + 3, 0]) for part in landed]
-    loss = ((values[0] + values[2]) + (values[1] + values[3])) / (768 * tokens)
+    loss = jnp.sum(summed[4 * 6 * tokens : 4 * 6 * tokens + 3, 0]) / (768 * tokens)
 
     rows = 6 * tokens
     done = jnp.concatenate([early, jnp.sum(arrived.astype(f32), axis=0)])

time: 158 us -> 148 us (0.937)
  other arithmetic: 6.45 us -> 3.82 us
  between operations: 4.68 us -> 2.75 us
  Pallas kernels: 67.4 us -> 65.8 us
    ppermute x6, waiting for transfers between devices: 12.1 us -> 9.4 us  [rotate(): return lax.ppermute(value, 'x', [(i, (i + step) % 4) for i in range(4)])]
    reduce_sum x4 -> x1, other arithmetic: 3.08 us -> 0.6 us  [body(): jnp.sum(summed[4 * 6 * tokens:4 * 6 * tokens + 3, 0]) / (768 * tokens)]
    pallas_call x4 -> x3, Pallas kernels: 39 us -> 37.4 us  [backward(): pl.pallas_call(lambda *refs: backward_kernel(stage, numbers, *refs), out_...]
  transfers between devices with their start and end apart: 26 -> 26, of which waited for: 9 -> 8; matrix products, arithmetic and copies ran while one was open for 4% -> 3% of each run, Pallas kernels for 21% -> 24%
where the time goes in v3:
time: 148 us
  Pallas kernels  65.8 us (44%)
  starting transfers between devices  34 us (23%)
  waiting for transfers between devices  20.7 us (14%)
  blocking collectives  15.6 us (11%)
  local copies, waits for them, and re-layouts  5.23 us (4%)
  other arithmetic  3.82 us (3%)
  between operations  2.75 us (2%)
    pallas_call x3, Pallas kernels, backward(): pl.pallas_call(lambda *refs: backward_kernel(stage, numbers, *refs), out_...  37.4 us
    pallas_call x2, Pallas kernels, forward(): pl.pallas_call(lambda *refs: forward_kernel(slots, first, copies, *refs),...  28.4 us
    all_to_all x1, blocking collectives, body(): gathered = lax.all_to_all(part, group, 0, 0, tiled=True)  15.6 us
    ppermute x13, starting transfers between devices, exchange(): return lax.ppermute(value, axes, [(i, i ^ step) for i in range(size)])  12.8 us
    ppermute x13, waiting for transfers between devices, exchange(): return lax.ppermute(value, axes, [(i, i ^ step) for i in range(size)])  11.3 us
    ppermute x6, waiting for transfers between devices, rotate(): return lax.ppermute(value, 'x', [(i, (i + step) % 4) for i in range(4)])  9.4 us
    ppermute x6, starting transfers between devices, rotate(): return lax.ppermute(value, 'x', [(i, (i + step) % 4) for i in range(4)])  7.32 us
    all_to_all x1, starting transfers between devices, body(): arrived = lax.all_to_all(qg.reshape(16, -1, dim), group, 0, 0, tiled=True)  5.86 us
  transfers between devices with their start and end apart: 26, of which 8 were waited for; matrix products, arithmetic and copies ran while one was open for 3% of the time, Pallas kernels for 24%

profile of v3, /device:TPU:0, one launch (start us, length us, event | category | flops | bytes accessed | tf_op | source)
XLA Modules:
  0.0 148.0 jit_solution(4043628294024930366)
XLA Ops:
  0.6 0.0 copy-start
  0.7 0.8 dynamic_slice.23
  1.4 0.1 slice.44
  1.5 0.1 broadcast_in_dim.12
  1.6 0.1 broadcast_in_dim.15
  1.6 0.1 reshape_reshape.4
  1.7 0.1 broadcast_in_dim.13
  1.8 0.1 broadcast_in_dim.14
  2.1 4.2 %collective-permute-start.5 = (bf16[416,128]{1,0:T(8,128)(2,1)S(1)}, bf16[416,128]{1,0:T(8,128)(2,1)S(1)}, u32[]{:S(2)}, u32[]{:S(2)}) collective-permute-start(bf16[416,128]{1,0:T(8,128)(2,1)S(1)} %constant_dynamic-update-slice_fusion), channel_id=1, source_target_pairs={{0,12},{4,0},{8,4},{12,8},{1,13},{5,1},{9,5},{13,9},{2,14},{6,2},{... | collective-permute-start | bytes 319496 | tf_op jit(solution)/shard_map/ppermute | solution.py:342
  6.3 0.0 collective-permute-start.4
  6.3 1.3 collective-permute-start.3
  7.5 0.9 constant_dynamic-slice_fusion.2
  8.4 1.9 %collective-permute-start.2 = (bf16[1,192,128]{2,1,0:T(8,128)(2,1)S(1)}, bf16[1,192,128]{2,1,0:T(8,128)(2,1)S(1)}, u32[]{:S(2)}, u32[]{:S(2)}) collective-permute-start(bf16[1,192,128]{2,1,0:T(8,128)(2,1)S(1)} %get-tuple-element.98), channel_id=1, source_target_pairs={{0,3},{1,2},{2,1},{3,0},{4,7},{5,6},{6,5},{7,4},{8,11},{9,10},{10,... | collective-permute-start | bytes 147464 | tf_op jit(solution)/shard_map/ppermute | solution.py:305
  10.3 1.5 %collective-permute-start.1 = (bf16[1,192,128]{2,1,0:T(8,128)(2,1)S(1)}, bf16[1,192,128]{2,1,0:T(8,128)(2,1)S(1)}, u32[]{:S(2)}, u32[]{:S(2)}) collective-permute-start(bf16[1,192,128]{2,1,0:T(8,128)(2,1)S(1)} %get-tuple-element.99), channel_id=1, source_target_pairs={{0,2},{1,3},{2,0},{3,1},{4,6},{5,7},{6,4},{7,5},{8,10},{9,11},{10,... | collective-permute-start | bytes 147464 | tf_op jit(solution)/shard_map/ppermute | solution.py:305
  11.8 2.0 %collective-permute-done.2 = bf16[1,192,128]{2,1,0:T(8,128)(2,1)S(1)} collective-permute-done((bf16[1,192,128]{2,1,0:T(8,128)(2,1)S(1)}, bf16[1,192,128]{2,1,0:T(8,128)(2,1)S(1)}, u32[]{:S(2)}, u32[]{:S(2)}) %collective-permute-start.2) | collective-permute-done | bytes 49184 | tf_op jit(solution)/shard_map/ppermute | solution.py:305
  13.8 0.1 collective-permute-start
  13.9 2.0 %collective-permute-done.1 = bf16[1,192,128]{2,1,0:T(8,128)(2,1)S(1)} collective-permute-done((bf16[1,192,128]{2,1,0:T(8,128)(2,1)S(1)}, bf16[1,192,128]{2,1,0:T(8,128)(2,1)S(1)}, u32[]{:S(2)}, u32[]{:S(2)}) %collective-permute-start.1) | collective-permute-done | bytes 49184 | tf_op jit(solution)/shard_map/ppermute | solution.py:305
  15.9 0.0 collective-permute-done.3
  15.9 0.1 pad_maximum_fusion.refs_1_
  16.0 0.8 collective-permute-start.9
  16.8 2.8 %collective-permute-start.8 = (bf16[4,192,128]{2,1,0:T(8,128)(2,1)S(1)}, bf16[4,192,128]{2,1,0:T(8,128)(2,1)S(1)}, u32[]{:S(2)}, u32[]{:S(2)}) collective-permute-start(bf16[4,192,128]{2,1,0:T(8,128)(2,1)S(1)} %constant_dynamic-update-slice_fusion.6), channel_id=1, source_target_pairs={{0,96},{32,0},{64,32},{96,64},{1,97},{33,1},{65,33},{97,65},{2,98}... | collective-permute-start | bytes 589832 | tf_op jit(solution)/shard_map/ppermute | solution.py:309
  19.6 0.8 collective-permute-start.7
  20.4 0.9 collective-permute-start.6
  21.3 0.6 pad_add_fusion.refs_0_
  21.9 0.6 add_convert_fusion
  22.5 5.7 %collective-permute-done.8 = bf16[4,192,128]{2,1,0:T(8,128)(2,1)S(1)} collective-permute-done((bf16[4,192,128]{2,1,0:T(8,128)(2,1)S(1)}, bf16[4,192,128]{2,1,0:T(8,128)(2,1)S(1)}, u32[]{:S(2)}, u32[]{:S(2)}) %collective-permute-start.8) | collective-permute-done | bytes 196640 | tf_op jit(solution)/shard_map/ppermute | solution.py:309
  28.3 0.7 collective-permute-done.7
  29.0 3.0 %collective-permute-done.6 = bf16[4,192,128]{2,1,0:T(8,128)(2,1)S(1)} collective-permute-done((bf16[4,192,128]{2,1,0:T(8,128)(2,1)S(1)}, bf16[4,192,128]{2,1,0:T(8,128)(2,1)S(1)}, u32[]{:S(2)}, u32[]{:S(2)}) %collective-permute-start.6) | collective-permute-done | bytes 196640 | tf_op jit(solution)/shard_map/ppermute | solution.py:309
  31.9 0.0 collective-permute-done.9.refs_2_
  32.1 0.1 collective-permute-start.10
  32.2 0.5 copy-done.7
  32.7 0.3 copy-done.4
  33.0 14.2 %shard_map.58 = (f32[24,3072]{1,0:T(8,128)}, f32[24,3072]{1,0:T(8,128)}, f32[2,3072]{1,0:T(2,128)}) custom-call(s32[2]{0:T(128)} %pad_add_fusion.refs_0_, bf16[4,416,128]{2,1,0:T(8,128)(2,1)} %copy-done.1, bf16[4,416,128]{2,1,0:T(8,128)(2,1)} %copy-done.7, bf16[16,192,128]{2,1,0:T(8,128)(2,1)} %copy-done.4, f32[24,1]{1,0:T(8,128)} %get-tuple-element.107.refs_4_), custom_call_target="tpu_custom_call" | custom-call | flops 30000001024 | bytes 8000000 | tf_op jit(solution)/shard_map/pallas_call | solution.py:149
  47.2 0.9 copy-done.6
  48.1 14.2 %shard_map.59 = (f32[24,3072]{1,0:T(8,128)}, f32[24,3072]{1,0:T(8,128)}, f32[16,2,3072]{2,1,0:T(2,128)}) custom-call(s32[2]{0:T(128)} %pad_add_fusion.refs_0_, bf16[4,416,128]{2,1,0:T(8,128)(2,1)} %copy-done.1, bf16[4,416,128]{2,1,0:T(8,128)(2,1)} %copy-done.7, bf16[16,192,128]{2,1,0:T(8,128)(2,1)} %copy-done.6, f32[24,1]{1,0:T(8,128)} %get-tuple-element.106.refs_4_, ...), custom_call_target="tpu_custom_call" | custom-call | flops 30000001024 | bytes 8000000 | tf_op jit(solution)/shard_map/pallas_call | solution.py:149
  62.3 15.6 %all_to_all.10.refs_7_ = f32[16,2,3072]{2,1,0:T(2,128)} all-to-all(f32[16,2,3072]{2,1,0:T(2,128)} %get-tuple-element.63), channel_id=1, replica_groups=mesh['x'=4,'yl'=2,'z'=4,'yh'=2,'c'=2] {'yl','z','yh'}, dimensions={0} | all-to-all | bytes 786432 | tf_op jit(solution)/shard_map/all_to_all | solution.py:360
  77.9 16.8 %shard_map.60 = (f32[3072,128]{1,0:T(8,128)}, f32[3072,128]{1,0:T(8,128)}, f32[8,128]{1,0:T(8,128)}) custom-call(s32[2]{0:T(128)} %pad_add_fusion.refs_0_, bf16[4,416,128]{2,1,0:T(8,128)(2,1)} %copy-done.1, bf16[4,416,128]{2,1,0:T(8,128)(2,1)} %copy-done.7, bf16[16,192,128]{2,1,0:T(8,128)(2,1)} %copy-done.6, f32[24,1]{1,0:T(8,128)} %get-tuple-element.106.refs_4_, ...), custom_call_target="tpu_custom_call" | custom-call | flops 30000001024 | bytes 8000000 | tf_op jit(solution)/shard_map/pallas_call | solution.py:293
  94.7 0.5 collective-permute-start.11
  95.2 12.0 %shard_map.61 = (f32[3072,128]{1,0:T(8,128)}, bf16[512,128]{1,0:T(8,128)(2,1)}, bf16[512,128]{1,0:T(8,128)(2,1)}, bf16[512,128]{1,0:T(8,128)(2,1)}, bf16[512,128]{1,0:T(8,128)(2,1)}) custom-call(s32[2]{0:T(128)} %pad_add_fusion.refs_0_, bf16[4,416,128]{2,1,0:T(8,128)(2,1)} %copy-done.1, bf16[4,416,128]{2,1,0:T(8,128)(2,1)} %copy-done.7, ...), custom_call_target="tpu_custom_call" | custom-call | flops 30000001024 | bytes 8000000 | tf_op jit(solution)/shard_map/pallas_call | solution.py:293
  107.2 1.2 collective-permute-start.13
  108.3 1.4 collective-permute-start.14
  109.7 0.0 collective-permute-start.15
  109.8 0.6 copy-done.8
  110.4 0.6 copy-done.5
  110.9 8.6 %shard_map.62 = (f32[784,128]{1,0:T(8,128)}, bf16[784,128]{1,0:T(8,128)(2,1)}, bf16[784,128]{1,0:T(8,128)(2,1)}, bf16[784,128]{1,0:T(8,128)(2,1)}, bf16[2048,128]{1,0:T(8,128)(2,1)}) custom-call(s32[2]{0:T(128)} %pad_add_fusion.refs_0_, bf16[4,416,128]{2,1,0:T(8,128)(2,1)} %copy-done.1, bf16[4,416,128]{2,1,0:T(8,128)(2,1)} %copy-done.7, ...), custom_call_target="tpu_custom_call" | custom-call | flops 30000001024 | bytes 8000000 | tf_op jit(solution)/shard_map/pallas_call | solution.py:293
  119.6 0.1 add_add_fusion.1
  119.7 0.7 collective-permute-start.16
  120.4 0.8 collective-permute-start.19
  121.1 0.9 collective-permute-start.20
  122.0 1.1 collective-permute-start.21
  123.2 1.6 %collective-permute-done.16 = f32[256,128]{1,0:T(8,128)S(1)} collective-permute-done((f32[256,128]{1,0:T(8,128)S(1)}, f32[256,128]{1,0:T(8,128)S(1)}, u32[]{:S(2)}, u32[]{:S(2)}) %collective-permute-start.16) | collective-permute-done | bytes 131104 | tf_op jit(solution)/shard_map/ppermute | solution.py:305
  124.8 5.9 %all-to-all-start.1 = ((bf16[16,128,128]{2,1,0:T(8,128)(2,1)}), bf16[16,128,128]{2,1,0:T(8,128)(2,1)S(1)}, u32[]{:S(2)}, u32[]{:S(2)}) async-start(bf16[16,128,128]{2,1,0:T(8,128)(2,1)} %bitcast.13), calls=%async_computation.1 | async-start | bytes 1048576 | tf_op jit(solution)/shard_map/all_to_all | solution.py:379
  130.6 3.4 %collective-permute-start.17 = (f32[256,128]{1,0:T(8,128)S(1)}, f32[256,128]{1,0:T(8,128)S(1)}, u32[]{:S(2)}, u32[]{:S(2)}) collective-permute-start(f32[256,128]{1,0:T(8,128)S(1)} %slice_add_fusion), channel_id=1, source_target_pairs={{0,2},{2,0},{1,3},{3,1},{4,6},{6,4},{5,7},{7,5},{8,10},{10,8},{9,1... | collective-permute-start | bytes 393224 | tf_op jit(solution)/shard_map/ppermute | solution.py:305
  134.1 0.1 add_add_fusion
  134.2 0.1 collective-permute-start.22
  134.3 0.8 collective-permute-start.24
  135.1 2.9 %collective-permute-start.23 = (f32[192,128]{1,0:T(8,128)S(1)}, f32[192,128]{1,0:T(8,128)S(1)}, u32[]{:S(2)}, u32[]{:S(2)}) collective-permute-start(f32[192,128]{1,0:T(8,128)S(1)} %get-tuple-element.95), channel_id=1, source_target_pairs={{0,2},{1,3},{2,0},{3,1},{4,6},{5,7},{6,4},{7,5},{8,10},{9,11},{10,... | collective-permute-start | bytes 294920 | tf_op jit(solution)/shard_map/ppermute | solution.py:305
  137.9 0.6 slice_reduce_fusion
  139.2 3.8 %collective-permute-done.17 = f32[256,128]{1,0:T(8,128)S(1)} collective-permute-done((f32[256,128]{1,0:T(8,128)S(1)}, f32[256,128]{1,0:T(8,128)S(1)}, u32[]{:S(2)}, u32[]{:S(2)}) %collective-permute-start.17) | collective-permute-done | bytes 131104 | tf_op jit(solution)/shard_map/ppermute | solution.py:305
  143.1 0.1 convert_reduce_fusion
  143.2 0.1 collective-permute-start.18
  143.3 1.9 %collective-permute-done.23 = f32[192,128]{1,0:T(8,128)S(1)} collective-permute-done((f32[192,128]{1,0:T(8,128)S(1)}, f32[192,128]{1,0:T(8,128)S(1)}, u32[]{:S(2)}, u32[]{:S(2)}) %collective-permute-start.23) | collective-permute-done | bytes 98336 | tf_op jit(solution)/shard_map/ppermute | solution.py:305
  145.2 0.8 pad_maximum_fusion.2
  146.1 0.8 pad_maximum_fusion.1
  (54 shorter events, 0.5 us)
Async XLA Ops:
  0.6 1.3 copy-start
  2.1 13.8 %collective-permute-start.5 = (bf16[416,128]{1,0:T(8,128)(2,1)S(1)}, bf16[416,128]{1,0:T(8,128)(2,1)S(1)}, u32[]{:S(2)}, u32[]{:S(2)}) collective-permute-start(bf16[416,128]{1,0:T(8,128)(2,1)S(1)} %constant_dynamic-update-slice_fusion), channel_id=1, source_target_pairs={{0,12},{4,0},{8,4},{12,8},{1,13},{5,1},{9,5},{13,9},{2,14},{6,2},{... | collective-permute-start | bytes 319496 | tf_op jit(solution)/shard_map/ppermute | solution.py:342
  6.3 9.6 %collective-permute-start.4 = (bf16[416,128]{1,0:T(8,128)(2,1)S(1)}, bf16[416,128]{1,0:T(8,128)(2,1)S(1)}, u32[]{:S(2)}, u32[]{:S(2)}) collective-permute-start(bf16[416,128]{1,0:T(8,128)(2,1)S(1)} %constant_dynamic-update-slice_fusion), channel_id=1, source_target_pairs={{0,8},{4,12},{8,0},{12,4},{1,9},{5,13},{9,1},{13,5},{2,10},{6,14},... | collective-permute-start | bytes 319496 | tf_op jit(solution)/shard_map/ppermute | solution.py:342
  6.3 9.6 %collective-permute-start.3 = (bf16[416,128]{1,0:T(8,128)(2,1)S(1)}, bf16[416,128]{1,0:T(8,128)(2,1)S(1)}, u32[]{:S(2)}, u32[]{:S(2)}) collective-permute-start(bf16[416,128]{1,0:T(8,128)(2,1)S(1)} %constant_dynamic-update-slice_fusion), channel_id=1, source_target_pairs={{0,4},{4,8},{8,12},{12,0},{1,5},{5,9},{9,13},{13,1},{2,6},{6,10},{... | collective-permute-start | bytes 319496 | tf_op jit(solution)/shard_map/ppermute | solution.py:342
  8.4 5.4 %collective-permute-start.2 = (bf16[1,192,128]{2,1,0:T(8,128)(2,1)S(1)}, bf16[1,192,128]{2,1,0:T(8,128)(2,1)S(1)}, u32[]{:S(2)}, u32[]{:S(2)}) collective-permute-start(bf16[1,192,128]{2,1,0:T(8,128)(2,1)S(1)} %get-tuple-element.98), channel_id=1, source_target_pairs={{0,3},{1,2},{2,1},{3,0},{4,7},{5,6},{6,5},{7,4},{8,11},{9,10},{10,... | collective-permute-start | bytes 147464 | tf_op jit(solution)/shard_map/ppermute | solution.py:305
  10.3 5.6 %collective-permute-start.1 = (bf16[1,192,128]{2,1,0:T(8,128)(2,1)S(1)}, bf16[1,192,128]{2,1,0:T(8,128)(2,1)S(1)}, u32[]{:S(2)}, u32[]{:S(2)}) collective-permute-start(bf16[1,192,128]{2,1,0:T(8,128)(2,1)S(1)} %get-tuple-element.99), channel_id=1, source_target_pairs={{0,2},{1,3},{2,0},{3,1},{4,6},{5,7},{6,4},{7,5},{8,10},{9,11},{10,... | collective-permute-start | bytes 147464 | tf_op jit(solution)/shard_map/ppermute | solution.py:305
  13.8 2.1 %collective-permute-start = (bf16[1,192,128]{2,1,0:T(8,128)(2,1)S(1)}, bf16[1,192,128]{2,1,0:T(8,128)(2,1)S(1)}, u32[]{:S(2)}, u32[]{:S(2)}) collective-permute-start(bf16[1,192,128]{2,1,0:T(8,128)(2,1)S(1)} %get-tuple-element.100), channel_id=1, source_target_pairs={{0,1},{1,0},{2,3},{3,2},{4,5},{5,4},{6,7},{7,6},{8,9},{9,8},{10,11... | collective-permute-start | bytes 147464 | tf_op jit(solution)/shard_map/ppermute | solution.py:305
  16.0 16.2 %copy-start.1 = (bf16[4,416,128]{2,1,0:T(8,128)(2,1)}, bf16[4,416,128]{2,1,0:T(8,128)(2,1)S(1)}, u32[]{:S(2)}) copy-start(bf16[4,416,128]{2,1,0:T(8,128)(2,1)S(1)} %pad_maximum_fusion.refs_1_) | copy-start | bytes 1277956
  16.0 16.0 %collective-permute-start.9 = (bf16[4,416,128]{2,1,0:T(8,128)(2,1)S(1)}, bf16[4,416,128]{2,1,0:T(8,128)(2,1)S(1)}, u32[]{:S(2)}, u32[]{:S(2)}) collective-permute-start(bf16[4,416,128]{2,1,0:T(8,128)(2,1)S(1)} %pad_maximum_fusion.refs_1_), channel_id=1, source_target_pairs={{0,16},{16,0},{1,17},{17,1},{2,18},{18,2},{3,19},{19,3},{4,20},{20... | collective-permute-start | bytes 1277960 | tf_op jit(solution)/shard_map/ppermute | solution.py:305
  16.8 11.5 %collective-permute-start.8 = (bf16[4,192,128]{2,1,0:T(8,128)(2,1)S(1)}, bf16[4,192,128]{2,1,0:T(8,128)(2,1)S(1)}, u32[]{:S(2)}, u32[]{:S(2)}) collective-permute-start(bf16[4,192,128]{2,1,0:T(8,128)(2,1)S(1)} %constant_dynamic-update-slice_fusion.6), channel_id=1, source_target_pairs={{0,96},{32,0},{64,32},{96,64},{1,97},{33,1},{65,33},{97,65},{2,98}... | collective-permute-start | bytes 589832 | tf_op jit(solution)/shard_map/ppermute | solution.py:309
  19.6 9.3 %collective-permute-start.7 = (bf16[4,192,128]{2,1,0:T(8,128)(2,1)S(1)}, bf16[4,192,128]{2,1,0:T(8,128)(2,1)S(1)}, u32[]{:S(2)}, u32[]{:S(2)}) collective-permute-start(bf16[4,192,128]{2,1,0:T(8,128)(2,1)S(1)} %constant_dynamic-update-slice_fusion.6), channel_id=1, source_target_pairs={{0,64},{32,96},{64,0},{96,32},{1,65},{33,97},{65,1},{97,33},{2,66}... | collective-permute-start | bytes 589832 | tf_op jit(solution)/shard_map/ppermute | solution.py:309
  20.4 11.5 %collective-permute-start.6 = (bf16[4,192,128]{2,1,0:T(8,128)(2,1)S(1)}, bf16[4,192,128]{2,1,0:T(8,128)(2,1)S(1)}, u32[]{:S(2)}, u32[]{:S(2)}) collective-permute-start(bf16[4,192,128]{2,1,0:T(8,128)(2,1)S(1)} %constant_dynamic-update-slice_fusion.6), channel_id=1, source_target_pairs={{0,32},{32,64},{64,96},{96,0},{1,33},{33,65},{65,97},{97,1},{2,34}... | collective-permute-start | bytes 589832 | tf_op jit(solution)/shard_map/ppermute | solution.py:309
  31.9 0.8 copy-start.7
  32.1 0.9 copy-start.4
  32.1 15.2 %collective-permute-start.10 = (bf16[16,192,128]{2,1,0:T(8,128)(2,1)S(1)}, bf16[16,192,128]{2,1,0:T(8,128)(2,1)S(1)}, u32[]{:S(2)}, u32[]{:S(2)}) collective-permute-start(bf16[16,192,128]{2,1,0:T(8,128)(2,1)S(1)} %constant_dynamic-update-slice_fusion.10.refs_3_), channel_id=1, source_target_pairs={{0,1},{1,0},{2,3},{3,2},{4,5},{5,4},{6,7},{7,6},{8,9},{9,8},{10,11... | collective-permute-start | bytes 2359304 | tf_op jit(solution)/shard_map/ppermute | solution.py:305
  47.2 0.9 copy-start.6
  94.7 15.1 %collective-permute-start.12 = (f32[8,128]{1,0:T(8,128)}, f32[8,128]{1,0:T(8,128)S(1)}, u32[]{:S(2)}, u32[]{:S(2)}) collective-permute-start(f32[8,128]{1,0:T(8,128)} %get-tuple-element.69.refs_11_), channel_id=1, source_target_pairs={{0,1},{1,0},{2,3},{3,2},{4,5},{5,4},{6,7},{7,6},{8,9},{9,8},{10,11... | collective-permute-start | bytes 12296 | tf_op jit(solution)/shard_map/ppermute | solution.py:305
  94.7 15.1 %collective-permute-start.11 = (f32[3072,128]{1,0:T(8,128)}, f32[3072,128]{1,0:T(8,128)S(1)}, u32[]{:S(2)}, u32[]{:S(2)}) collective-permute-start(f32[3072,128]{1,0:T(8,128)} %get-tuple-element.68), channel_id=1, source_target_pairs={{0,1},{1,0},{2,3},{3,2},{4,5},{5,4},{6,7},{7,6},{8,9},{9,8},{10,11... | collective-permute-start | bytes 4718600 | tf_op jit(solution)/shard_map/ppermute | solution.py:305
  107.2 12.4 %collective-permute-start.13 = (bf16[512,128]{1,0:T(8,128)(2,1)}, bf16[512,128]{1,0:T(8,128)(2,1)S(1)}, u32[]{:S(2)}, u32[]{:S(2)}) collective-permute-start(bf16[512,128]{1,0:T(8,128)(2,1)} %get-tuple-element.76), channel_id=1, source_target_pairs={{0,12},{4,0},{8,4},{12,8},{1,13},{5,1},{9,5},{13,9},{2,14},{6,2},{... | collective-permute-start | bytes 393224 | tf_op jit(solution)/shard_map/ppermute | solution.py:369
  108.3 11.2 %collective-permute-start.14 = (bf16[512,128]{1,0:T(8,128)(2,1)}, bf16[512,128]{1,0:T(8,128)(2,1)S(1)}, u32[]{:S(2)}, u32[]{:S(2)}) collective-permute-start(bf16[512,128]{1,0:T(8,128)(2,1)} %get-tuple-element.77), channel_id=1, source_target_pairs={{0,8},{4,12},{8,0},{12,4},{1,9},{5,13},{9,1},{13,5},{2,10},{6,14},... | collective-permute-start | bytes 393224 | tf_op jit(solution)/shard_map/ppermute | solution.py:369
  109.7 9.9 %collective-permute-start.15 = (bf16[512,128]{1,0:T(8,128)(2,1)}, bf16[512,128]{1,0:T(8,128)(2,1)S(1)}, u32[]{:S(2)}, u32[]{:S(2)}) collective-permute-start(bf16[512,128]{1,0:T(8,128)(2,1)} %get-tuple-element.78), channel_id=1, source_target_pairs={{0,4},{4,8},{8,12},{12,0},{1,5},{5,9},{9,13},{13,1},{2,6},{6,10},{... | collective-permute-start | bytes 393224 | tf_op jit(solution)/shard_map/ppermute | solution.py:369
  109.8 0.6 copy-start.8
  109.8 1.1 copy-start.5
  110.9 8.7 %copy-start.3 = (bf16[512,128]{1,0:T(8,128)(2,1)S(1)}, bf16[512,128]{1,0:T(8,128)(2,1)}, u32[]{:S(2)}) copy-start(bf16[512,128]{1,0:T(8,128)(2,1)} %get-tuple-element.79) | copy-start | bytes 393220
  119.6 14.5 %copy-start.2 = (f32[784,128]{1,0:T(8,128)S(1)}, f32[784,128]{1,0:T(8,128)}, u32[]{:S(2)}) copy-start(f32[784,128]{1,0:T(8,128)} %get-tuple-element.85) | copy-start | bytes 1204228
  119.7 5.0 %collective-permute-start.16 = (f32[256,128]{1,0:T(8,128)S(1)}, f32[256,128]{1,0:T(8,128)S(1)}, u32[]{:S(2)}, u32[]{:S(2)}) collective-permute-start(f32[256,128]{1,0:T(8,128)S(1)} %slice.53), channel_id=1, source_target_pairs={{0,16},{16,0},{1,17},{17,1},{2,18},{18,2},{3,19},{19,3},{4,20},{20... | collective-permute-start | bytes 393224 | tf_op jit(solution)/shard_map/ppermute | solution.py:305
  120.4 13.7 %collective-permute-start.19 = (bf16[784,128]{1,0:T(8,128)(2,1)}, bf16[784,128]{1,0:T(8,128)(2,1)S(1)}, u32[]{:S(2)}, u32[]{:S(2)}) collective-permute-start(bf16[784,128]{1,0:T(8,128)(2,1)} %get-tuple-element.86), channel_id=1, source_target_pairs={{0,64},{32,96},{64,0},{96,32},{1,65},{33,97},{65,1},{97,33},{2,66}... | collective-permute-start | bytes 602120 | tf_op jit(solution)/shard_map/ppermute | solution.py:309
  121.1 12.9 %collective-permute-start.20 = (bf16[784,128]{1,0:T(8,128)(2,1)}, bf16[784,128]{1,0:T(8,128)(2,1)S(1)}, u32[]{:S(2)}, u32[]{:S(2)}) collective-permute-start(bf16[784,128]{1,0:T(8,128)(2,1)} %get-tuple-element.87), channel_id=1, source_target_pairs={{0,96},{32,0},{64,32},{96,64},{1,97},{33,1},{65,33},{97,65},{2,98}... | collective-permute-start | bytes 602120 | tf_op jit(solution)/shard_map/ppermute | solution.py:309
  122.0 12.0 %collective-permute-start.21 = (bf16[784,128]{1,0:T(8,128)(2,1)}, bf16[784,128]{1,0:T(8,128)(2,1)S(1)}, u32[]{:S(2)}, u32[]{:S(2)}) collective-permute-start(bf16[784,128]{1,0:T(8,128)(2,1)} %get-tuple-element.88), channel_id=1, source_target_pairs={{0,32},{32,64},{64,96},{96,0},{1,33},{33,65},{65,97},{97,1},{2,34}... | collective-permute-start | bytes 602120 | tf_op jit(solution)/shard_map/ppermute | solution.py:309
  124.8 18.3 %all-to-all-start.1 = ((bf16[16,128,128]{2,1,0:T(8,128)(2,1)}), bf16[16,128,128]{2,1,0:T(8,128)(2,1)S(1)}, u32[]{:S(2)}, u32[]{:S(2)}) async-start(bf16[16,128,128]{2,1,0:T(8,128)(2,1)} %bitcast.13), calls=%async_computation.1 | async-start | bytes 1048576 | tf_op jit(solution)/shard_map/all_to_all | solution.py:379
  130.6 12.4 %collective-permute-start.17 = (f32[256,128]{1,0:T(8,128)S(1)}, f32[256,128]{1,0:T(8,128)S(1)}, u32[]{:S(2)}, u32[]{:S(2)}) collective-permute-start(f32[256,128]{1,0:T(8,128)S(1)} %slice_add_fusion), channel_id=1, source_target_pairs={{0,2},{2,0},{1,3},{3,1},{4,6},{6,4},{5,7},{7,5},{8,10},{10,8},{9,1... | collective-permute-start | bytes 393224 | tf_op jit(solution)/shard_map/ppermute | solution.py:305
  134.2 9.1 %collective-permute-start.22 = (f32[192,128]{1,0:T(8,128)S(1)}, f32[192,128]{1,0:T(8,128)S(1)}, u32[]{:S(2)}, u32[]{:S(2)}) collective-permute-start(f32[192,128]{1,0:T(8,128)S(1)} %get-tuple-element.93), channel_id=1, source_target_pairs={{0,1},{1,0},{2,3},{3,2},{4,5},{5,4},{6,7},{7,6},{8,9},{9,8},{10,11... | collective-permute-start | bytes 294920 | tf_op jit(solution)/shard_map/ppermute | solution.py:305
  134.3 9.0 %collective-permute-start.24 = (f32[192,128]{1,0:T(8,128)S(1)}, f32[192,128]{1,0:T(8,128)S(1)}, u32[]{:S(2)}, u32[]{:S(2)}) collective-permute-start(f32[192,128]{1,0:T(8,128)S(1)} %get-tuple-element.94), channel_id=1, source_target_pairs={{0,3},{1,2},{2,1},{3,0},{4,7},{5,6},{6,5},{7,4},{8,11},{9,10},{10,... | collective-permute-start | bytes 294920 | tf_op jit(solution)/shard_map/ppermute | solution.py:305
  135.1 10.1 %collective-permute-start.23 = (f32[192,128]{1,0:T(8,128)S(1)}, f32[192,128]{1,0:T(8,128)S(1)}, u32[]{:S(2)}, u32[]{:S(2)}) collective-permute-start(f32[192,128]{1,0:T(8,128)S(1)} %get-tuple-element.95), channel_id=1, source_target_pairs={{0,2},{1,3},{2,0},{3,1},{4,6},{5,7},{6,4},{7,5},{8,10},{9,11},{10,... | collective-permute-start | bytes 294920 | tf_op jit(solution)/shard_map/ppermute | solution.py:305
  143.2 2.8 %collective-permute-start.18 = (f32[384,128]{1,0:T(8,128)S(1)}, f32[384,128]{1,0:T(8,128)S(1)}, u32[]{:S(2)}, u32[]{:S(2)}) collective-permute-start(f32[384,128]{1,0:T(8,128)S(1)} %pad_maximum_fusion.3), channel_id=1, source_target_pairs={{0,1},{1,0},{2,3},{3,2},{4,5},{5,4},{6,7},{7,6},{8,9},{9,8},{10,11... | collective-permute-start | bytes 589832 | tf_op jit(solution)/shard_map/ppermute | solution.py:305

commit v4 on v3

--- a/solution.py
+++ b/solution.py
@@ -23,7 +23,7 @@
 block = 1024
 
 nt = (((1,), (1,)), ((), ()))
-params = pltpu.CompilerParams(vmem_limit_bytes=56 * 2**20)
+params = pltpu.CompilerParams(vmem_limit_bytes=36 * 2**20)
 cost = pl.CostEstimate(flops=3 * 10**10, bytes_accessed=8 * 10**6, transcendentals=10**7)
 smem = pl.BlockSpec(memory_space=pltpu.SMEM)
 vmem = pl.BlockSpec(memory_space=pltpu.VMEM)
@@ -91,10 +91,10 @@
     ]
     ones[...] = (groups[0] == groups[1]).astype(f32).astype(bf16)
 
-    @pl.loop(0, qs.shape[0] // (2 * lane_tile))
+    @pl.loop(0, qs.shape[0] // (4 * lane_tile))
     def _(step):
-        for side in range(2):
-            start = pl.multiple_of(step * (2 * lane_tile) + side * lane_tile, lane_tile)
+        for side in range(4):
+            start = pl.multiple_of(step * (4 * lane_tile) + side * lane_tile, lane_tile)
             here = pl.ds(start, lane_tile)
             tile = qs[here, :]
             for i in range(slots * span):
@@ -149,6 +149,7 @@
     outs = pl.pallas_call(
         lambda *refs: forward_kernel(slots, first, copies, *refs),
         out_shape=[jax.ShapeDtypeStruct(s, f32) for s in shapes],
+        out_specs=[vmem] * len(shapes),
         in_specs=[smem] + [vmem] * (len(ops) - 1),
         scratch_shapes=[
             pltpu.VMEM((lanes, dim), bf16),
@@ -293,6 +294,7 @@
     return pl.pallas_call(
         lambda *refs: backward_kernel(stage, numbers, *refs),
         out_shape=outs,
+        out_specs=[vmem] * len(outs),
         in_specs=[smem] + [vmem] * (len(ops) - 1),
         scratch_shapes=scratch,
         compiler_params=params,

time: 148 us -> 136 us (0.919)
  Pallas kernels: 65.8 us -> 54 us
  waiting for transfers between devices: 20.7 us -> 25.4 us
  local copies, waits for them, and re-layouts: 5.23 us -> 2.39 us
  starting transfers between devices: 34 us -> 32.2 us
    pallas_call x3, Pallas kernels: 37.4 us -> 29.6 us  [backward(): pl.pallas_call(lambda *refs: backward_kernel(stage, numbers, *refs), out_...]
    pallas_call x2, Pallas kernels: 28.4 us -> 24.4 us  [forward(): pl.pallas_call(lambda *refs: forward_kernel(slots, first, copies, *refs),...]
    unnamed x29 -> x13, local copies, waits for them, and re-layouts: 3 us -> 0.16 us
    ppermute x3, waiting for transfers between devices: 0.01 us -> 2.18 us  [body(): lax.ppermute(terms[s], 'z', [(i, (i + 4 - s) % 4) for i in range(4)])]
    all_to_all x1, starting transfers between devices: 5.86 us -> 3.83 us  [body(): arrived = lax.all_to_all(qg.reshape(16, -1, dim), group, 0, 0, tiled=True)]
  transfers between devices with their start and end apart: 26 -> 26, of which waited for: 8 -> 11; matrix products, arithmetic and copies ran while one was open for 3% -> 2% of each run, Pallas kernels for 24% -> 20%
where the time goes in v4:
time: 136 us; the launch traced here: 135 us
  Pallas kernels  54 us (40%)
  starting transfers between devices  32.2 us (24%)
  waiting for transfers between devices  25.4 us (19%)
  blocking collectives  15.8 us (12%)
  between operations  2.71 us (2%)
  other arithmetic  2.7 us (2%)
  local copies, waits for them, and re-layouts  2.39 us (2%)
    pallas_call x3, Pallas kernels, backward(): pl.pallas_call(lambda *refs: backward_kernel(stage, numbers, *refs), out_...  29.6 us
    pallas_call x2, Pallas kernels, forward(): pl.pallas_call(lambda *refs: forward_kernel(slots, first, copies, *refs),...  24.4 us
    all_to_all x1, blocking collectives, body(): gathered = lax.all_to_all(part, group, 0, 0, tiled=True)  15.8 us
    ppermute x13, starting transfers between devices, exchange(): return lax.ppermute(value, axes, [(i, i ^ step) for i in range(size)])  12.8 us
    ppermute x13, waiting for transfers between devices, exchange(): return lax.ppermute(value, axes, [(i, i ^ step) for i in range(size)])  12.4 us
    ppermute x6, waiting for transfers between devices, rotate(): return lax.ppermute(value, 'x', [(i, (i + step) % 4) for i in range(4)])  10.9 us
    ppermute x6, starting transfers between devices, rotate(): return lax.ppermute(value, 'x', [(i, (i + step) % 4) for i in range(4)])  7.37 us
    ppermute x3, starting transfers between devices, body(): lax.ppermute(piece, 'z', [(i, (i + s) % 4) for i in range(4)])  5.45 us
  transfers between devices with their start and end apart: 26, of which 11 were waited for; matrix products, arithmetic and copies ran while one was open for 2% of the time, Pallas kernels for 20%

profile of v4, /device:TPU:0, one launch (start us, length us, event | category | flops | bytes accessed | tf_op | source)
XLA Modules:
  0.0 135.2 jit_solution(9992949264287044970)
XLA Ops:
  0.6 0.0 copy-start
  0.7 0.8 dynamic_slice.23
  1.4 0.1 slice.44
  1.5 0.1 broadcast_in_dim.12
  1.6 0.1 broadcast_in_dim.15
  1.6 0.1 reshape_reshape.4
  1.7 0.1 broadcast_in_dim.13
  1.8 0.1 broadcast_in_dim.14
  2.1 4.2 %collective-permute-start.5 = (bf16[416,128]{1,0:T(8,128)(2,1)S(1)}, bf16[416,128]{1,0:T(8,128)(2,1)S(1)}, u32[]{:S(2)}, u32[]{:S(2)}) collective-permute-start(bf16[416,128]{1,0:T(8,128)(2,1)S(1)} %constant_dynamic-update-slice_fusion), channel_id=1, source_target_pairs={{0,12},{4,0},{8,4},{12,8},{1,13},{5,1},{9,5},{13,9},{2,14},{6,2},{... | collective-permute-start | bytes 319496 | tf_op jit(solution)/shard_map/ppermute | solution.py:344
  6.3 1.3 collective-permute-start.3
  7.5 0.9 constant_dynamic-slice_fusion.2
  8.4 1.9 %collective-permute-start.2 = (bf16[1,192,128]{2,1,0:T(8,128)(2,1)S(1)}, bf16[1,192,128]{2,1,0:T(8,128)(2,1)S(1)}, u32[]{:S(2)}, u32[]{:S(2)}) collective-permute-start(bf16[1,192,128]{2,1,0:T(8,128)(2,1)S(1)} %get-tuple-element.98), channel_id=1, source_target_pairs={{0,3},{1,2},{2,1},{3,0},{4,7},{5,6},{6,5},{7,4},{8,11},{9,10},{10,... | collective-permute-start | bytes 147464 | tf_op jit(solution)/shard_map/ppermute | solution.py:307
  10.3 1.5 %collective-permute-start.1 = (bf16[1,192,128]{2,1,0:T(8,128)(2,1)S(1)}, bf16[1,192,128]{2,1,0:T(8,128)(2,1)S(1)}, u32[]{:S(2)}, u32[]{:S(2)}) collective-permute-start(bf16[1,192,128]{2,1,0:T(8,128)(2,1)S(1)} %get-tuple-element.99), channel_id=1, source_target_pairs={{0,2},{1,3},{2,0},{3,1},{4,6},{5,7},{6,4},{7,5},{8,10},{9,11},{10,... | collective-permute-start | bytes 147464 | tf_op jit(solution)/shard_map/ppermute | solution.py:307
  11.8 2.0 %collective-permute-done.2 = bf16[1,192,128]{2,1,0:T(8,128)(2,1)S(1)} collective-permute-done((bf16[1,192,128]{2,1,0:T(8,128)(2,1)S(1)}, bf16[1,192,128]{2,1,0:T(8,128)(2,1)S(1)}, u32[]{:S(2)}, u32[]{:S(2)}) %collective-permute-start.2) | collective-permute-done | bytes 49184 | tf_op jit(solution)/shard_map/ppermute | solution.py:307
  13.8 0.1 collective-permute-start
  13.9 2.0 %collective-permute-done.1 = bf16[1,192,128]{2,1,0:T(8,128)(2,1)S(1)} collective-permute-done((bf16[1,192,128]{2,1,0:T(8,128)(2,1)S(1)}, bf16[1,192,128]{2,1,0:T(8,128)(2,1)S(1)}, u32[]{:S(2)}, u32[]{:S(2)}) %collective-permute-start.1) | collective-permute-done | bytes 49184 | tf_op jit(solution)/shard_map/ppermute | solution.py:307
  15.9 0.0 collective-permute-done
  15.9 0.0 collective-permute-done.5
  15.9 0.1 pad_maximum_fusion.refs_1_
  16.0 0.8 collective-permute-start.9
  16.8 2.8 %collective-permute-start.8 = (bf16[4,192,128]{2,1,0:T(8,128)(2,1)S(1)}, bf16[4,192,128]{2,1,0:T(8,128)(2,1)S(1)}, u32[]{:S(2)}, u32[]{:S(2)}) collective-permute-start(bf16[4,192,128]{2,1,0:T(8,128)(2,1)S(1)} %constant_dynamic-update-slice_fusion.6), channel_id=1, source_target_pairs={{0,96},{32,0},{64,32},{96,64},{1,97},{33,1},{65,33},{97,65},{2,98}... | collective-permute-start | bytes 589832 | tf_op jit(solution)/shard_map/ppermute | solution.py:311
  19.6 0.8 collective-permute-start.7
  20.4 0.9 collective-permute-start.6
  21.3 0.1 pad_add_fusion.refs_0_
  21.4 6.9 %collective-permute-done.8 = bf16[4,192,128]{2,1,0:T(8,128)(2,1)S(1)} collective-permute-done((bf16[4,192,128]{2,1,0:T(8,128)(2,1)S(1)}, bf16[4,192,128]{2,1,0:T(8,128)(2,1)S(1)}, u32[]{:S(2)}, u32[]{:S(2)}) %collective-permute-start.8) | collective-permute-done | bytes 196640 | tf_op jit(solution)/shard_map/ppermute | solution.py:311
  28.3 0.7 collective-permute-done.7
  29.0 3.0 %collective-permute-done.6 = bf16[4,192,128]{2,1,0:T(8,128)(2,1)S(1)} collective-permute-done((bf16[4,192,128]{2,1,0:T(8,128)(2,1)S(1)}, bf16[4,192,128]{2,1,0:T(8,128)(2,1)S(1)}, u32[]{:S(2)}, u32[]{:S(2)}) %collective-permute-start.6) | collective-permute-done | bytes 196640 | tf_op jit(solution)/shard_map/ppermute | solution.py:311
  32.1 0.1 collective-permute-start.10
  32.2 12.2 %shard_map.58 = (f32[24,3072]{1,0:T(8,128)S(1)}, f32[24,3072]{1,0:T(8,128)S(1)}, f32[2,3072]{1,0:T(2,128)S(1)}) custom-call(s32[2]{0:T(128)S(1)} %pad_add_fusion.refs_0_, bf16[4,416,128]{2,1,0:T(8,128)(2,1)S(1)} %pad_maximum_fusion.refs_1_, bf16[4,416,128]{2,1,0:T(8,128)(2,1)S(1)} %collective-permute-done.9.refs_2_, ...), custom_call_target="tpu_custom_call" | custom-call | flops 30000001024 | bytes 8000000 | tf_op jit(solution)/shard_map/pallas_call | solution.py:149
  44.4 0.0 collective-permute-done.10.refs_3_
  44.4 12.2 %shard_map.59 = (f32[24,3072]{1,0:T(8,128)S(1)}, f32[24,3072]{1,0:T(8,128)S(1)}, f32[16,2,3072]{2,1,0:T(2,128)S(1)}) custom-call(s32[2]{0:T(128)S(1)} %pad_add_fusion.refs_0_, bf16[4,416,128]{2,1,0:T(8,128)(2,1)S(1)} %pad_maximum_fusion.refs_1_, bf16[4,416,128]{2,1,0:T(8,128)(2,1)S(1)} %collective-permute-done.9.refs_2_, ...), custom_call_target="tpu_custom_call" | custom-call | flops 30000001024 | bytes 8000000 | tf_op jit(solution)/shard_map/pallas_call | solution.py:149
  56.6 15.8 %all_to_all.10.refs_7_ = f32[16,2,3072]{2,1,0:T(2,128)S(1)} all-to-all(f32[16,2,3072]{2,1,0:T(2,128)S(1)} %get-tuple-element.63), channel_id=1, replica_groups=mesh['x'=4,'yl'=2,'z'=4,'yh'=2,'c'=2] {'yl','z','yh'}, dimensions={0} | all-to-all | bytes 786432 | tf_op jit(solution)/shard_map/all_to_all | solution.py:362
  72.4 14.5 %shard_map.60 = (f32[3072,128]{1,0:T(8,128)S(1)}, f32[3072,128]{1,0:T(8,128)S(1)}, f32[8,128]{1,0:T(8,128)S(1)}) custom-call(s32[2]{0:T(128)S(1)} %pad_add_fusion.refs_0_, bf16[4,416,128]{2,1,0:T(8,128)(2,1)S(1)} %pad_maximum_fusion.refs_1_, bf16[4,416,128]{2,1,0:T(8,128)(2,1)S(1)} %collective-permute-done.9.refs_2_, ...), custom_call_target="tpu_custom_call" | custom-call | flops 30000001024 | bytes 8000000 | tf_op jit(solution)/shard_map/pallas_call | solution.py:294
  86.9 0.1 collective-permute-start.12
  87.0 0.5 collective-permute-start.11
  87.5 9.2 %shard_map.61 = (f32[3072,128]{1,0:T(8,128)S(1)}, bf16[512,128]{1,0:T(8,128)(2,1)S(1)}, bf16[512,128]{1,0:T(8,128)(2,1)S(1)}, bf16[512,128]{1,0:T(8,128)(2,1)S(1)}, bf16[512,128]{1,0:T(8,128)(2,1)S(1)}) custom-call(s32[2]{0:T(128)S(1)} %pad_add_fusion.refs_0_, bf16[4,416,128]{2,1,0:T(8,128)(2,1)S(1)} %pad_maximum_fusion.refs_1_, ...), custom_call_target="tpu_custom_call" | custom-call | flops 30000001024 | bytes 8000000 | tf_op jit(solution)/shard_map/pallas_call | solution.py:294
  96.7 1.2 collective-permute-start.13
  97.9 1.3 collective-permute-start.14
  99.2 0.1 collective-permute-start.15
  99.4 0.0 collective-permute-done.12.refs_12_
  99.4 0.0 collective-permute-done.11.refs_10_
  99.4 5.9 %shard_map.62 = (f32[784,128]{1,0:T(8,128)S(1)}, bf16[784,128]{1,0:T(8,128)(2,1)S(1)}, bf16[784,128]{1,0:T(8,128)(2,1)S(1)}, bf16[784,128]{1,0:T(8,128)(2,1)S(1)}, bf16[2048,128]{1,0:T(8,128)(2,1)}) custom-call(s32[2]{0:T(128)S(1)} %pad_add_fusion.refs_0_, bf16[4,416,128]{2,1,0:T(8,128)(2,1)S(1)} %pad_maximum_fusion.refs_1_, ...), custom_call_target="tpu_custom_call" | custom-call | flops 30000001024 | bytes 8000000 | tf_op jit(solution)/shard_map/pallas_call | solution.py:294
  105.3 0.5 collective-permute-done.14
  105.8 1.6 %collective-permute-done.15 = bf16[512,128]{1,0:T(8,128)(2,1)S(1)} collective-permute-done((bf16[512,128]{1,0:T(8,128)(2,1)S(1)}, bf16[512,128]{1,0:T(8,128)(2,1)S(1)}, u32[]{:S(2)}, u32[]{:S(2)}) %collective-permute-start.15) | collective-permute-done | bytes 131104 | tf_op jit(solution)/shard_map/ppermute | solution.py:371
  107.5 0.1 add_add_fusion.1
  107.5 0.7 collective-permute-start.16
  108.2 0.8 collective-permute-start.19
  109.0 1.2 collective-permute-start.20
  110.2 0.8 collective-permute-start.21
  111.1 1.8 %collective-permute-done.16 = f32[256,128]{1,0:T(8,128)S(1)} collective-permute-done((f32[256,128]{1,0:T(8,128)S(1)}, f32[256,128]{1,0:T(8,128)S(1)}, u32[]{:S(2)}, u32[]{:S(2)}) %collective-permute-start.16) | collective-permute-done | bytes 131104 | tf_op jit(solution)/shard_map/ppermute | solution.py:307
  112.9 3.8 %all-to-all-start.1 = ((bf16[16,128,128]{2,1,0:T(8,128)(2,1)}), bf16[16,128,128]{2,1,0:T(8,128)(2,1)S(1)}, u32[]{:S(2)}, u32[]{:S(2)}) async-start(bf16[16,128,128]{2,1,0:T(8,128)(2,1)} %bitcast.9), calls=%async_computation.1 | async-start | bytes 1048576 | tf_op jit(solution)/shard_map/all_to_all | solution.py:381
  116.7 3.4 %collective-permute-start.17 = (f32[256,128]{1,0:T(8,128)S(1)}, f32[256,128]{1,0:T(8,128)S(1)}, u32[]{:S(2)}, u32[]{:S(2)}) collective-permute-start(f32[256,128]{1,0:T(8,128)S(1)} %slice_add_fusion), channel_id=1, source_target_pairs={{0,2},{2,0},{1,3},{3,1},{4,6},{6,4},{5,7},{7,5},{8,10},{10,8},{9,1... | collective-permute-start | bytes 393224 | tf_op jit(solution)/shard_map/ppermute | solution.py:307
  120.2 0.3 collective-permute-done.21
  120.5 0.1 add_add_fusion
  120.6 0.1 collective-permute-start.22
  120.7 2.4 %collective-permute-start.24 = (f32[192,128]{1,0:T(8,128)S(1)}, f32[192,128]{1,0:T(8,128)S(1)}, u32[]{:S(2)}, u32[]{:S(2)}) collective-permute-start(f32[192,128]{1,0:T(8,128)S(1)} %get-tuple-element.94), channel_id=1, source_target_pairs={{0,3},{1,2},{2,1},{3,0},{4,7},{5,6},{6,5},{7,4},{8,11},{9,10},{10,... | collective-permute-start | bytes 294920 | tf_op jit(solution)/shard_map/ppermute | solution.py:307
  123.1 1.3 collective-permute-start.23
  124.4 0.6 slice_reduce_fusion
  125.6 4.7 %collective-permute-done.17 = f32[256,128]{1,0:T(8,128)S(1)} collective-permute-done((f32[256,128]{1,0:T(8,128)S(1)}, f32[256,128]{1,0:T(8,128)S(1)}, u32[]{:S(2)}, u32[]{:S(2)}) %collective-permute-start.17) | collective-permute-done | bytes 131104 | tf_op jit(solution)/shard_map/ppermute | solution.py:307
  130.4 0.1 convert_reduce_fusion
  130.5 0.1 collective-permute-start.18
  130.6 1.9 %collective-permute-done.23 = f32[192,128]{1,0:T(8,128)S(1)} collective-permute-done((f32[192,128]{1,0:T(8,128)S(1)}, f32[192,128]{1,0:T(8,128)S(1)}, u32[]{:S(2)}, u32[]{:S(2)}) %collective-permute-start.23) | collective-permute-done | bytes 98336 | tf_op jit(solution)/shard_map/ppermute | solution.py:307
  132.5 0.8 pad_maximum_fusion.2
  133.3 0.8 pad_maximum_fusion.1
  (38 shorter events, 0.5 us)
Async XLA Ops:
  0.6 1.3 copy-start
  2.1 13.8 %collective-permute-start.5 = (bf16[416,128]{1,0:T(8,128)(2,1)S(1)}, bf16[416,128]{1,0:T(8,128)(2,1)S(1)}, u32[]{:S(2)}, u32[]{:S(2)}) collective-permute-start(bf16[416,128]{1,0:T(8,128)(2,1)S(1)} %constant_dynamic-update-slice_fusion), channel_id=1, source_target_pairs={{0,12},{4,0},{8,4},{12,8},{1,13},{5,1},{9,5},{13,9},{2,14},{6,2},{... | collective-permute-start | bytes 319496 | tf_op jit(solution)/shard_map/ppermute | solution.py:344
  6.3 9.6 %collective-permute-start.4 = (bf16[416,128]{1,0:T(8,128)(2,1)S(1)}, bf16[416,128]{1,0:T(8,128)(2,1)S(1)}, u32[]{:S(2)}, u32[]{:S(2)}) collective-permute-start(bf16[416,128]{1,0:T(8,128)(2,1)S(1)} %constant_dynamic-update-slice_fusion), channel_id=1, source_target_pairs={{0,8},{4,12},{8,0},{12,4},{1,9},{5,13},{9,1},{13,5},{2,10},{6,14},... | collective-permute-start | bytes 319496 | tf_op jit(solution)/shard_map/ppermute | solution.py:344
  6.3 9.6 %collective-permute-start.3 = (bf16[416,128]{1,0:T(8,128)(2,1)S(1)}, bf16[416,128]{1,0:T(8,128)(2,1)S(1)}, u32[]{:S(2)}, u32[]{:S(2)}) collective-permute-start(bf16[416,128]{1,0:T(8,128)(2,1)S(1)} %constant_dynamic-update-slice_fusion), channel_id=1, source_target_pairs={{0,4},{4,8},{8,12},{12,0},{1,5},{5,9},{9,13},{13,1},{2,6},{6,10},{... | collective-permute-start | bytes 319496 | tf_op jit(solution)/shard_map/ppermute | solution.py:344
  8.4 5.4 %collective-permute-start.2 = (bf16[1,192,128]{2,1,0:T(8,128)(2,1)S(1)}, bf16[1,192,128]{2,1,0:T(8,128)(2,1)S(1)}, u32[]{:S(2)}, u32[]{:S(2)}) collective-permute-start(bf16[1,192,128]{2,1,0:T(8,128)(2,1)S(1)} %get-tuple-element.98), channel_id=1, source_target_pairs={{0,3},{1,2},{2,1},{3,0},{4,7},{5,6},{6,5},{7,4},{8,11},{9,10},{10,... | collective-permute-start | bytes 147464 | tf_op jit(solution)/shard_map/ppermute | solution.py:307
  10.3 5.6 %collective-permute-start.1 = (bf16[1,192,128]{2,1,0:T(8,128)(2,1)S(1)}, bf16[1,192,128]{2,1,0:T(8,128)(2,1)S(1)}, u32[]{:S(2)}, u32[]{:S(2)}) collective-permute-start(bf16[1,192,128]{2,1,0:T(8,128)(2,1)S(1)} %get-tuple-element.99), channel_id=1, source_target_pairs={{0,2},{1,3},{2,0},{3,1},{4,6},{5,7},{6,4},{7,5},{8,10},{9,11},{10,... | collective-permute-start | bytes 147464 | tf_op jit(solution)/shard_map/ppermute | solution.py:307
  13.8 2.1 %collective-permute-start = (bf16[1,192,128]{2,1,0:T(8,128)(2,1)S(1)}, bf16[1,192,128]{2,1,0:T(8,128)(2,1)S(1)}, u32[]{:S(2)}, u32[]{:S(2)}) collective-permute-start(bf16[1,192,128]{2,1,0:T(8,128)(2,1)S(1)} %get-tuple-element.100), channel_id=1, source_target_pairs={{0,1},{1,0},{2,3},{3,2},{4,5},{5,4},{6,7},{7,6},{8,9},{9,8},{10,11... | collective-permute-start | bytes 147464 | tf_op jit(solution)/shard_map/ppermute | solution.py:307
  16.0 16.0 %collective-permute-start.9 = (bf16[4,416,128]{2,1,0:T(8,128)(2,1)S(1)}, bf16[4,416,128]{2,1,0:T(8,128)(2,1)S(1)}, u32[]{:S(2)}, u32[]{:S(2)}) collective-permute-start(bf16[4,416,128]{2,1,0:T(8,128)(2,1)S(1)} %pad_maximum_fusion.refs_1_), channel_id=1, source_target_pairs={{0,16},{16,0},{1,17},{17,1},{2,18},{18,2},{3,19},{19,3},{4,20},{20... | collective-permute-start | bytes 1277960 | tf_op jit(solution)/shard_map/ppermute | solution.py:307
  16.8 11.5 %collective-permute-start.8 = (bf16[4,192,128]{2,1,0:T(8,128)(2,1)S(1)}, bf16[4,192,128]{2,1,0:T(8,128)(2,1)S(1)}, u32[]{:S(2)}, u32[]{:S(2)}) collective-permute-start(bf16[4,192,128]{2,1,0:T(8,128)(2,1)S(1)} %constant_dynamic-update-slice_fusion.6), channel_id=1, source_target_pairs={{0,96},{32,0},{64,32},{96,64},{1,97},{33,1},{65,33},{97,65},{2,98}... | collective-permute-start | bytes 589832 | tf_op jit(solution)/shard_map/ppermute | solution.py:311
  19.6 9.3 %collective-permute-start.7 = (bf16[4,192,128]{2,1,0:T(8,128)(2,1)S(1)}, bf16[4,192,128]{2,1,0:T(8,128)(2,1)S(1)}, u32[]{:S(2)}, u32[]{:S(2)}) collective-permute-start(bf16[4,192,128]{2,1,0:T(8,128)(2,1)S(1)} %constant_dynamic-update-slice_fusion.6), channel_id=1, source_target_pairs={{0,64},{32,96},{64,0},{96,32},{1,65},{33,97},{65,1},{97,33},{2,66}... | collective-permute-start | bytes 589832 | tf_op jit(solution)/shard_map/ppermute | solution.py:311
  20.4 11.5 %collective-permute-start.6 = (bf16[4,192,128]{2,1,0:T(8,128)(2,1)S(1)}, bf16[4,192,128]{2,1,0:T(8,128)(2,1)S(1)}, u32[]{:S(2)}, u32[]{:S(2)}) collective-permute-start(bf16[4,192,128]{2,1,0:T(8,128)(2,1)S(1)} %constant_dynamic-update-slice_fusion.6), channel_id=1, source_target_pairs={{0,32},{32,64},{64,96},{96,0},{1,33},{33,65},{65,97},{97,1},{2,34}... | collective-permute-start | bytes 589832 | tf_op jit(solution)/shard_map/ppermute | solution.py:311
  32.1 12.3 %collective-permute-start.10 = (bf16[16,192,128]{2,1,0:T(8,128)(2,1)S(1)}, bf16[16,192,128]{2,1,0:T(8,128)(2,1)S(1)}, u32[]{:S(2)}, u32[]{:S(2)}) collective-permute-start(bf16[16,192,128]{2,1,0:T(8,128)(2,1)S(1)} %constant_dynamic-update-slice_fusion.10.refs_3_), channel_id=1, source_target_pairs={{0,1},{1,0},{2,3},{3,2},{4,5},{5,4},{6,7},{7,6},{8,9},{9,8},{10,11... | collective-permute-start | bytes 2359304 | tf_op jit(solution)/shard_map/ppermute | solution.py:307
  86.9 12.4 %collective-permute-start.12 = (f32[8,128]{1,0:T(8,128)S(1)}, f32[8,128]{1,0:T(8,128)S(1)}, u32[]{:S(2)}, u32[]{:S(2)}) collective-permute-start(f32[8,128]{1,0:T(8,128)S(1)} %get-tuple-element.69.refs_11_), channel_id=1, source_target_pairs={{0,1},{1,0},{2,3},{3,2},{4,5},{5,4},{6,7},{7,6},{8,9},{9,8},{10,11... | collective-permute-start | bytes 12296 | tf_op jit(solution)/shard_map/ppermute | solution.py:307
  87.0 12.4 %collective-permute-start.11 = (f32[3072,128]{1,0:T(8,128)S(1)}, f32[3072,128]{1,0:T(8,128)S(1)}, u32[]{:S(2)}, u32[]{:S(2)}) collective-permute-start(f32[3072,128]{1,0:T(8,128)S(1)} %get-tuple-element.68), channel_id=1, source_target_pairs={{0,1},{1,0},{2,3},{3,2},{4,5},{5,4},{6,7},{7,6},{8,9},{9,8},{10,11... | collective-permute-start | bytes 4718600 | tf_op jit(solution)/shard_map/ppermute | solution.py:307
  96.7 8.6 %collective-permute-start.13 = (bf16[512,128]{1,0:T(8,128)(2,1)S(1)}, bf16[512,128]{1,0:T(8,128)(2,1)S(1)}, u32[]{:S(2)}, u32[]{:S(2)}) collective-permute-start(bf16[512,128]{1,0:T(8,128)(2,1)S(1)} %get-tuple-element.76), channel_id=1, source_target_pairs={{0,12},{4,0},{8,4},{12,8},{1,13},{5,1},{9,5},{13,9},{2,14},{6,2},{... | collective-permute-start | bytes 393224 | tf_op jit(solution)/shard_map/ppermute | solution.py:371
  97.9 7.9 %collective-permute-start.14 = (bf16[512,128]{1,0:T(8,128)(2,1)S(1)}, bf16[512,128]{1,0:T(8,128)(2,1)S(1)}, u32[]{:S(2)}, u32[]{:S(2)}) collective-permute-start(bf16[512,128]{1,0:T(8,128)(2,1)S(1)} %get-tuple-element.77), channel_id=1, source_target_pairs={{0,8},{4,12},{8,0},{12,4},{1,9},{5,13},{9,1},{13,5},{2,10},{6,14},... | collective-permute-start | bytes 393224 | tf_op jit(solution)/shard_map/ppermute | solution.py:371
  99.2 8.2 %collective-permute-start.15 = (bf16[512,128]{1,0:T(8,128)(2,1)S(1)}, bf16[512,128]{1,0:T(8,128)(2,1)S(1)}, u32[]{:S(2)}, u32[]{:S(2)}) collective-permute-start(bf16[512,128]{1,0:T(8,128)(2,1)S(1)} %get-tuple-element.78), channel_id=1, source_target_pairs={{0,4},{4,8},{8,12},{12,0},{1,5},{5,9},{9,13},{13,1},{2,6},{6,10},{... | collective-permute-start | bytes 393224 | tf_op jit(solution)/shard_map/ppermute | solution.py:371
  107.5 5.3 %collective-permute-start.16 = (f32[256,128]{1,0:T(8,128)S(1)}, f32[256,128]{1,0:T(8,128)S(1)}, u32[]{:S(2)}, u32[]{:S(2)}) collective-permute-start(f32[256,128]{1,0:T(8,128)S(1)} %slice.53), channel_id=1, source_target_pairs={{0,16},{16,0},{1,17},{17,1},{2,18},{18,2},{3,19},{19,3},{4,20},{20... | collective-permute-start | bytes 393224 | tf_op jit(solution)/shard_map/ppermute | solution.py:307
  108.2 12.0 %collective-permute-start.19 = (bf16[784,128]{1,0:T(8,128)(2,1)S(1)}, bf16[784,128]{1,0:T(8,128)(2,1)S(1)}, u32[]{:S(2)}, u32[]{:S(2)}) collective-permute-start(bf16[784,128]{1,0:T(8,128)(2,1)S(1)} %get-tuple-element.86), channel_id=1, source_target_pairs={{0,64},{32,96},{64,0},{96,32},{1,65},{33,97},{65,1},{97,33},{2,66}... | collective-permute-start | bytes 602120 | tf_op jit(solution)/shard_map/ppermute | solution.py:311
  109.0 11.1 %collective-permute-start.20 = (bf16[784,128]{1,0:T(8,128)(2,1)S(1)}, bf16[784,128]{1,0:T(8,128)(2,1)S(1)}, u32[]{:S(2)}, u32[]{:S(2)}) collective-permute-start(bf16[784,128]{1,0:T(8,128)(2,1)S(1)} %get-tuple-element.87), channel_id=1, source_target_pairs={{0,96},{32,0},{64,32},{96,64},{1,97},{33,1},{65,33},{97,65},{2,98}... | collective-permute-start | bytes 602120 | tf_op jit(solution)/shard_map/ppermute | solution.py:311
  110.2 10.3 %collective-permute-start.21 = (bf16[784,128]{1,0:T(8,128)(2,1)S(1)}, bf16[784,128]{1,0:T(8,128)(2,1)S(1)}, u32[]{:S(2)}, u32[]{:S(2)}) collective-permute-start(bf16[784,128]{1,0:T(8,128)(2,1)S(1)} %get-tuple-element.88), channel_id=1, source_target_pairs={{0,32},{32,64},{64,96},{96,0},{1,33},{33,65},{65,97},{97,1},{2,34}... | collective-permute-start | bytes 602120 | tf_op jit(solution)/shard_map/ppermute | solution.py:311
  112.9 17.5 %all-to-all-start.1 = ((bf16[16,128,128]{2,1,0:T(8,128)(2,1)}), bf16[16,128,128]{2,1,0:T(8,128)(2,1)S(1)}, u32[]{:S(2)}, u32[]{:S(2)}) async-start(bf16[16,128,128]{2,1,0:T(8,128)(2,1)} %bitcast.9), calls=%async_computation.1 | async-start | bytes 1048576 | tf_op jit(solution)/shard_map/all_to_all | solution.py:381
  116.7 13.6 %collective-permute-start.17 = (f32[256,128]{1,0:T(8,128)S(1)}, f32[256,128]{1,0:T(8,128)S(1)}, u32[]{:S(2)}, u32[]{:S(2)}) collective-permute-start(f32[256,128]{1,0:T(8,128)S(1)} %slice_add_fusion), channel_id=1, source_target_pairs={{0,2},{2,0},{1,3},{3,1},{4,6},{6,4},{5,7},{7,5},{8,10},{10,8},{9,1... | collective-permute-start | bytes 393224 | tf_op jit(solution)/shard_map/ppermute | solution.py:307
  120.6 9.9 %collective-permute-start.22 = (f32[192,128]{1,0:T(8,128)S(1)}, f32[192,128]{1,0:T(8,128)S(1)}, u32[]{:S(2)}, u32[]{:S(2)}) collective-permute-start(f32[192,128]{1,0:T(8,128)S(1)} %get-tuple-element.93), channel_id=1, source_target_pairs={{0,1},{1,0},{2,3},{3,2},{4,5},{5,4},{6,7},{7,6},{8,9},{9,8},{10,11... | collective-permute-start | bytes 294920 | tf_op jit(solution)/shard_map/ppermute | solution.py:307
  120.7 9.9 %collective-permute-start.24 = (f32[192,128]{1,0:T(8,128)S(1)}, f32[192,128]{1,0:T(8,128)S(1)}, u32[]{:S(2)}, u32[]{:S(2)}) collective-permute-start(f32[192,128]{1,0:T(8,128)S(1)} %get-tuple-element.94), channel_id=1, source_target_pairs={{0,3},{1,2},{2,1},{3,0},{4,7},{5,6},{6,5},{7,4},{8,11},{9,10},{10,... | collective-permute-start | bytes 294920 | tf_op jit(solution)/shard_map/ppermute | solution.py:307
  123.1 9.4 %collective-permute-start.23 = (f32[192,128]{1,0:T(8,128)S(1)}, f32[192,128]{1,0:T(8,128)S(1)}, u32[]{:S(2)}, u32[]{:S(2)}) collective-permute-start(f32[192,128]{1,0:T(8,128)S(1)} %get-tuple-element.95), channel_id=1, source_target_pairs={{0,2},{1,3},{2,0},{3,1},{4,6},{5,7},{6,4},{7,5},{8,10},{9,11},{10,... | collective-permute-start | bytes 294920 | tf_op jit(solution)/shard_map/ppermute | solution.py:307
  130.5 2.8 %collective-permute-start.18 = (f32[384,128]{1,0:T(8,128)S(1)}, f32[384,128]{1,0:T(8,128)S(1)}, u32[]{:S(2)}, u32[]{:S(2)}) collective-permute-start(f32[384,128]{1,0:T(8,128)S(1)} %pad_maximum_fusion.3), channel_id=1, source_target_pairs={{0,1},{1,0},{2,3},{3,2},{4,5},{5,4},{6,7},{7,6},{8,9},{9,8},{10,11... | collective-permute-start | bytes 589832 | tf_op jit(solution)/shard_map/ppermute | solution.py:307

commit v5 on v4

--- a/solution.py
+++ b/solution.py
@@ -372,7 +372,7 @@
     ]
     *sent, qg = backward(2, *common, *own_side, qg1, pg0, other, loss, loss_other)
 
-    sent, terms = lax.optimization_barrier((sent, terms))
+    sent, terms[1], terms[3] = lax.optimization_barrier((sent, terms[1], terms[3]))
     landed = [sent[0]] + [rotate(sent[s], 4 - s) for s in (1, 2, 3)]
     terms = [t.astype(f32).reshape(2, -1, dim) for t in terms]
     early = (terms[0] + terms[1]) + (terms[2] + terms[3])

time: 136 us -> 134 us (0.985)
  waiting for transfers between devices: 25.4 us -> 23.3 us
  transfers between devices with their start and end apart: 26 -> 26, of which waited for: 11 -> 10; matrix products, arithmetic and copies ran while one was open for 2% -> 2% of each run, Pallas kernels for 20% -> 20%
where the time goes in v5:
time: 134 us; the launch traced here: 133 us
  Pallas kernels  54 us (40%)
  starting transfers between devices  32.4 us (24%)
  waiting for transfers between devices  23.3 us (17%)
  blocking collectives  15.8 us (12%)
  between operations  2.71 us (2%)
  other arithmetic  2.7 us (2%)
  local copies, waits for them, and re-layouts  2.39 us (2%)
    pallas_call x3, Pallas kernels, backward(): pl.pallas_call(lambda *refs: backward_kernel(stage, numbers, *refs), out_...  29.6 us
    pallas_call x2, Pallas kernels, forward(): pl.pallas_call(lambda *refs: forward_kernel(slots, first, copies, *refs),...  24.4 us
    all_to_all x1, blocking collectives, body(): gathered = lax.all_to_all(part, group, 0, 0, tiled=True)  15.8 us
    ppermute x13, starting transfers between devices, exchange(): return lax.ppermute(value, axes, [(i, i ^ step) for i in range(size)])  12.7 us
    ppermute x13, waiting for transfers between devices, exchange(): return lax.ppermute(value, axes, [(i, i ^ step) for i in range(size)])  11.3 us
    ppermute x6, waiting for transfers between devices, rotate(): return lax.ppermute(value, 'x', [(i, (i + step) % 4) for i in range(4)])  10.7 us
    ppermute x6, starting transfers between devices, rotate(): return lax.ppermute(value, 'x', [(i, (i + step) % 4) for i in range(4)])  7.37 us
    ppermute x3, starting transfers between devices, body(): lax.ppermute(piece, 'z', [(i, (i + s) % 4) for i in range(4)])  5.45 us
  transfers between devices with their start and end apart: 26, of which 10 were waited for; matrix products, arithmetic and copies ran while one was open for 2% of the time, Pallas kernels for 20%

profile of v5, /device:TPU:0, one launch (start us, length us, event | category | flops | bytes accessed | tf_op | source)
XLA Modules:
  0.0 133.3 jit_solution(17599634035420521440)
XLA Ops:
  0.6 0.0 copy-start
  0.7 0.8 dynamic_slice.23
  1.4 0.1 slice.44
  1.5 0.1 broadcast_in_dim.12
  1.6 0.1 broadcast_in_dim.15
  1.6 0.1 reshape_reshape.4
  1.7 0.1 broadcast_in_dim.13
  1.8 0.1 broadcast_in_dim.14
  2.1 4.2 %collective-permute-start.5 = (bf16[416,128]{1,0:T(8,128)(2,1)S(1)}, bf16[416,128]{1,0:T(8,128)(2,1)S(1)}, u32[]{:S(2)}, u32[]{:S(2)}) collective-permute-start(bf16[416,128]{1,0:T(8,128)(2,1)S(1)} %constant_dynamic-update-slice_fusion), channel_id=1, source_target_pairs={{0,12},{4,0},{8,4},{12,8},{1,13},{5,1},{9,5},{13,9},{2,14},{6,2},{... | collective-permute-start | bytes 319496 | tf_op jit(solution)/shard_map/ppermute | solution.py:344
  6.3 1.3 collective-permute-start.3
  7.5 0.9 constant_dynamic-slice_fusion.2
  8.4 1.9 %collective-permute-start.2 = (bf16[1,192,128]{2,1,0:T(8,128)(2,1)S(1)}, bf16[1,192,128]{2,1,0:T(8,128)(2,1)S(1)}, u32[]{:S(2)}, u32[]{:S(2)}) collective-permute-start(bf16[1,192,128]{2,1,0:T(8,128)(2,1)S(1)} %get-tuple-element.94), channel_id=1, source_target_pairs={{0,3},{1,2},{2,1},{3,0},{4,7},{5,6},{6,5},{7,4},{8,11},{9,10},{10,... | collective-permute-start | bytes 147464 | tf_op jit(solution)/shard_map/ppermute | solution.py:307
  10.3 1.5 %collective-permute-start.1 = (bf16[1,192,128]{2,1,0:T(8,128)(2,1)S(1)}, bf16[1,192,128]{2,1,0:T(8,128)(2,1)S(1)}, u32[]{:S(2)}, u32[]{:S(2)}) collective-permute-start(bf16[1,192,128]{2,1,0:T(8,128)(2,1)S(1)} %get-tuple-element.95), channel_id=1, source_target_pairs={{0,2},{1,3},{2,0},{3,1},{4,6},{5,7},{6,4},{7,5},{8,10},{9,11},{10,... | collective-permute-start | bytes 147464 | tf_op jit(solution)/shard_map/ppermute | solution.py:307
  11.8 2.0 %collective-permute-done.2 = bf16[1,192,128]{2,1,0:T(8,128)(2,1)S(1)} collective-permute-done((bf16[1,192,128]{2,1,0:T(8,128)(2,1)S(1)}, bf16[1,192,128]{2,1,0:T(8,128)(2,1)S(1)}, u32[]{:S(2)}, u32[]{:S(2)}) %collective-permute-start.2) | collective-permute-done | bytes 49184 | tf_op jit(solution)/shard_map/ppermute | solution.py:307
  13.8 0.1 collective-permute-start
  13.9 2.0 %collective-permute-done.1 = bf16[1,192,128]{2,1,0:T(8,128)(2,1)S(1)} collective-permute-done((bf16[1,192,128]{2,1,0:T(8,128)(2,1)S(1)}, bf16[1,192,128]{2,1,0:T(8,128)(2,1)S(1)}, u32[]{:S(2)}, u32[]{:S(2)}) %collective-permute-start.1) | collective-permute-done | bytes 49184 | tf_op jit(solution)/shard_map/ppermute | solution.py:307
  15.9 0.0 collective-permute-done
  15.9 0.0 collective-permute-done.5
  15.9 0.0 collective-permute-done.4
  15.9 0.1 pad_maximum_fusion.refs_1_
  16.0 0.8 collective-permute-start.9
  16.8 2.8 %collective-permute-start.8 = (bf16[4,192,128]{2,1,0:T(8,128)(2,1)S(1)}, bf16[4,192,128]{2,1,0:T(8,128)(2,1)S(1)}, u32[]{:S(2)}, u32[]{:S(2)}) collective-permute-start(bf16[4,192,128]{2,1,0:T(8,128)(2,1)S(1)} %constant_dynamic-update-slice_fusion.6), channel_id=1, source_target_pairs={{0,96},{32,0},{64,32},{96,64},{1,97},{33,1},{65,33},{97,65},{2,98}... | collective-permute-start | bytes 589832 | tf_op jit(solution)/shard_map/ppermute | solution.py:311
  19.6 0.8 collective-permute-start.7
  20.4 0.9 collective-permute-start.6
  21.3 0.1 pad_add_fusion.refs_0_
  21.4 6.9 %collective-permute-done.8 = bf16[4,192,128]{2,1,0:T(8,128)(2,1)S(1)} collective-permute-done((bf16[4,192,128]{2,1,0:T(8,128)(2,1)S(1)}, bf16[4,192,128]{2,1,0:T(8,128)(2,1)S(1)}, u32[]{:S(2)}, u32[]{:S(2)}) %collective-permute-start.8) | collective-permute-done | bytes 196640 | tf_op jit(solution)/shard_map/ppermute | solution.py:311
  28.3 0.7 collective-permute-done.7
  29.0 3.0 %collective-permute-done.6 = bf16[4,192,128]{2,1,0:T(8,128)(2,1)S(1)} collective-permute-done((bf16[4,192,128]{2,1,0:T(8,128)(2,1)S(1)}, bf16[4,192,128]{2,1,0:T(8,128)(2,1)S(1)}, u32[]{:S(2)}, u32[]{:S(2)}) %collective-permute-start.6) | collective-permute-done | bytes 196640 | tf_op jit(solution)/shard_map/ppermute | solution.py:311
  32.1 0.1 collective-permute-start.10
  32.2 12.2 %shard_map.58 = (f32[24,3072]{1,0:T(8,128)S(1)}, f32[24,3072]{1,0:T(8,128)S(1)}, f32[2,3072]{1,0:T(2,128)S(1)}) custom-call(s32[2]{0:T(128)S(1)} %pad_add_fusion.refs_0_, bf16[4,416,128]{2,1,0:T(8,128)(2,1)S(1)} %pad_maximum_fusion.refs_1_, bf16[4,416,128]{2,1,0:T(8,128)(2,1)S(1)} %collective-permute-done.9.refs_2_, ...), custom_call_target="tpu_custom_call" | custom-call | flops 30000001024 | bytes 8000000 | tf_op jit(solution)/shard_map/pallas_call | solution.py:149
  44.4 0.0 collective-permute-done.10.refs_3_
  44.4 12.2 %shard_map.59 = (f32[24,3072]{1,0:T(8,128)S(1)}, f32[24,3072]{1,0:T(8,128)S(1)}, f32[16,2,3072]{2,1,0:T(2,128)S(1)}) custom-call(s32[2]{0:T(128)S(1)} %pad_add_fusion.refs_0_, bf16[4,416,128]{2,1,0:T(8,128)(2,1)S(1)} %pad_maximum_fusion.refs_1_, bf16[4,416,128]{2,1,0:T(8,128)(2,1)S(1)} %collective-permute-done.9.refs_2_, ...), custom_call_target="tpu_custom_call" | custom-call | flops 30000001024 | bytes 8000000 | tf_op jit(solution)/shard_map/pallas_call | solution.py:149
  56.6 15.8 %all_to_all.10.refs_7_ = f32[16,2,3072]{2,1,0:T(2,128)S(1)} all-to-all(f32[16,2,3072]{2,1,0:T(2,128)S(1)} %get-tuple-element.61), channel_id=1, replica_groups=mesh['x'=4,'yl'=2,'z'=4,'yh'=2,'c'=2] {'yl','z','yh'}, dimensions={0} | all-to-all | bytes 786432 | tf_op jit(solution)/shard_map/all_to_all | solution.py:362
  72.4 14.5 %shard_map.60 = (f32[3072,128]{1,0:T(8,128)S(1)}, f32[3072,128]{1,0:T(8,128)S(1)}, f32[8,128]{1,0:T(8,128)S(1)}) custom-call(s32[2]{0:T(128)S(1)} %pad_add_fusion.refs_0_, bf16[4,416,128]{2,1,0:T(8,128)(2,1)S(1)} %pad_maximum_fusion.refs_1_, bf16[4,416,128]{2,1,0:T(8,128)(2,1)S(1)} %collective-permute-done.9.refs_2_, ...), custom_call_target="tpu_custom_call" | custom-call | flops 30000001024 | bytes 8000000 | tf_op jit(solution)/shard_map/pallas_call | solution.py:294
  86.9 0.1 collective-permute-start.12
  87.0 0.5 collective-permute-start.11
  87.5 9.2 %shard_map.61 = (f32[3072,128]{1,0:T(8,128)S(1)}, bf16[512,128]{1,0:T(8,128)(2,1)S(1)}, bf16[512,128]{1,0:T(8,128)(2,1)S(1)}, bf16[512,128]{1,0:T(8,128)(2,1)S(1)}, bf16[512,128]{1,0:T(8,128)(2,1)S(1)}) custom-call(s32[2]{0:T(128)S(1)} %pad_add_fusion.refs_0_, bf16[4,416,128]{2,1,0:T(8,128)(2,1)S(1)} %pad_maximum_fusion.refs_1_, ...), custom_call_target="tpu_custom_call" | custom-call | flops 30000001024 | bytes 8000000 | tf_op jit(solution)/shard_map/pallas_call | solution.py:294
  96.7 1.2 collective-permute-start.13
  97.9 0.9 collective-permute-start.14
  98.8 1.2 collective-permute-start.15
  100.0 0.0 collective-permute-done.12.refs_12_
  100.0 5.9 %shard_map.62 = (f32[784,128]{1,0:T(8,128)S(1)}, bf16[784,128]{1,0:T(8,128)(2,1)S(1)}, bf16[784,128]{1,0:T(8,128)(2,1)S(1)}, bf16[784,128]{1,0:T(8,128)(2,1)S(1)}, bf16[2048,128]{1,0:T(8,128)(2,1)}) custom-call(s32[2]{0:T(128)S(1)} %pad_add_fusion.refs_0_, bf16[4,416,128]{2,1,0:T(8,128)(2,1)S(1)} %pad_maximum_fusion.refs_1_, ...), custom_call_target="tpu_custom_call" | custom-call | flops 30000001024 | bytes 8000000 | tf_op jit(solution)/shard_map/pallas_call | solution.py:294
  105.9 0.0 collective-permute-done.13
  105.9 1.3 collective-permute-done.14
  107.2 0.1 add_add_fusion.1
  107.3 0.7 collective-permute-start.16
  107.9 0.8 collective-permute-start.19
  108.8 1.2 collective-permute-start.20
  109.9 0.8 collective-permute-start.21
  110.8 1.5 %collective-permute-done.16 = f32[256,128]{1,0:T(8,128)S(1)} collective-permute-done((f32[256,128]{1,0:T(8,128)S(1)}, f32[256,128]{1,0:T(8,128)S(1)}, u32[]{:S(2)}, u32[]{:S(2)}) %collective-permute-start.16) | collective-permute-done | bytes 131104 | tf_op jit(solution)/shard_map/ppermute | solution.py:307
  112.3 3.6 %all-to-all-start.1 = ((bf16[16,128,128]{2,1,0:T(8,128)(2,1)}), bf16[16,128,128]{2,1,0:T(8,128)(2,1)S(1)}, u32[]{:S(2)}, u32[]{:S(2)}) async-start(bf16[16,128,128]{2,1,0:T(8,128)(2,1)} %bitcast.9), calls=%async_computation.1 | async-start | bytes 1048576 | tf_op jit(solution)/shard_map/all_to_all | solution.py:381
  115.9 3.3 %collective-permute-start.17 = (f32[256,128]{1,0:T(8,128)S(1)}, f32[256,128]{1,0:T(8,128)S(1)}, u32[]{:S(2)}, u32[]{:S(2)}) collective-permute-start(f32[256,128]{1,0:T(8,128)S(1)} %slice_add_fusion), channel_id=1, source_target_pairs={{0,2},{2,0},{1,3},{3,1},{4,6},{6,4},{5,7},{7,5},{8,10},{10,8},{9,1... | collective-permute-start | bytes 393224 | tf_op jit(solution)/shard_map/ppermute | solution.py:307
  119.2 0.2 collective-permute-done.21
  119.4 0.1 add_add_fusion
  119.6 0.1 collective-permute-start.22
  119.6 2.4 %collective-permute-start.24 = (f32[192,128]{1,0:T(8,128)S(1)}, f32[192,128]{1,0:T(8,128)S(1)}, u32[]{:S(2)}, u32[]{:S(2)}) collective-permute-start(f32[192,128]{1,0:T(8,128)S(1)} %get-tuple-element.90), channel_id=1, source_target_pairs={{0,3},{1,2},{2,1},{3,0},{4,7},{5,6},{6,5},{7,4},{8,11},{9,10},{10,... | collective-permute-start | bytes 294920 | tf_op jit(solution)/shard_map/ppermute | solution.py:307
  122.1 1.2 collective-permute-start.23
  123.3 0.6 slice_reduce_fusion
  124.5 3.9 %collective-permute-done.17 = f32[256,128]{1,0:T(8,128)S(1)} collective-permute-done((f32[256,128]{1,0:T(8,128)S(1)}, f32[256,128]{1,0:T(8,128)S(1)}, u32[]{:S(2)}, u32[]{:S(2)}) %collective-permute-start.17) | collective-permute-done | bytes 131104 | tf_op jit(solution)/shard_map/ppermute | solution.py:307
  128.5 0.1 convert_reduce_fusion
  128.6 0.1 collective-permute-start.18
  128.7 1.9 %collective-permute-done.23 = f32[192,128]{1,0:T(8,128)S(1)} collective-permute-done((f32[192,128]{1,0:T(8,128)S(1)}, f32[192,128]{1,0:T(8,128)S(1)}, u32[]{:S(2)}, u32[]{:S(2)}) %collective-permute-start.23) | collective-permute-done | bytes 98336 | tf_op jit(solution)/shard_map/ppermute | solution.py:307
  130.6 0.8 pad_maximum_fusion.2
  131.4 0.8 pad_maximum_fusion.1
  (38 shorter events, 0.5 us)
Async XLA Ops:
  0.6 1.3 copy-start
  2.1 13.8 %collective-permute-start.5 = (bf16[416,128]{1,0:T(8,128)(2,1)S(1)}, bf16[416,128]{1,0:T(8,128)(2,1)S(1)}, u32[]{:S(2)}, u32[]{:S(2)}) collective-permute-start(bf16[416,128]{1,0:T(8,128)(2,1)S(1)} %constant_dynamic-update-slice_fusion), channel_id=1, source_target_pairs={{0,12},{4,0},{8,4},{12,8},{1,13},{5,1},{9,5},{13,9},{2,14},{6,2},{... | collective-permute-start | bytes 319496 | tf_op jit(solution)/shard_map/ppermute | solution.py:344
  6.3 9.6 %collective-permute-start.4 = (bf16[416,128]{1,0:T(8,128)(2,1)S(1)}, bf16[416,128]{1,0:T(8,128)(2,1)S(1)}, u32[]{:S(2)}, u32[]{:S(2)}) collective-permute-start(bf16[416,128]{1,0:T(8,128)(2,1)S(1)} %constant_dynamic-update-slice_fusion), channel_id=1, source_target_pairs={{0,8},{4,12},{8,0},{12,4},{1,9},{5,13},{9,1},{13,5},{2,10},{6,14},... | collective-permute-start | bytes 319496 | tf_op jit(solution)/shard_map/ppermute | solution.py:344
  6.3 9.6 %collective-permute-start.3 = (bf16[416,128]{1,0:T(8,128)(2,1)S(1)}, bf16[416,128]{1,0:T(8,128)(2,1)S(1)}, u32[]{:S(2)}, u32[]{:S(2)}) collective-permute-start(bf16[416,128]{1,0:T(8,128)(2,1)S(1)} %constant_dynamic-update-slice_fusion), channel_id=1, source_target_pairs={{0,4},{4,8},{8,12},{12,0},{1,5},{5,9},{9,13},{13,1},{2,6},{6,10},{... | collective-permute-start | bytes 319496 | tf_op jit(solution)/shard_map/ppermute | solution.py:344
  8.4 5.4 %collective-permute-start.2 = (bf16[1,192,128]{2,1,0:T(8,128)(2,1)S(1)}, bf16[1,192,128]{2,1,0:T(8,128)(2,1)S(1)}, u32[]{:S(2)}, u32[]{:S(2)}) collective-permute-start(bf16[1,192,128]{2,1,0:T(8,128)(2,1)S(1)} %get-tuple-element.94), channel_id=1, source_target_pairs={{0,3},{1,2},{2,1},{3,0},{4,7},{5,6},{6,5},{7,4},{8,11},{9,10},{10,... | collective-permute-start | bytes 147464 | tf_op jit(solution)/shard_map/ppermute | solution.py:307
  10.3 5.6 %collective-permute-start.1 = (bf16[1,192,128]{2,1,0:T(8,128)(2,1)S(1)}, bf16[1,192,128]{2,1,0:T(8,128)(2,1)S(1)}, u32[]{:S(2)}, u32[]{:S(2)}) collective-permute-start(bf16[1,192,128]{2,1,0:T(8,128)(2,1)S(1)} %get-tuple-element.95), channel_id=1, source_target_pairs={{0,2},{1,3},{2,0},{3,1},{4,6},{5,7},{6,4},{7,5},{8,10},{9,11},{10,... | collective-permute-start | bytes 147464 | tf_op jit(solution)/shard_map/ppermute | solution.py:307
  13.8 2.1 %collective-permute-start = (bf16[1,192,128]{2,1,0:T(8,128)(2,1)S(1)}, bf16[1,192,128]{2,1,0:T(8,128)(2,1)S(1)}, u32[]{:S(2)}, u32[]{:S(2)}) collective-permute-start(bf16[1,192,128]{2,1,0:T(8,128)(2,1)S(1)} %get-tuple-element.96), channel_id=1, source_target_pairs={{0,1},{1,0},{2,3},{3,2},{4,5},{5,4},{6,7},{7,6},{8,9},{9,8},{10,11... | collective-permute-start | bytes 147464 | tf_op jit(solution)/shard_map/ppermute | solution.py:307
  16.0 16.0 %collective-permute-start.9 = (bf16[4,416,128]{2,1,0:T(8,128)(2,1)S(1)}, bf16[4,416,128]{2,1,0:T(8,128)(2,1)S(1)}, u32[]{:S(2)}, u32[]{:S(2)}) collective-permute-start(bf16[4,416,128]{2,1,0:T(8,128)(2,1)S(1)} %pad_maximum_fusion.refs_1_), channel_id=1, source_target_pairs={{0,16},{16,0},{1,17},{17,1},{2,18},{18,2},{3,19},{19,3},{4,20},{20... | collective-permute-start | bytes 1277960 | tf_op jit(solution)/shard_map/ppermute | solution.py:307
  16.8 11.5 %collective-permute-start.8 = (bf16[4,192,128]{2,1,0:T(8,128)(2,1)S(1)}, bf16[4,192,128]{2,1,0:T(8,128)(2,1)S(1)}, u32[]{:S(2)}, u32[]{:S(2)}) collective-permute-start(bf16[4,192,128]{2,1,0:T(8,128)(2,1)S(1)} %constant_dynamic-update-slice_fusion.6), channel_id=1, source_target_pairs={{0,96},{32,0},{64,32},{96,64},{1,97},{33,1},{65,33},{97,65},{2,98}... | collective-permute-start | bytes 589832 | tf_op jit(solution)/shard_map/ppermute | solution.py:311
  19.6 9.3 %collective-permute-start.7 = (bf16[4,192,128]{2,1,0:T(8,128)(2,1)S(1)}, bf16[4,192,128]{2,1,0:T(8,128)(2,1)S(1)}, u32[]{:S(2)}, u32[]{:S(2)}) collective-permute-start(bf16[4,192,128]{2,1,0:T(8,128)(2,1)S(1)} %constant_dynamic-update-slice_fusion.6), channel_id=1, source_target_pairs={{0,64},{32,96},{64,0},{96,32},{1,65},{33,97},{65,1},{97,33},{2,66}... | collective-permute-start | bytes 589832 | tf_op jit(solution)/shard_map/ppermute | solution.py:311
  20.4 11.5 %collective-permute-start.6 = (bf16[4,192,128]{2,1,0:T(8,128)(2,1)S(1)}, bf16[4,192,128]{2,1,0:T(8,128)(2,1)S(1)}, u32[]{:S(2)}, u32[]{:S(2)}) collective-permute-start(bf16[4,192,128]{2,1,0:T(8,128)(2,1)S(1)} %constant_dynamic-update-slice_fusion.6), channel_id=1, source_target_pairs={{0,32},{32,64},{64,96},{96,0},{1,33},{33,65},{65,97},{97,1},{2,34}... | collective-permute-start | bytes 589832 | tf_op jit(solution)/shard_map/ppermute | solution.py:311
  32.1 12.3 %collective-permute-start.10 = (bf16[16,192,128]{2,1,0:T(8,128)(2,1)S(1)}, bf16[16,192,128]{2,1,0:T(8,128)(2,1)S(1)}, u32[]{:S(2)}, u32[]{:S(2)}) collective-permute-start(bf16[16,192,128]{2,1,0:T(8,128)(2,1)S(1)} %constant_dynamic-update-slice_fusion.10.refs_3_), channel_id=1, source_target_pairs={{0,1},{1,0},{2,3},{3,2},{4,5},{5,4},{6,7},{7,6},{8,9},{9,8},{10,11... | collective-permute-start | bytes 2359304 | tf_op jit(solution)/shard_map/ppermute | solution.py:307
  86.9 13.1 %collective-permute-start.12 = (f32[8,128]{1,0:T(8,128)S(1)}, f32[8,128]{1,0:T(8,128)S(1)}, u32[]{:S(2)}, u32[]{:S(2)}) collective-permute-start(f32[8,128]{1,0:T(8,128)S(1)} %get-tuple-element.67.refs_11_), channel_id=1, source_target_pairs={{0,1},{1,0},{2,3},{3,2},{4,5},{5,4},{6,7},{7,6},{8,9},{9,8},{10,11... | collective-permute-start | bytes 12296 | tf_op jit(solution)/shard_map/ppermute | solution.py:307
  87.0 13.0 %collective-permute-start.11 = (f32[3072,128]{1,0:T(8,128)S(1)}, f32[3072,128]{1,0:T(8,128)S(1)}, u32[]{:S(2)}, u32[]{:S(2)}) collective-permute-start(f32[3072,128]{1,0:T(8,128)S(1)} %get-tuple-element.66), channel_id=1, source_target_pairs={{0,1},{1,0},{2,3},{3,2},{4,5},{5,4},{6,7},{7,6},{8,9},{9,8},{10,11... | collective-permute-start | bytes 4718600 | tf_op jit(solution)/shard_map/ppermute | solution.py:307
  96.7 9.2 %collective-permute-start.13 = (bf16[512,128]{1,0:T(8,128)(2,1)S(1)}, bf16[512,128]{1,0:T(8,128)(2,1)S(1)}, u32[]{:S(2)}, u32[]{:S(2)}) collective-permute-start(bf16[512,128]{1,0:T(8,128)(2,1)S(1)} %get-tuple-element.74), channel_id=1, source_target_pairs={{0,12},{4,0},{8,4},{12,8},{1,13},{5,1},{9,5},{13,9},{2,14},{6,2},{... | collective-permute-start | bytes 393224 | tf_op jit(solution)/shard_map/ppermute | solution.py:371
  97.9 9.2 %collective-permute-start.14 = (bf16[512,128]{1,0:T(8,128)(2,1)S(1)}, bf16[512,128]{1,0:T(8,128)(2,1)S(1)}, u32[]{:S(2)}, u32[]{:S(2)}) collective-permute-start(bf16[512,128]{1,0:T(8,128)(2,1)S(1)} %get-tuple-element.75), channel_id=1, source_target_pairs={{0,4},{4,8},{8,12},{12,0},{1,5},{5,9},{9,13},{13,1},{2,6},{6,10},{... | collective-permute-start | bytes 393224 | tf_op jit(solution)/shard_map/ppermute | solution.py:371
  98.8 8.4 %collective-permute-start.15 = (bf16[512,128]{1,0:T(8,128)(2,1)S(1)}, bf16[512,128]{1,0:T(8,128)(2,1)S(1)}, u32[]{:S(2)}, u32[]{:S(2)}) collective-permute-start(bf16[512,128]{1,0:T(8,128)(2,1)S(1)} %get-tuple-element.77), channel_id=1, source_target_pairs={{0,8},{4,12},{8,0},{12,4},{1,9},{5,13},{9,1},{13,5},{2,10},{6,14},... | collective-permute-start | bytes 393224 | tf_op jit(solution)/shard_map/ppermute | solution.py:371
  107.3 5.0 %collective-permute-start.16 = (f32[256,128]{1,0:T(8,128)S(1)}, f32[256,128]{1,0:T(8,128)S(1)}, u32[]{:S(2)}, u32[]{:S(2)}) collective-permute-start(f32[256,128]{1,0:T(8,128)S(1)} %slice.53), channel_id=1, source_target_pairs={{0,16},{16,0},{1,17},{17,1},{2,18},{18,2},{3,19},{19,3},{4,20},{20... | collective-permute-start | bytes 393224 | tf_op jit(solution)/shard_map/ppermute | solution.py:307
  107.9 11.3 %collective-permute-start.19 = (bf16[784,128]{1,0:T(8,128)(2,1)S(1)}, bf16[784,128]{1,0:T(8,128)(2,1)S(1)}, u32[]{:S(2)}, u32[]{:S(2)}) collective-permute-start(bf16[784,128]{1,0:T(8,128)(2,1)S(1)} %get-tuple-element.82), channel_id=1, source_target_pairs={{0,64},{32,96},{64,0},{96,32},{1,65},{33,97},{65,1},{97,33},{2,66}... | collective-permute-start | bytes 602120 | tf_op jit(solution)/shard_map/ppermute | solution.py:311
  108.8 10.5 %collective-permute-start.20 = (bf16[784,128]{1,0:T(8,128)(2,1)S(1)}, bf16[784,128]{1,0:T(8,128)(2,1)S(1)}, u32[]{:S(2)}, u32[]{:S(2)}) collective-permute-start(bf16[784,128]{1,0:T(8,128)(2,1)S(1)} %get-tuple-element.83), channel_id=1, source_target_pairs={{0,96},{32,0},{64,32},{96,64},{1,97},{33,1},{65,33},{97,65},{2,98}... | collective-permute-start | bytes 602120 | tf_op jit(solution)/shard_map/ppermute | solution.py:311
  109.9 9.5 %collective-permute-start.21 = (bf16[784,128]{1,0:T(8,128)(2,1)S(1)}, bf16[784,128]{1,0:T(8,128)(2,1)S(1)}, u32[]{:S(2)}, u32[]{:S(2)}) collective-permute-start(bf16[784,128]{1,0:T(8,128)(2,1)S(1)} %get-tuple-element.84), channel_id=1, source_target_pairs={{0,32},{32,64},{64,96},{96,0},{1,33},{33,65},{65,97},{97,1},{2,34}... | collective-permute-start | bytes 602120 | tf_op jit(solution)/shard_map/ppermute | solution.py:311
  112.3 16.1 %all-to-all-start.1 = ((bf16[16,128,128]{2,1,0:T(8,128)(2,1)}), bf16[16,128,128]{2,1,0:T(8,128)(2,1)S(1)}, u32[]{:S(2)}, u32[]{:S(2)}) async-start(bf16[16,128,128]{2,1,0:T(8,128)(2,1)} %bitcast.9), calls=%async_computation.1 | async-start | bytes 1048576 | tf_op jit(solution)/shard_map/all_to_all | solution.py:381
  115.9 12.5 %collective-permute-start.17 = (f32[256,128]{1,0:T(8,128)S(1)}, f32[256,128]{1,0:T(8,128)S(1)}, u32[]{:S(2)}, u32[]{:S(2)}) collective-permute-start(f32[256,128]{1,0:T(8,128)S(1)} %slice_add_fusion), channel_id=1, source_target_pairs={{0,2},{2,0},{1,3},{3,1},{4,6},{6,4},{5,7},{7,5},{8,10},{10,8},{9,1... | collective-permute-start | bytes 393224 | tf_op jit(solution)/shard_map/ppermute | solution.py:307
  119.6 9.1 %collective-permute-start.22 = (f32[192,128]{1,0:T(8,128)S(1)}, f32[192,128]{1,0:T(8,128)S(1)}, u32[]{:S(2)}, u32[]{:S(2)}) collective-permute-start(f32[192,128]{1,0:T(8,128)S(1)} %get-tuple-element.89), channel_id=1, source_target_pairs={{0,1},{1,0},{2,3},{3,2},{4,5},{5,4},{6,7},{7,6},{8,9},{9,8},{10,11... | collective-permute-start | bytes 294920 | tf_op jit(solution)/shard_map/ppermute | solution.py:307
  119.6 9.0 %collective-permute-start.24 = (f32[192,128]{1,0:T(8,128)S(1)}, f32[192,128]{1,0:T(8,128)S(1)}, u32[]{:S(2)}, u32[]{:S(2)}) collective-permute-start(f32[192,128]{1,0:T(8,128)S(1)} %get-tuple-element.90), channel_id=1, source_target_pairs={{0,3},{1,2},{2,1},{3,0},{4,7},{5,6},{6,5},{7,4},{8,11},{9,10},{10,... | collective-permute-start | bytes 294920 | tf_op jit(solution)/shard_map/ppermute | solution.py:307
  122.1 8.5 %collective-permute-start.23 = (f32[192,128]{1,0:T(8,128)S(1)}, f32[192,128]{1,0:T(8,128)S(1)}, u32[]{:S(2)}, u32[]{:S(2)}) collective-permute-start(f32[192,128]{1,0:T(8,128)S(1)} %get-tuple-element.91), channel_id=1, source_target_pairs={{0,2},{1,3},{2,0},{3,1},{4,6},{5,7},{6,4},{7,5},{8,10},{9,11},{10,... | collective-permute-start | bytes 294920 | tf_op jit(solution)/shard_map/ppermute | solution.py:307
  128.6 2.8 %collective-permute-start.18 = (f32[384,128]{1,0:T(8,128)S(1)}, f32[384,128]{1,0:T(8,128)S(1)}, u32[]{:S(2)}, u32[]{:S(2)}) collective-permute-start(f32[384,128]{1,0:T(8,128)S(1)} %pad_maximum_fusion.3), channel_id=1, source_target_pairs={{0,1},{1,0},{2,3},{3,2},{4,5},{5,4},{6,7},{7,6},{8,9},{9,8},{10,11... | collective-permute-start | bytes 589832 | tf_op jit(solution)/shard_map/ppermute | solution.py:307
